TPU v7x, 128 devices: a whole 4x4x4 slice. The times are simulated.
128 devices in a mesh: seq: 4 (over z_hi, core), dp: 32 (over y, z_lo, x).
Axes of the slice: x: 4, y: 4, z: 4 (z_hi: 2, z_lo: 2; z = z_hi * 2 + z_lo), core: 2. Of those that a mesh axis runs over, the one named last changes fastest.
Arguments:
- token_ids: int32 [32, 1024], P(None, 'seq'), may hold values from 0 to 50303
- doc_ids: int32 [32, 1024], P('dp'), may hold values from 0 to 1023, as said below
- pick_slots: int32 [32, 256], P(None, 'seq'), may hold values from -1 to 255, as said below
- labels: int32 [32, 256], P(None, 'seq'), may hold values from 0 to 50303
- vocab_table: float32 [25152, 1536], P('dp', 'seq'), may hold values from -0.4330127 to 0.4330127
- vocab_first: float32 [25152, 1536], P('dp', 'seq'), may hold values from -1.9073486e-06 to 1.9073486e-06
- vocab_second: float32 [25152, 1536], P('dp', 'seq'), may hold values from 7.463293e-15 to 2.985317e-14
- positions: float32 [1024, 768], P('seq'), may hold values from -0.625 to 0.625
- positions_first: float32 [1024, 768], P('seq'), may hold values from -1.9073486e-06 to 1.9073486e-06
- positions_second: float32 [1024, 768], P('seq'), may hold values from 7.463293e-15 to 2.985317e-14
- small_params: float32 [26, 768], replicated, may hold values from -0.4 to 1.3
- small_first: float32 [26, 768], replicated, may hold values from -9.536743e-06 to 9.536743e-06
- small_second: float32 [26, 768], replicated, may hold values from 1.8658232e-13 to 7.4632927e-13
- weights: float32 [384, 36864], P(('seq', 'dp')), may hold values from -0.14433757 to 0.14433757
- stat_left: float32 [384, 36864], P(('seq', 'dp')), may hold values from -3.181154e-11 to 6.680423e-10, as said below
- stat_right: float32 [384, 36864], P(('seq', 'dp')), may hold values from -3.181154e-11 to 6.680423e-10, as said below
- root_left: float32 [384, 36864], P(('seq', 'dp')), may hold values from -32.51477 to 563.17235, as said below
- root_right: float32 [384, 36864], P(('seq', 'dp')), may hold values from -32.51477 to 563.17235, as said below
- anchor: float32 [384, 36864], P(('seq', 'dp')), may hold values from -0.185334635 to 0.185334635
- fisher: float32 [384, 36864], P(('seq', 'dp')), may hold values from 4.6645576e-09 to 1.865823e-08
- owners: int32 [2, 192], replicated, may hold values from 0 to 191, as said below
Outputs:
- ce_sum: float32 [], replicated
- pick_count: float32 [], replicated
- grad_norm: float32 [], replicated
- vocab_new: float32 [25152, 1536], P('dp', 'seq')
- vocab_first_new: float32 [25152, 1536], P('dp', 'seq')
- vocab_second_new: float32 [25152, 1536], P('dp', 'seq')
- positions_new: float32 [1024, 768], P('seq')
- positions_first_new: float32 [1024, 768], P('seq')
- positions_second_new: float32 [1024, 768], P('seq')
- small_new: float32 [26, 768], replicated
- small_first_new: float32 [26, 768], replicated
- small_second_new: float32 [26, 768], replicated
- weights_new: float32 [384, 36864], P(('seq', 'dp'))
- stat_left_new: float32 [384, 36864], P(('seq', 'dp'))
- stat_right_new: float32 [384, 36864], P(('seq', 'dp'))
- block_grad: float32 [384, 36864], P(('seq', 'dp'))
- fisher_new: float32 [384, 36864], P(('seq', 'dp'))
Inputs may be any that keep to these rules, and one draw needn't show every extreme that they name: `doc_ids`: each row starts at 0 and never falls; a document's number is the position of its first token; in each row one document covers all positions from one below 256 to one at or past 1024 - 256, and the last position is a document of its own. `pick_slots`: columns s * 64 to (s + 1) * 64 - 1 of a row hold distinct offsets into positions s * 256 to (s + 1) * 256 - 1 of that sequence, or -1; the last row's last 64 columns hold no -1. `owners`: each row is a permutation. `stat_left`: each block symmetric. `stat_right`: each block symmetric. `root_left`: each block symmetric. `root_right`: each block symmetric.
All inputs are finite; a program needn't handle non-finite values.
Results may differ from a plain program's by a relative error of at most 0.004.
The roundings to bfloat16 on the way count: a program that leaves them out, or rounds other values in their place, can miss the bound.
Values may be sent and summed in bfloat16 or wider, within the bound.
No kernel may reach another device: no remote copies, remote signals or barrier semaphores. Data moves between devices by JAX's collectives and lax.ppermute only.
A program may use at most 448 MiB of HBM per device.

v0:
```python
import jax
import jax.numpy as jnp
from jax import lax
from jax.sharding import PartitionSpec as P

HEADS = 12
HEAD_DIM = 64
LAYERS = 2
BS = 192
STEP = 10


exact_prec = lax.Precision.HIGHEST
clip_bound = 0.02
ewc_weight = 1000000.0
fisher_decay = 0.8
first_decay = 0.9
second_decay = 0.999
adam_epsilon = 1e-08
table_rate = 0.05
small_rate = 0.1
decay_rate = 0.1
stat_decay = 0.9
shampoo_rate = 0.02
graft_epsilon = 1e-06


def joined(value, axis, join):
    pieces = jax.tree.map(lambda part: lax.all_gather(part, axis), value)
    head = jax.tree.map(lambda part: part[0], pieces)
    tail = jax.tree.map(lambda part: part[1:], pieces)
    running, _ = lax.scan(lambda running, section: (join(running, section), None), head, tail)
    return running


def product(left, right):
    return jnp.dot(left, right, preferred_element_type=jnp.float32)


def product_tn(left, right):
    return lax.dot_general(
        left, right, (((0,), (0,)), ((), ())), preferred_element_type=jnp.float32
    )


def product_nt(left, right):
    return lax.dot_general(
        left, right, (((1,), (1,)), ((), ())), preferred_element_type=jnp.float32
    )


def exact_mm(left, right):
    return jnp.dot(left, right, precision=exact_prec, preferred_element_type=jnp.float32)


def layer_norm(values_in, gain, shift):
    centre = jnp.mean(values_in, axis=-1, keepdims=True)
    cent = values_in - centre
    spread = jnp.mean(cent * cent, axis=-1, keepdims=True)
    return cent * lax.rsqrt(spread + 1e-05) * gain + shift


def assemble(blocks, row_count, col_count):
    tile_size = blocks.shape[-1]
    grid = blocks.reshape(row_count, col_count, tile_size, tile_size).transpose(0, 2, 1, 3)
    return grid.reshape(row_count * tile_size, col_count * tile_size)


def disassemble(matrix, row_count, col_count):
    grid = matrix.reshape(row_count, BS, col_count, BS).transpose(0, 2, 1, 3)
    return grid.reshape(row_count * col_count, BS, BS)


def tile_shape(model_width, hidden):
    unit = model_width // BS
    return (unit, hidden // BS)


def split_mats(natural, model_width, hidden):
    unit, wide = tile_shape(model_width, hidden)
    first_end = 3 * unit * unit
    second_end = first_end + unit * unit
    third_end = second_end + unit * wide
    return (
        assemble(natural[:first_end], unit, 3 * unit),
        assemble(natural[first_end:second_end], unit, unit),
        assemble(natural[second_end:third_end], unit, wide),
        assemble(natural[third_end:], wide, unit),
    )


def join_mats(mats, model_width, hidden):
    unit, wide = tile_shape(model_width, hidden)
    return jnp.concatenate(
        [
            disassemble(mats[0], unit, 3 * unit),
            disassemble(mats[1], unit, unit),
            disassemble(mats[2], unit, wide),
            disassemble(mats[3], wide, unit),
        ],
        axis=0,
    )


def layer_params(small_params, layer_idx):
    gain_rows = 2 * LAYERS + 1
    base_row = 2 * gain_rows + 8 * layer_idx
    model_width = small_params.shape[1]
    bias_qkv = jnp.concatenate(
        [small_params[base_row], jnp.zeros((model_width,), jnp.float32), small_params[base_row + 1]]
    )
    return (
        small_params[2 * layer_idx],
        small_params[2 * layer_idx + 1],
        small_params[gain_rows + 2 * layer_idx],
        small_params[gain_rows + 2 * layer_idx + 1],
        bias_qkv,
        small_params[base_row + 2],
        small_params[base_row + 3 : base_row + 7].reshape(-1),
        small_params[base_row + 7],
    )


def attend(queries_bf, key_values, doc_mask):
    model_width = queries_bf.shape[1]
    queries = queries_bf.reshape(-1, HEADS, HEAD_DIM)
    key_heads = key_values[:, :model_width].reshape(-1, HEADS, HEAD_DIM)
    scores = (
        jnp.einsum("qhd,khd->hqk", queries, key_heads, preferred_element_type=jnp.float32) * 0.125
    )
    scores = jnp.where(doc_mask[None], scores, -1e30)
    peak = jnp.max(scores, axis=-1, keepdims=True)
    expo = jnp.exp(scores - peak)
    return expo / jnp.sum(expo, axis=-1, keepdims=True)


def layer_forward(residual, mats, params, doc_mask):
    w_qkv, w_proj, w_fc, w_out = mats
    gain_a, gain_b, shift_a, shift_b, bias_qkv, bias_proj, bias_fc, bias_out = params
    model_width = residual.shape[1]
    normed = layer_norm(residual, gain_a, shift_a).astype(jnp.bfloat16)
    qkv_bf = (product(normed, w_qkv) + bias_qkv).astype(jnp.bfloat16)
    key_values = lax.all_gather(qkv_bf[:, model_width:], "seq", axis=0, tiled=True)
    soft_probs = attend(qkv_bf[:, :model_width], key_values, doc_mask)
    value_heads = key_values[:, model_width:].reshape(-1, HEADS, HEAD_DIM)
    attended = jnp.einsum(
        "hqk,khd->qhd",
        soft_probs.astype(jnp.bfloat16),
        value_heads,
        preferred_element_type=jnp.float32,
    )
    attended = attended.reshape(-1, model_width).astype(jnp.bfloat16)
    middle = residual + product(attended, w_proj) + bias_proj
    normed_b = layer_norm(middle, gain_b, shift_b).astype(jnp.bfloat16)
    inner_pre = product(normed_b, w_fc) + bias_fc
    activated = jax.nn.gelu(inner_pre, approximate=True).astype(jnp.bfloat16)
    result = middle + product(activated, w_out) + bias_out
    return (
        result,
        (residual, qkv_bf, key_values, attended, middle, normed_b, inner_pre, activated),
    )


def layer_backward(grad_in, kept_values, mats, params, doc_mask):
    residual, qkv_bf, key_values, attended, middle, normed_b, inner_pre, activated = kept_values
    w_qkv, w_proj, w_fc, w_out = mats
    gain_a, gain_b, shift_a, shift_b = params[:4]
    model_width = residual.shape[1]
    grad_out = grad_in.astype(jnp.bfloat16)
    d_out = product_tn(activated, grad_out)
    b_out = jnp.sum(grad_out.astype(jnp.float32), axis=0)
    _, gelu_back = jax.vjp(lambda inner_in: jax.nn.gelu(inner_in, approximate=True), inner_pre)
    grad_inner = gelu_back(product_nt(grad_out, w_out))[0].astype(jnp.bfloat16)
    d_fc = product_tn(normed_b, grad_inner)
    b_fc = jnp.sum(grad_inner.astype(jnp.float32), axis=0)
    _, norm_back_b = jax.vjp(layer_norm, middle, gain_b, shift_b)
    grad_mid, g_gain_b, g_shift_b = norm_back_b(product_nt(grad_inner, w_fc))
    grad_mid = grad_mid + grad_in
    grad_branch = grad_mid.astype(jnp.bfloat16)
    d_proj = product_tn(attended, grad_branch)
    b_proj = jnp.sum(grad_branch.astype(jnp.float32), axis=0)
    grad_att = product_nt(grad_branch, w_proj).astype(jnp.bfloat16)
    all_pairs = lax.all_gather(qkv_bf[:, model_width:], "seq", axis=0, tiled=True)
    soft_probs = attend(qkv_bf[:, :model_width], all_pairs, doc_mask)
    seq_len = all_pairs.shape[0]
    queries = qkv_bf[:, :model_width].reshape(-1, HEADS, HEAD_DIM)
    key_heads = all_pairs[:, :model_width].reshape(seq_len, HEADS, HEAD_DIM)
    value_heads = all_pairs[:, model_width:].reshape(seq_len, HEADS, HEAD_DIM)
    grad_heads = grad_att.reshape(-1, HEADS, HEAD_DIM)
    grad_prob = jnp.einsum(
        "qhd,khd->hqk", grad_heads, value_heads, preferred_element_type=jnp.float32
    )
    grad_score = soft_probs * (grad_prob - jnp.sum(soft_probs * grad_prob, axis=-1, keepdims=True))
    grad_score = grad_score.astype(jnp.bfloat16)
    grad_query = (
        jnp.einsum(
            "hqk,khd->qhd", grad_score, key_heads, preferred_element_type=jnp.float32
        ).reshape(-1, model_width)
        * 0.125
    )
    grad_keys = (
        jnp.einsum("hqk,qhd->khd", grad_score, queries, preferred_element_type=jnp.float32).reshape(
            seq_len, model_width
        )
        * 0.125
    )
    grad_values = jnp.einsum(
        "hqk,qhd->khd",
        soft_probs.astype(jnp.bfloat16),
        grad_heads,
        preferred_element_type=jnp.float32,
    ).reshape(seq_len, model_width)
    grad_pairs = lax.psum_scatter(
        jnp.concatenate([grad_keys, grad_values], axis=1), "seq", scatter_dimension=0, tiled=True
    )
    grad_mixed = jnp.concatenate([grad_query, grad_pairs], axis=1).astype(jnp.bfloat16)
    normed_a, norm_back_a = jax.vjp(layer_norm, residual, gain_a, shift_a)
    d_qkv = product_tn(normed_a.astype(jnp.bfloat16), grad_mixed)
    mixed_sums = jnp.sum(grad_mixed.astype(jnp.float32), axis=0)
    grad_resid, g_gain_a, g_shift_a = norm_back_a(product_nt(grad_mixed, w_qkv))
    grad_resid = grad_resid + grad_mid
    bias_rows = jnp.concatenate(
        [
            jnp.stack([mixed_sums[:model_width], mixed_sums[2 * model_width :], b_proj]),
            b_fc.reshape(-1, model_width),
            b_out[None],
        ],
        axis=0,
    )
    return (
        grad_resid,
        (d_qkv, d_proj, d_fc, d_out),
        (g_gain_a, g_gain_b, g_shift_a, g_shift_b, bias_rows),
    )


def merge_stats(first_part, second_part):
    peak = jnp.maximum(first_part[0], second_part[0])
    summed = first_part[1] * jnp.exp(first_part[0] - peak) + second_part[1] * jnp.exp(
        second_part[0] - peak
    )
    return (peak, summed, first_part[2] + second_part[2])


def adam_update(param, grad, first, second, rate, decay):
    first = first_decay * first + (1.0 - first_decay) * grad
    second = second_decay * second + (1.0 - second_decay) * grad * grad
    fixed_first = first / (1.0 - first_decay**STEP)
    fixed_second = second / (1.0 - second_decay**STEP)
    return (
        param - rate * (fixed_first / (jnp.sqrt(fixed_second) + adam_epsilon) + decay * param),
        first,
        second,
    )


def shampoo(param, grad, left, right, root_l, root_r):
    left = stat_decay * left + (1.0 - stat_decay) * exact_mm(grad, grad.T)
    right = stat_decay * right + (1.0 - stat_decay) * exact_mm(grad.T, grad)
    direction = exact_mm(exact_mm(root_l, grad), root_r)
    direction = direction * lax.rsqrt(jnp.mean(direction * direction) + graft_epsilon)
    return (param - shampoo_rate * (direction + decay_rate * param), left, right)


def squared_blocks(flat):
    return flat.reshape(-1, BS, BS)


def shards(
    token_ids,
    doc_ids,
    pick_slots,
    labels,
    vocab_table,
    vocab_first,
    vocab_second,
    positions,
    positions_first,
    positions_second,
    small_params,
    small_first,
    small_second,
    weights,
    stat_left,
    stat_right,
    root_left,
    root_right,
    anchor,
    fisher,
    owners,
):
    row_at = lax.axis_index("dp")
    seq_at = lax.axis_index("seq")
    span_len = token_ids.shape[1]
    model_width = small_params.shape[1]
    hidden = 4 * model_width
    per_layer = owners.shape[1]
    pick_dev = pick_slots.shape[1]
    table_pairs = lax.all_gather(vocab_table.astype(jnp.bfloat16), "seq", axis=1, tiled=True)
    table_bf = table_pairs.reshape(-1, model_width)
    vocab_rows = table_bf.shape[0]
    vocab_start = row_at * vocab_rows
    slot_blocks = squared_blocks(
        lax.all_gather(weights.astype(jnp.bfloat16), ("seq", "dp"), axis=0, tiled=True)
    )
    inverse = jnp.argsort(owners, axis=1)
    layer_weights = [
        split_mats(
            jnp.take(
                slot_blocks[layer_idx * per_layer : (layer_idx + 1) * per_layer],
                inverse[layer_idx],
                axis=0,
            ),
            model_width,
            hidden,
        )
        for layer_idx in range(LAYERS)
    ]
    all_params = [layer_params(small_params, layer_idx) for layer_idx in range(LAYERS)]
    local_ids = token_ids.reshape(-1) - vocab_start
    inside = (local_ids >= 0) & (local_ids < vocab_rows)
    clipped = jnp.clip(local_ids, 0, vocab_rows - 1)
    found = jnp.take(table_bf, clipped, axis=0)
    residual = (
        lax.psum_scatter(
            jnp.where(inside[:, None], found.astype(jnp.float32), 0.0).astype(jnp.bfloat16),
            "dp",
            scatter_dimension=0,
            tiled=True,
        ).astype(jnp.float32)
        + positions
    )
    doc_row = doc_ids[0]
    seq_len = doc_row.shape[0]
    query_places = seq_at * span_len + jnp.arange(span_len)
    own_docs = lax.dynamic_slice_in_dim(doc_row, seq_at * span_len, span_len)
    doc_mask = (query_places[:, None] >= jnp.arange(seq_len)[None, :]) & (
        own_docs[:, None] == doc_row[None, :]
    )
    kept_layers = []
    for layer_idx in range(LAYERS):
        residual, kept_values = layer_forward(
            residual, layer_weights[layer_idx], all_params[layer_idx], doc_mask
        )
        kept_layers.append(kept_values)
    gain_rows = 2 * LAYERS + 1
    final_norm, final_back = jax.vjp(
        layer_norm, residual, small_params[2 * LAYERS], small_params[gain_rows + 2 * LAYERS]
    )
    final_bf = final_norm.astype(jnp.bfloat16)
    own_picks = lax.dynamic_index_in_dim(pick_slots, row_at, 0, keepdims=False)
    own_valid = own_picks >= 0
    pick_rows = jnp.maximum(own_picks, 0)
    chosen = jnp.where(
        own_valid[:, None], jnp.take(final_bf, pick_rows, axis=0), jnp.zeros((), jnp.bfloat16)
    )
    gathered = lax.all_gather(chosen, "dp", axis=0, tiled=True)
    logits = product_nt(gathered, table_bf)
    valid_all = pick_slots.reshape(-1) >= 0
    hits = (labels.reshape(-1) - vocab_start)[:, None] == jnp.arange(vocab_rows)[None, :]
    peak = jnp.max(logits, axis=1)
    exp_total = jnp.sum(jnp.exp(logits - peak[:, None]), axis=1)
    target = jnp.sum(jnp.where(hits, logits, 0.0), axis=1)
    peak_all, total_all, target_all = joined((peak, exp_total, target), "dp", merge_stats)
    log_total = peak_all + jnp.log(total_all)
    losses = jnp.where(valid_all, log_total - target_all, 0.0)
    loss_own = jnp.sum(lax.dynamic_slice_in_dim(losses, row_at * pick_dev, pick_dev))
    count_own = jnp.sum(own_valid.astype(jnp.float32))
    grad_logits = jnp.where(
        valid_all[:, None], jnp.exp(logits - log_total[:, None]) - hits.astype(jnp.float32), 0.0
    ).astype(jnp.bfloat16)
    grad_table = product_tn(grad_logits, gathered)
    grad_chosen = lax.psum_scatter(
        product(grad_logits, table_bf), "dp", scatter_dimension=0, tiled=True
    )
    grad_final = (
        jnp.zeros((span_len, model_width), jnp.float32)
        .at[pick_rows]
        .add(jnp.where(own_valid[:, None], grad_chosen, 0.0))
    )
    grad_resid, g_final_gain, g_final_shift = final_back(grad_final)
    slot_grads = [None] * LAYERS
    small_parts = [None] * LAYERS
    for layer_idx in reversed(range(LAYERS)):
        grad_resid, mat_grads, small_part = layer_backward(
            grad_resid,
            kept_layers[layer_idx],
            layer_weights[layer_idx],
            all_params[layer_idx],
            doc_mask,
        )
        slot_grads[layer_idx] = jnp.take(
            join_mats(mat_grads, model_width, hidden), owners[layer_idx], axis=0
        )
        small_parts[layer_idx] = small_part
    token_grads = lax.all_gather(grad_resid.astype(jnp.bfloat16), "dp", axis=0, tiled=True)
    grad_table = grad_table.at[clipped].add(
        jnp.where(inside[:, None], token_grads.astype(jnp.float32), 0.0)
    )
    grad_table = lax.psum_scatter(
        grad_table.reshape(vocab_rows // 2, 2 * model_width), "seq", scatter_dimension=1, tiled=True
    )
    all_slots = jnp.concatenate(slot_grads, axis=0).reshape(-1, BS * BS)
    own_blocks = lax.psum_scatter(all_slots, ("seq", "dp"), scatter_dimension=0, tiled=True)
    gain_list = []
    shift_list = []
    for layer_idx in range(LAYERS):
        gain_list += [small_parts[layer_idx][0], small_parts[layer_idx][1]]
        shift_list += [small_parts[layer_idx][2], small_parts[layer_idx][3]]
    small_grad = jnp.concatenate(
        [jnp.stack(gain_list + [g_final_gain]), jnp.stack(shift_list + [g_final_shift])]
        + [small_parts[layer_idx][4] for layer_idx in range(LAYERS)],
        axis=0,
    )
    pos_full = lax.dynamic_update_slice_in_dim(
        jnp.zeros((seq_len, model_width), jnp.float32), grad_resid, seq_at * span_len, 0
    )
    small_sum, pos_sum, ce_sum, pick_count = lax.psum(
        (small_grad, pos_full, loss_own, count_own), ("seq", "dp")
    )
    g_table = grad_table / pick_count
    g_pos = lax.dynamic_slice_in_dim(pos_sum, seq_at * span_len, span_len, 0) / pick_count
    g_small = small_sum / pick_count
    g_ce = own_blocks / pick_count
    g_blocks = g_ce + ewc_weight * fisher * (weights - anchor)
    first_row = row_at == 0
    first_seq = seq_at == 0
    local_squares = jnp.sum(g_table * g_table) + jnp.sum(g_blocks * g_blocks)
    local_squares = local_squares + jnp.where(first_row, jnp.sum(g_pos * g_pos), 0.0)
    local_squares = local_squares + jnp.where(
        first_row & first_seq, jnp.sum(g_small * g_small), 0.0
    )
    grad_norm = jnp.sqrt(lax.psum(local_squares, ("seq", "dp")))
    factor = jnp.minimum(1.0, clip_bound / grad_norm)
    table_new, table_first, table_second = adam_update(
        vocab_table, factor * g_table, vocab_first, vocab_second, table_rate, decay_rate
    )
    pos_new, pos_first, pos_second = adam_update(
        positions, factor * g_pos, positions_first, positions_second, table_rate, 0.0
    )
    small_new, small_first_new, small_second_new = adam_update(
        small_params, factor * g_small, small_first, small_second, small_rate, 0.0
    )
    block_grad = factor * g_blocks
    weights_new, left_new, right_new = jax.vmap(shampoo)(
        squared_blocks(weights),
        squared_blocks(block_grad),
        squared_blocks(stat_left),
        squared_blocks(stat_right),
        squared_blocks(root_left),
        squared_blocks(root_right),
    )
    fisher_new = fisher_decay * fisher + (1.0 - fisher_decay) * g_ce * g_ce
    return (
        ce_sum,
        pick_count,
        grad_norm,
        table_new,
        table_first,
        table_second,
        pos_new,
        pos_first,
        pos_second,
        small_new,
        small_first_new,
        small_second_new,
        weights_new.reshape(-1, BS * BS),
        left_new.reshape(-1, BS * BS),
        right_new.reshape(-1, BS * BS),
        block_grad,
        fisher_new,
    )


def solution(mesh):
    in_specs = (
        P(None, "seq"),
        P("dp", None),
        P(None, "seq"),
        P(None, "seq"),
        P("dp", "seq"),
        P("dp", "seq"),
        P("dp", "seq"),
        P("seq", None),
        P("seq", None),
        P("seq", None),
        P(),
        P(),
        P(),
        P(("seq", "dp"), None),
        P(("seq", "dp"), None),
        P(("seq", "dp"), None),
        P(("seq", "dp"), None),
        P(("seq", "dp"), None),
        P(("seq", "dp"), None),
        P(("seq", "dp"), None),
        P(),
    )
    out_specs = (
        P(),
        P(),
        P(),
        P("dp", "seq"),
        P("dp", "seq"),
        P("dp", "seq"),
        P("seq", None),
        P("seq", None),
        P("seq", None),
        P(),
        P(),
        P(),
        P(("seq", "dp"), None),
        P(("seq", "dp"), None),
        P(("seq", "dp"), None),
        P(("seq", "dp"), None),
        P(("seq", "dp"), None),
    )
    return jax.shard_map(shards, mesh=mesh, in_specs=in_specs, out_specs=out_specs, check_vma=False)
```

profile of v0, /device:TPU:1, one launch (start us, length us, event | category | flops | bytes accessed | tf_op | source)
XLA Modules:
  0.0 2860.0 jit_solution(2507803099455156570)
XLA Ops:
  12.7 30.7 %all-gather.11.cloned.1.call-done = bf16[786,1536]{1,0:T(8,128)(2,1)} async-done(((bf16[786,384]{1,0:T(8,128)(2,1)}), bf16[786,1536]{1,0:T(8,128)(2,1)}) %all-gather.11.cloned.1.call-update) | async-done | bytes 2414608 | tf_op jit(solution)/shard_map/all_gather | solution.py:299
  47.0 34.4 %gather_fusion = bf16[8192,768]{1,0:T(8,128)(2,1)} fusion(bf16[1572,768]{1,0:T(8,128)(2,1)S(1)} %reshape.583, s32[8192]{0:T(1024)S(1)} %broadcast_clamp_fusion), kind=kCustom, calls=%fused_computation.4 | custom fusion | bytes 25198592 | tf_op jit(solution)/shard_map/jit(_take)/gather | solution.py:323
  81.4 13.3 select_convert_fusion
  101.4 176.7 %reduce-scatter.7.cloned.1.call-done = bf16[256,768]{1,0:T(8,128)(2,1)} async-done(((bf16[8192,768]{1,0:T(8,128)(2,1)}), bf16[256,768]{1,0:T(8,128)(2,1)}) %reduce-scatter.7.cloned.1.call-update) | async-done | bytes 393232 | tf_op jit(solution)/shard_map/reduce_scatter | solution.py:325
  279.5 270.0 %all-gather.21.cloned.1.call-done = bf16[128,3,36864]{2,1,0:T(4,128)(2,1)} async-done(((bf16[1,3,36864]{2,1,0:T(4,128)(2,1)}), bf16[128,3,36864]{2,1,0:T(4,128)(2,1)}) %all-gather.21.cloned.1.call-update) | async-done | bytes 28311568 | tf_op jit(solution)/shard_map/all_gather | solution.py:304
  549.5 31.4 %fusion.110 = (bf16[64,3,36864]{2,1,0:T(4,128)(2,1)}, bf16[64,3,36864]{2,1,0:T(4,128)(2,1)}) fusion(bf16[128,3,36864]{2,1,0:T(4,128)(2,1)} %all-gather.21.cloned.1.call-done), kind=kLoop, calls=%fused_computation.304 | loop fusion | bytes 56623104 | tf_op jit(solution)/shard_map/slice | solution.py:310
  580.9 32.3 %slice.177 = bf16[192,192,192]{2,1,0:T(8,128)(2,1)} reshape(bf16[64,3,36864]{2,1,0:T(4,128)(2,1)} %get-tuple-element.193) | data formatting | bytes 28311552 | tf_op jit(solution)/shard_map/slice | solution.py:310
  613.2 16.8 gather_fusion.2
  680.4 11.5 fusion.112
  732.3 32.3 %slice.197 = bf16[192,192,192]{2,1,0:T(8,128)(2,1)} reshape(bf16[64,3,36864]{2,1,0:T(4,128)(2,1)} %get-tuple-element.192) | data formatting | bytes 28311552 | tf_op jit(solution)/shard_map/slice | solution.py:310
  764.6 16.8 gather_fusion.3
  861.6 11.7 fusion.111
  950.5 131.5 %all-gather.17.cloned.1.call-done = bf16[2048,768]{1,0:T(8,128)(2,1)} async-done(((bf16[64,768]{1,0:T(8,128)(2,1)}), bf16[2048,768]{1,0:T(8,128)(2,1)}) %all-gather.17.cloned.1.call-update) | async-done | bytes 3145744 | tf_op jit(solution)/shard_map/all_gather | solution.py:357
  1089.3 68.2 %all-gather = f32[65536]{0:T(1024)S(1)} all-gather(f32[2048]{0:T(1024)S(1)} %get-tuple-element.233), channel_id=2, replica_groups=mesh['seq'=4,'dp'=32] {'dp'}, dimensions={0}, use_global_device_ids=true | all-gather | bytes 270336 | tf_op jit(solution)/shard_map/all_gather | solution.py:29
  1160.9 62.9 %all-gather.1 = f32[65536]{0:T(1024)S(1)} all-gather(f32[2048]{0:T(1024)S(1)} %get-tuple-element.98), channel_id=3, replica_groups=mesh['seq'=4,'dp'=32] {'dp'}, dimensions={0}, use_global_device_ids=true | all-gather | bytes 270336 | tf_op jit(solution)/shard_map/all_gather | solution.py:29
  1224.6 64.9 %all-gather.2 = f32[65536]{0:T(1024)S(1)} all-gather(f32[2048]{0:T(1024)S(1)} %get-tuple-element.97), channel_id=4, replica_groups=mesh['seq'=4,'dp'=32] {'dp'}, dimensions={0}, use_global_device_ids=true | all-gather | bytes 270336 | tf_op jit(solution)/shard_map/all_gather | solution.py:29
  1294.3 55.5 %while.14 = (s32[]{:T(128)}, f32[2048]{0:T(1024)S(1)}, f32[2048]{0:T(1024)S(1)}, f32[2048]{0:T(1024)S(1)}, f32[31,2048]{1,0:T(8,128)}, /*index=5*/f32[31,2048]{1,0:T(8,128)}, f32[31,2048]{1,0:T(8,128)}, s32[]{:T(128)}) while((s32[]{:T(128)}, f32[2048]{0:T(1024)S(1)}, f32[2048]{0:T(1024)S(1)}, f32[2048]{0:T(1024)S(1)}, ...), condition=%wide.region_20.22_spmd, body=%wide.region_19.21_spmd.sunk | while | flops 14338 | bytes 122981 | solution.py:32
  1349.8 11.8 fusion.94
  1361.7 210.3 %reduce-scatter.9.cloned.1.call-done = f32[64,768]{1,0:T(8,128)} async-done(((f32[2048,768]{1,0:T(8,128)}), f32[64,768]{1,0:T(8,128)}) %reduce-scatter.9.cloned.1.call-update) | async-done | bytes 196624 | tf_op jit(solution)/shard_map/reduce_scatter | solution.py:373
  1621.1 77.8 %reduce-scatter.11.cloned.1.call-done = f32[256,1536]{0,1:T(8,128)} async-done(((f32[1024,1536]{0,1:T(8,128)}), f32[256,1536]{0,1:T(8,128)}) %reduce-scatter.11.cloned.1.call-update) | async-done | bytes 1572880 | tf_op jit(solution)/shard_map/reduce_scatter | solution.py:213
  1751.7 58.4 %reduce-scatter.13.cloned.1.call-done = f32[256,1536]{0,1:T(8,128)} async-done(((f32[1024,1536]{0,1:T(8,128)}), f32[256,1536]{0,1:T(8,128)}) %reduce-scatter.13.cloned.1.call-update) | async-done | bytes 1572880 | tf_op jit(solution)/shard_map/reduce_scatter | solution.py:213
  1828.4 14.6 reshape.623
  1843.0 11.5 copy.162
  1859.6 13.8 reshape.621
  1873.5 16.5 copy.161
  1901.2 11.4 reshape.618
  1912.6 13.2 copy.159
  1933.5 14.6 reshape.616
  1948.1 11.5 copy.157
  1964.9 13.6 reshape.614
  1978.6 16.4 copy.156
  2003.0 27.1 pad_maximum_fusion.2
  2030.0 27.1 gather_fusion.5
  2057.2 28.2 broadcast_select_fusion
  2089.6 11.4 reshape.611
  2101.0 12.9 copy.154
  2115.5 24.9 pad_maximum_fusion.1
  2140.3 27.4 gather_fusion.4
  2167.8 27.5 broadcast_select_fusion.1
  2195.3 49.2 %pad_maximum_fusion = f32[384,192,192]{2,1,0:T(8,128)} fusion(f32[192,192,192]{2,1,0:T(8,128)} %broadcast_select_fusion, f32[192,192,192]{2,1,0:T(8,128)} %broadcast_select_fusion.1), kind=kLoop, calls=%fused_computation.14 | loop fusion | flops 14155776 | bytes 113246208 | tf_op jit(solution)/shard_map/concatenate | solution.py:403
  2244.7 66.9 %copy.163 = f32[384,192,192]{0,2,1:T(8,128)} copy(f32[384,192,192]{2,1,0:T(8,128)} %pad_maximum_fusion) | data formatting | bytes 113246208 | tf_op jit(solution)/shard_map/concatenate | solution.py:403
  2319.2 65.9 %psum.36 = f32[]{:T(128)} all-reduce(f32[]{:T(128)} %get-tuple-element.176), channel_id=1, replica_groups=mesh['seq'=4,'dp'=32] {'seq','dp'}, use_global_device_ids=true, to_apply=%region_24.26 | all-reduce | flops 1 | bytes 8 | tf_op jit(solution)/shard_map/psum | solution.py:418
  2387.6 12.9 fusion.95
  2400.5 65.9 %scatter_custom_fusion.1 = f32[1572,768]{1,0:T(8,128)} fusion(f32[1572,768]{1,0:T(8,128)} %fusion.95, s32[8192]{0:T(1024)} %bitcast.306, bf16[8192,768]{1,0:T(8,128)(2,1)} %all-gather.19.cloned.1.call-done, f32[]{:T(128)} %constant.70.clone.1, pred[8192]{0:T(1024)(128)(4,1)S(1)} %copy-done.83), kind=kCustom, calls=%fused_computation.17 | custom fusion | flops 18874368 | bytes 17420800 | tf_op jit(solution)/shard_map/scatter-add | solution.py:397
  2475.6 243.7 %all-reduce.5.cloned.1.call-done = (f32[384,36864]{0,1:T(8,128)}, f32[1024,768]{1,0:T(8,128)}, f32[26,768]{1,0:T(8,128)}) async-done(((f32[384,36864]{0,1:T(8,128)}, f32[1024,768]{1,0:T(8,128)}, f32[26,768]{1,0:T(8,128)}), (f32[384,36864]{0,1:T(8,128)}, f32[1024,768]{1,0:T(8,128)}, f32[26,768]{1,0:T(8,128)})) %all-reduce.5.cloned.1.call-update) | async-done | bytes 59848720
  2719.3 20.5 constant_dynamic-slice_fusion.5
  2739.8 10.7 copy.164
  2766.0 65.2 %all-reduce.1 = (f32[]{:T(128)}, f32[]{:T(128)}) all-reduce(f32[]{:T(128)} %fusion.81, f32[]{:T(128)S(6)} %add.471), channel_id=1, replica_groups=mesh['seq'=4,'dp'=32] {'seq','dp'}, use_global_device_ids=true, to_apply=%region_22.24 | all-reduce | flops 2 | bytes 16 | tf_op jit(solution)/shard_map/psum | solution.py:418
  (749 shorter events, 547.9 us)
Async XLA Ops:
  8.0 35.4 %all-gather.11.cloned.1.call-start = ((), (), s32[]{:S(2)}) async-start(), calls=%async_computation.5 | async-start | bytes 3041280 | tf_op jit(solution)/shard_map/all_gather | solution.py:299
  10.3 267.8 %reduce-scatter.7.cloned.1.call-start = ((), (), s32[]{:S(2)}) async-start(), calls=%async_computation.6 | async-start | bytes 12976128 | tf_op jit(solution)/shard_map/reduce_scatter | solution.py:325
  11.9 69.5 %copy-start.82 = (pred[8192]{0:T(1024)(128)(4,1)}, pred[8192]{0:T(1024)(128)(4,1)S(1)}, u32[]{:S(2)}) copy-start(pred[8192]{0:T(1024)(128)(4,1)S(1)} %and.43) | copy-start | bytes 24580
  94.7 183.3 %copy-start.38 = (f32[256,768]{1,0:T(8,128)S(1)}, f32[256,768]{1,0:T(8,128)}, u32[]{:S(2)}) copy-start(f32[256,768]{1,0:T(8,128)} %param.34) | copy-start | bytes 2359300
  94.8 454.7 %all-gather.21.cloned.1.call-start = ((), (), s32[]{:S(2)}) async-start(), calls=%async_computation.15 | async-start | bytes 38043648 | tf_op jit(solution)/shard_map/all_gather | solution.py:304
  96.6 722.7 %all-gather.13.cloned.1.call-start = ((), (), s32[]{:S(2)}) async-start(), calls=%async_computation.7 | async-start | bytes 3932160 | tf_op jit(solution)/shard_map/all_gather | solution.py:143
  100.7 567.1 %copy-start.87 = (f32[768]{0:T(1024)}, f32[768]{0:T(1024)S(1)}, u32[]{:S(2)}) copy-start(f32[768]{0:T(1024)S(1)} %get-tuple-element.130) | copy-start | bytes 9220
  100.7 567.1 %copy-start.96 = (f32[768]{0:T(1024)}, f32[768]{0:T(1024)S(1)}, u32[]{:S(2)}) copy-start(f32[768]{0:T(1024)S(1)} %get-tuple-element.129) | copy-start | bytes 9220
  100.7 746.2 %copy-start.72 = (f32[768]{0:T(1024)}, f32[768]{0:T(1024)S(1)}, u32[]{:S(2)}) copy-start(f32[768]{0:T(1024)S(1)} %get-tuple-element.125) | copy-start | bytes 9220
  100.7 746.2 %copy-start.76 = (f32[768]{0:T(1024)}, f32[768]{0:T(1024)S(1)}, u32[]{:S(2)}) copy-start(f32[768]{0:T(1024)S(1)} %get-tuple-element.124) | copy-start | bytes 9220
  279.2 566.8 %copy-start.6 = (f32[256,768]{1,0:T(8,128)}, f32[256,768]{1,0:T(8,128)S(1)}, u32[]{:S(2)}) copy-start(f32[256,768]{1,0:T(8,128)S(1)} %get-tuple-element.189) | copy-start | bytes 2359300
  279.2 388.6 %copy-start.102 = (f32[256]{0:T(256)}, f32[256]{0:T(256)S(1)}, u32[]{:S(2)}) copy-start(f32[256]{0:T(256)S(1)} %broadcast_multiply_fusion.7) | copy-start | bytes 3076
  279.5 301.4 %copy-start.138 = (f32[256]{0:T(256)}, f32[256]{0:T(256)S(1)}, u32[]{:S(2)}) copy-start(f32[256]{0:T(256)S(1)} %multiply_reduce_fusion.18) | copy-start | bytes 3076
  279.5 388.3 %copy-start.134 = (f32[256]{0:T(256)}, f32[256]{0:T(256)S(1)}, u32[]{:S(2)}) copy-start(f32[256]{0:T(256)S(1)} %fusion.76) | copy-start | bytes 3076
  673.0 240.7 %all-gather.15.cloned.1.call-start = ((), (), s32[]{:S(2)}) async-start(), calls=%async_computation.8 | async-start | bytes 3932160 | tf_op jit(solution)/shard_map/all_gather | solution.py:143
  674.7 153.6 %copy-start.40 = (bf16[256,768]{0,1:T(8,128)(2,1)}, bf16[256,768]{0,1:T(8,128)(2,1)S(1)}, u32[]{:S(2)}) copy-start(bf16[256,768]{0,1:T(8,128)(2,1)S(1)} %copy.139) | copy-start | bytes 1179652
  680.4 165.6 %copy-start.15 = (bf16[768,768]{1,0:T(8,128)(2,1)}, bf16[768,768]{1,0:T(8,128)(2,1)S(1)}, u32[]{:S(2)}) copy-start(bf16[768,768]{1,0:T(8,128)(2,1)S(1)} %reshape.590) | copy-start | bytes 3538948
  854.9 227.2 %all-gather.17.cloned.1.call-start = ((), (), s32[]{:S(2)}) async-start(), calls=%async_computation.9 | async-start | bytes 3244032 | tf_op jit(solution)/shard_map/all_gather | solution.py:357
  856.0 93.3 %copy-start.149 = (pred[64]{0:T(512)(128)(4,1)}, pred[64]{0:T(512)(128)(4,1)S(1)}, u32[]{:S(2)}) copy-start(pred[64]{0:T(512)(128)(4,1)S(1)} %get-tuple-element.177) | copy-start | bytes 196
  861.6 79.1 %copy-start.17 = (bf16[768,768]{1,0:T(8,128)(2,1)}, bf16[768,768]{1,0:T(8,128)(2,1)S(1)}, u32[]{:S(2)}) copy-start(bf16[768,768]{1,0:T(8,128)(2,1)S(1)} %reshape.601) | copy-start | bytes 3538948
  945.7 136.4 %copy-start.1 = (bf16[1572,768]{1,0:T(8,128)(2,1)S(1)}, bf16[1572,768]{1,0:T(8,128)(2,1)}, u32[]{:S(2)}) copy-start(bf16[1572,768]{1,0:T(8,128)(2,1)} %copy-done) | copy-start | bytes 7243780
  950.1 621.9 %reduce-scatter.9.cloned.1.call-start = ((), (), s32[]{:S(2)}) async-start(), calls=%async_computation.10 | async-start | bytes 6488064 | tf_op jit(solution)/shard_map/reduce_scatter | solution.py:373
  950.4 399.4 %copy-start.159 = (pred[2048]{0:T(1024)(128)(4,1)}, pred[2048]{0:T(1024)(128)(4,1)S(1)}, u32[]{:S(2)}) copy-start(pred[2048]{0:T(1024)(128)(4,1)S(1)} %ge.76) | copy-start | bytes 6148
  950.5 399.3 %copy-start.91 = (s32[2048]{0:T(1024)}, s32[2048]{0:T(1024)S(1)}, u32[]{:S(2)}) copy-start(s32[2048]{0:T(1024)S(1)} %sub.198) | copy-start | bytes 24580
  1089.3 71.7 %copy-start.8 = (f32[2048,1572]{0,1:T(8,128)}, f32[2048,1572]{0,1:T(8,128)S(1)}, u32[]{:S(2)}) copy-start(f32[2048,1572]{0,1:T(8,128)S(1)} %get-tuple-element.234) | copy-start | bytes 38633476
  1361.6 210.4 %copy-start.150 = (pred[64]{0:T(512)(128)(4,1)S(1)}, pred[64]{0:T(512)(128)(4,1)}, u32[]{:S(2)}) copy-start(pred[64]{0:T(512)(128)(4,1)} %copy-done.149) | copy-start | bytes 196
  1361.6 212.4 %copy-start.10 = (f32[256,768]{1,0:T(8,128)S(1)}, f32[256,768]{1,0:T(8,128)}, u32[]{:S(2)}) copy-start(f32[256,768]{1,0:T(8,128)} %copy-done.9) | copy-start | bytes 2359300
  1361.7 213.3 %copy-start.145 = (f32[256]{0:T(256)S(1)}, f32[256]{0:T(256)}, u32[]{:S(2)}) copy-start(f32[256]{0:T(256)} %copy-done.144) | copy-start | bytes 3076
  1361.7 337.2 %reduce-scatter.11.cloned.1.call-start = ((), (), s32[]{:S(2)}) async-start(), calls=%async_computation.11 | async-start | bytes 7864320 | tf_op jit(solution)/shard_map/reduce_scatter | solution.py:213
  1614.8 85.6 %copy-start.90 = (f32[768]{0:T(1024)S(1)}, f32[768]{0:T(1024)}, u32[]{:S(2)}) copy-start(f32[768]{0:T(1024)} %get-tuple-element.122) | copy-start | bytes 9220
  1614.8 85.6 %copy-start.105 = (f32[256]{0:T(256)S(1)}, f32[256]{0:T(256)}, u32[]{:S(2)}) copy-start(f32[256]{0:T(256)} %copy-done.104) | copy-start | bytes 3076
  1614.8 85.6 %copy-start.137 = (f32[256]{0:T(256)S(1)}, f32[256]{0:T(256)}, u32[]{:S(2)}) copy-start(f32[256]{0:T(256)} %copy-done.136) | copy-start | bytes 3076
  1614.8 195.2 %reduce-scatter.13.cloned.1.call-start = ((), (), s32[]{:S(2)}) async-start(), calls=%async_computation.12 | async-start | bytes 7864320 | tf_op jit(solution)/shard_map/reduce_scatter | solution.py:213
  1745.4 655.1 %all-gather.19.cloned.1.call-start = ((), (), s32[]{:S(2)}) async-start(), calls=%async_computation.13 | async-start | bytes 12976128 | tf_op jit(solution)/shard_map/all_gather | solution.py:396
  1819.5 899.8 %all-reduce.5.cloned.1.call-start = ((), (), s32[]{:S(2)}) async-start(), calls=%async_computation.16 | async-start | bytes 119734272
  2244.5 67.5 %copy-start.85 = (f32[4,768]{1,0:T(4,128)S(1)}, f32[4,768]{1,0:T(4,128)}, u32[]{:S(2)}) copy-start(f32[4,768]{1,0:T(4,128)} %reshape.637) | copy-start | bytes 36868
  2244.5 67.5 %copy-start.86 = (f32[4,768]{1,0:T(4,128)S(1)}, f32[4,768]{1,0:T(4,128)}, u32[]{:S(2)}) copy-start(f32[4,768]{1,0:T(4,128)} %reshape.636) | copy-start | bytes 36868
  2244.5 67.5 %copy-start.118 = (f32[1,768]{1,0:T(1,128)S(1)}, f32[1,768]{1,0:T(1,128)}, u32[]{:S(2)}) copy-start(f32[1,768]{1,0:T(1,128)} %reshape.629) | copy-start | bytes 9220
  2244.6 67.5 %copy-start.119 = (f32[1,768]{1,0:T(1,128)S(1)}, f32[1,768]{1,0:T(1,128)}, u32[]{:S(2)}) copy-start(f32[1,768]{1,0:T(1,128)} %reshape.630) | copy-start | bytes 9220
  2244.6 67.5 %copy-start.120 = (f32[1,768]{1,0:T(1,128)S(1)}, f32[1,768]{1,0:T(1,128)}, u32[]{:S(2)}) copy-start(f32[1,768]{1,0:T(1,128)} %reshape.634) | copy-start | bytes 9220
  2244.6 67.5 %copy-start.121 = (f32[1,768]{1,0:T(1,128)S(1)}, f32[1,768]{1,0:T(1,128)}, u32[]{:S(2)}) copy-start(f32[1,768]{1,0:T(1,128)} %reshape.635) | copy-start | bytes 9220
  2244.6 67.5 %copy-start.122 = (f32[1,768]{1,0:T(1,128)S(1)}, f32[1,768]{1,0:T(1,128)}, u32[]{:S(2)}) copy-start(f32[1,768]{1,0:T(1,128)} %stack.33) | copy-start | bytes 9220
  2244.6 67.5 %copy-start.123 = (f32[1,768]{1,0:T(1,128)S(1)}, f32[1,768]{1,0:T(1,128)}, u32[]{:S(2)}) copy-start(f32[1,768]{1,0:T(1,128)} %broadcast_in_dim.232) | copy-start | bytes 9220
  2244.6 67.5 %copy-start.124 = (f32[1,768]{1,0:T(1,128)S(1)}, f32[1,768]{1,0:T(1,128)}, u32[]{:S(2)}) copy-start(f32[1,768]{1,0:T(1,128)} %reshape.627) | copy-start | bytes 9220
  2319.1 67.9 %copy-start.66 = (f32[3,36864]{1,0:T(4,128)S(1)}, f32[3,36864]{1,0:T(4,128)}, u32[]{:S(2)}) copy-start(f32[3,36864]{1,0:T(4,128)} %param.41) | copy-start | bytes 1327108
  2319.1 68.4 %copy-start.92 = (s32[2048]{0:T(1024)S(1)}, s32[2048]{0:T(1024)}, u32[]{:S(2)}) copy-start(s32[2048]{0:T(1024)} %copy-done.91) | copy-start | bytes 24580
  2319.1 68.4 %copy-start.133 = (f32[2048]{0:T(1024)S(1)}, f32[2048]{0:T(1024)}, u32[]{:S(2)}) copy-start(f32[2048]{0:T(1024)} %copy-done.132) | copy-start | bytes 24580
  2319.1 441.5 %reduce-scatter.15.cloned.1.call-start = ((), (), s32[]{:S(2)}) async-start(), calls=%async_computation.14 | async-start | bytes 6082560 | tf_op jit(solution)/shard_map/reduce_scatter | solution.py:400
  (147 other events, 2232.5 us)
Sparse Core Ops, SparseCore 0:
  11.1 32.2 all-gather.10
  94.9 183.1 reduce-scatter.6
  673.1 30.1 all-gather.12
  855.0 30.1 all-gather.14
  950.2 131.8 all-gather.16
  1361.8 210.1 reduce-scatter.8
  1614.9 83.9 reduce-scatter.10
  1745.4 64.5 reduce-scatter.12
  1819.6 158.9 all-gather.18
  2473.1 51.8 reduce-scatter.14
Sparse Core Ops, SparseCore 1:
  97.5 451.9 all-gather.20
  2319.2 400.0 all-reduce.4
where the time goes:
time: 2880 us; the launch traced here: 2860 us
  waiting for transfers between devices  1200 us (42%)
  local copies, waits for them, and re-layouts  782 us (27%)
  other arithmetic  331 us (11%)
  blocking collectives  327 us (11%)
  matrix products  195 us (7%)
    all_gather x1, waiting for transfers between devices, shards(): lax.all_gather(weights.astype(jnp.bfloat16), ('seq', 'dp'), axis=0, tiled...  270 us
    unnamed x13, waiting for transfers between devices  244 us
    reduce_scatter x1, waiting for transfers between devices, shards(): lax.psum_scatter(product(grad_logits, table_bf), 'dp', scatter_dimension=...  210 us
    all_gather x3, blocking collectives, joined(): pieces = jax.tree.map(lambda part: lax.all_gather(part, axis), value)  196 us
    reduce_scatter x1, waiting for transfers between devices, shards(): lax.psum_scatter(jnp.where(inside[:, None], found.astype(jnp.float32), 0....  177 us
    reduce_scatter x2, waiting for transfers between devices, layer_backward(): lax.psum_scatter(jnp.concatenate([grad_keys, grad_values], axis=1), 'seq'...  136 us
    reshape x10, local copies, waits for them, and re-layouts, disassemble(): grid = matrix.reshape(row_count, BS, col_count, BS).transpose(0, 2, 1, 3)  135 us
    all_gather x1, waiting for transfers between devices, shards(): gathered = lax.all_gather(chosen, 'dp', axis=0, tiled=True)  132 us
  transfers between devices with their start and end apart: 12, of which 8 were waited for; matrix products, arithmetic and copies ran while one was open for 30% of the time, Pallas kernels for 0%

commit v1 on v0

v1 whole, which is shorter than its diff:
```python
import functools

import jax
import jax.numpy as jnp
from jax import lax
from jax.experimental import pallas as pl
from jax.experimental.pallas import tpu as pltpu
from jax.sharding import PartitionSpec as P

HEADS = 12
HEAD_DIM = 64
LAYERS = 2
BS = 192
STEP = 10
PACK = 288
LANES = 128
HALF = 96

exact_prec = lax.Precision.HIGHEST
clip_bound = 0.02
ewc_weight = 1000000.0
fisher_decay = 0.8
first_decay = 0.9
second_decay = 0.999
adam_epsilon = 1e-08
table_rate = 0.05
small_rate = 0.1
decay_rate = 0.1
stat_decay = 0.9
shampoo_rate = 0.02
graft_epsilon = 1e-06

BF = jnp.bfloat16
F32 = jnp.float32


def line(zh, c, y, zl, x):
    return (zh * 2 + c) * 32 + y * 8 + zl * 4 + x


def moved(axis, step, zh, c, y, zl, x):
    z = zh * 2 + zl
    if axis == "x":
        x = step(x, c)
    elif axis == "y":
        y = step(y, c)
    elif axis == "z":
        z = step(z, c)
        zh, zl = z // 2, z % 2
    elif axis == "c":
        c = 1 - c
    elif axis == "zl":
        zl = 1 - zl
    elif axis == "zh":
        zh = 1 - zh
    return zh, c, y, zl, x


COORDS = [
    (zh, c, y, zl, x)
    for zh in range(2)
    for c in range(2)
    for y in range(4)
    for zl in range(2)
    for x in range(4)
]


def permuted(value, axis, step, keep=None):
    pairs = [
        (line(*at), line(*moved(axis, step, *at))) for at in COORDS if keep is None or keep(*at)
    ]
    return lax.ppermute(value, ("seq", "dp"), pairs)


def turn(value, axis, amount):
    return permuted(value, axis, lambda at, c: (at + (amount if c == 0 else -amount)) % 4)


def swap(value, axis):
    return permuted(value, axis, None)


def crossed(value, axis, mask):
    return permuted(value, axis, lambda at, c: at ^ mask)


def z_flip(value):
    return turn(turn(value, "z", 1), "z", 1)


def gather4(value, axis):
    near = turn(value, axis, -1)
    other = turn(value, axis, 1)
    return [value, near, turn(near, axis, -1), other]


def gather4_direct(value, axis):
    return [value, turn(value, axis, -1), turn(value, axis, 2), turn(value, axis, 1)]


def wide(value):
    return value.astype(F32)


def reduce4(parts, axis, kind):
    first = turn(parts[2].astype(kind), axis, 1)
    onward = (wide(parts[1]) + wide(first)).astype(kind)
    near = turn(onward, axis, 1)
    other = turn(parts[3].astype(kind), axis, -1)
    return wide(parts[0]) + wide(near) + wide(other)


def reduce4_direct(parts, axis, kind):
    near = turn(parts[1].astype(kind), axis, 1)
    far = turn(parts[2].astype(kind), axis, 2)
    other = turn(parts[3].astype(kind), axis, -1)
    return wide(parts[0]) + wide(near) + wide(far) + wide(other)


def sum_everywhere(value):
    value = value + swap(value, "c")
    for axis in ("z", "y", "x"):
        one, two, three = (crossed(value, axis, mask) for mask in (1, 2, 3))
        value = (value + one) + (two + three)
    return value


def pack_blocks(blocks, odd):
    odd = odd[:, None, None]
    main = jnp.where(odd, blocks[:, :, BS - LANES :], blocks[:, :, :LANES])
    half = jnp.where(odd, blocks[:, :, : BS - LANES], blocks[:, :, LANES:])
    top, low = half[:, :HALF], half[:, HALF:]
    rest = jnp.concatenate([jnp.where(odd, low, top), jnp.where(odd, top, low)], axis=2)
    return jnp.concatenate([main, rest], axis=1)


def unpack_blocks(packed, odd):
    odd = odd[:, None, None]
    main, rest = packed[:, :BS], packed[:, BS:]
    left, right = rest[:, :, : LANES // 2], rest[:, :, LANES // 2 :]
    half = jnp.concatenate([jnp.where(odd, right, left), jnp.where(odd, left, right)], axis=1)
    return jnp.where(
        odd, jnp.concatenate([half, main], axis=2), jnp.concatenate([main, half], axis=2)
    )


def pieces_of(chunk):
    return (("y", 8, 4), ("x", 8, 4), ("zl", 16, 2))[chunk]


def inner_moves(chunk):
    if chunk == 0:
        return [(my, kz, mx) for my in range(4) for mx in range(4) for kz in range(2)]
    if chunk == 1:
        return [(my, kz, mx) for mx in range(4) for my in range(4) for kz in range(2)]
    return [(my, kz, mx) for kz in range(2) for my in range(4) for mx in range(4)]


MATRICES = ((0, 4, 12), (48, 4, 4), (64, 4, 16), (128, 16, 4))


def assemble_kernel(places, *refs):
    arrays, outs, (natural, sem) = refs[:20], refs[20:24], refs[24:]
    at = 0
    for array in arrays:
        count = array.shape[0]

        def fetch(q, carry, array=array, at=at):
            pltpu.make_async_copy(array.at[q], natural.at[places[at + q]], sem).start()
            return carry

        lax.fori_loop(0, count, fetch, 0)
        at += count
    pltpu.make_async_copy(natural, natural, sem).wait()
    left = lax.broadcasted_iota(jnp.int32, (HALF, LANES), 1) < LANES // 2
    for out, (base, tall, across) in zip(outs, MATRICES, strict=True):
        pairs = across // 2

        def place(t, carry, out=out, base=base, pairs=pairs):
            row = pl.multiple_of((t // pairs) * BS, HALF)
            col = pl.multiple_of((t % pairs) * 2 * BS, LANES)
            even, odd = base + 2 * t, base + 2 * t + 1
            out[pl.ds(row, BS), pl.ds(col, LANES)] = natural[even, :BS]
            out[pl.ds(row, BS), pl.ds(col + 2 * LANES, LANES)] = natural[odd, :BS]
            he, ho = wide(natural[even, BS:]), wide(natural[odd, BS:])
            out[pl.ds(row, HALF), pl.ds(col + LANES, LANES)] = jnp.where(left, he, ho).astype(BF)
            out[pl.ds(row + HALF, HALF), pl.ds(col + LANES, LANES)] = pltpu.roll(
                jnp.where(left, ho, he), LANES // 2, 1
            ).astype(BF)
            return carry

        lax.fori_loop(0, tall * pairs, place, 0)


def assemble_layer(places, arrays):
    shapes = [jax.ShapeDtypeStruct((t * BS, a * BS), BF) for _, t, a in MATRICES]
    return pl.pallas_call(
        assemble_kernel,
        grid_spec=pltpu.PrefetchScalarGridSpec(
            num_scalar_prefetch=1,
            grid=(),
            in_specs=[pl.BlockSpec(memory_space=pl.ANY)] * len(arrays),
            out_specs=[pl.BlockSpec(memory_space=pltpu.VMEM)] * 4,
            scratch_shapes=[pltpu.VMEM((BS, PACK, LANES), BF), pltpu.SemaphoreType.DMA],
        ),
        out_shape=shapes,
        compiler_params=pltpu.CompilerParams(vmem_limit_bytes=40 * 1024 * 1024),
        cost_estimate=pl.CostEstimate(flops=0, bytes_accessed=29_000_000, transcendentals=0),
        name="assemble",
    )(places, *arrays)


def weight_grad_kernel(places, *refs):
    lefts, rights, outs, (natural, sem) = refs[:4], refs[4:8], refs[8:14], refs[14:]
    left = lax.broadcasted_iota(jnp.int32, (HALF, LANES), 1) < LANES // 2
    for lhs, rhs, (base, tall, across) in zip(lefts, rights, MATRICES, strict=True):
        pairs = across // 2

        def unit(t, carry, lhs=lhs, rhs=rhs, base=base, across=across, pairs=pairs):
            rows, cols = t // pairs, t % pairs
            span = 2 * BS
            piece = lax.dot_general(
                lhs[:, pl.ds(pl.multiple_of(rows * span, LANES), span)],
                rhs[:, pl.ds(pl.multiple_of(cols * span, LANES), span)],
                (((0,), (0,)), ((), ())),
                preferred_element_type=F32,
            )
            for r in range(2):
                even = base + (2 * rows + r) * across + 2 * cols
                strip = piece[r * BS : (r + 1) * BS]
                natural[even, :BS] = strip[:, :LANES].astype(BF)
                natural[even + 1, :BS] = strip[:, 2 * LANES :].astype(BF)
                mid = strip[:, LANES : 2 * LANES]
                top = mid[:HALF]
                low = pltpu.roll(mid[HALF:], LANES // 2, 1)
                natural[even, BS:] = jnp.where(left, top, low).astype(BF)
                natural[even + 1, BS:] = jnp.where(left, low, top).astype(BF)
            return carry

        lax.fori_loop(0, (tall // 2) * pairs, unit, 0)
    at = 0
    for out in outs:

        def put(q, carry, out=out, at=at):
            pltpu.make_async_copy(natural.at[places[at + q]], out.at[q], sem).start()
            return carry

        lax.fori_loop(0, 32, put, 0)
        at += 32
    pltpu.make_async_copy(natural, natural, sem).wait()


def weight_grads(places, lefts, rights):
    return pl.pallas_call(
        weight_grad_kernel,
        grid_spec=pltpu.PrefetchScalarGridSpec(
            num_scalar_prefetch=1,
            grid=(),
            in_specs=[pl.BlockSpec(memory_space=pltpu.VMEM)] * 8,
            out_specs=[pl.BlockSpec(memory_space=pl.ANY)] * 6,
            scratch_shapes=[pltpu.VMEM((BS, PACK, LANES), BF), pltpu.SemaphoreType.DMA],
        ),
        out_shape=[jax.ShapeDtypeStruct((32, PACK, LANES), BF)] * 6,
        compiler_params=pltpu.CompilerParams(vmem_limit_bytes=40 * 1024 * 1024),
        cost_estimate=pl.CostEstimate(
            flops=2 * 256 * 7_077_888, bytes_accessed=21_000_000, transcendentals=0
        ),
        name="weight_grads",
    )(places, *lefts, *rights)


def lookup_kernel(ids, table, out0, out1, out2, out3):
    rows = table.shape[0]
    lane = lax.broadcasted_iota(jnp.int32, (ids.shape[0], LANES), 1)
    held = ids[...]
    hot = jnp.concatenate(
        [jnp.where(held == lane + at, 1.0, 0.0).astype(BF) for at in range(0, rows, LANES)], axis=1
    )
    found = jnp.dot(hot, table[...], preferred_element_type=F32).astype(BF)
    out0[...] = found[:, :256]
    out1[...] = found[:, 256:512]
    out2[...] = found[:256, 512:]
    out3[...] = found[256:, 512:]


def lookup(ids, table):
    tokens = ids.shape[0]
    steps = tokens // 512
    return pl.pallas_call(
        lookup_kernel,
        grid=(steps,),
        in_specs=[
            pl.BlockSpec((512, LANES), lambda t: (t, 0)),
            pl.BlockSpec(table.shape, lambda t: (0, 0)),
        ],
        out_specs=[
            pl.BlockSpec((512, 256), lambda t: (t, 0)),
            pl.BlockSpec((512, 256), lambda t: ((t % 4) * 4 + t // 4, 0)),
            pl.BlockSpec((256, 256), lambda t: (t, 0)),
            pl.BlockSpec((256, 256), lambda t: (t, 0)),
        ],
        out_shape=[
            jax.ShapeDtypeStruct((tokens, 256), BF),
            jax.ShapeDtypeStruct((tokens, 256), BF),
            jax.ShapeDtypeStruct((tokens // 2, 256), BF),
            jax.ShapeDtypeStruct((tokens // 2, 256), BF),
        ],
        compiler_params=pltpu.CompilerParams(vmem_limit_bytes=40 * 1024 * 1024),
        cost_estimate=pl.CostEstimate(
            flops=2 * tokens * table.shape[0] * 768, bytes_accessed=20_000_000, transcendentals=0
        ),
        name="lookup",
    )(ids, table)


def scatter_kernel(order, ids, start, part0, part1, part2, part3, out, sums):
    step = pl.program_id(0)

    @pl.when(step == 0)
    def _():
        out[...] = start[...]
        sums[...] = jnp.zeros(sums.shape, F32)

    rows, tokens = out.shape[0], ids.shape[2]
    place = lax.broadcasted_iota(jnp.int32, (rows, tokens), 0)
    hot = jnp.where(place == ids[0], 1.0, 0.0).astype(BF)
    last = jnp.concatenate([part2[...], part3[...]], axis=0)
    for at, part in enumerate((part0[...], part1[...], last)):
        cols = slice(at * 256, (at + 1) * 256)
        out[:, cols] += jnp.dot(hot, part, preferred_element_type=F32)
        sums[:, cols] += wide(part[:256]) + wide(part[256:])


def scatter_rows(order, ids, start, parts):
    return pl.pallas_call(
        scatter_kernel,
        grid_spec=pltpu.PrefetchScalarGridSpec(
            num_scalar_prefetch=1,
            grid=(16,),
            in_specs=[
                pl.BlockSpec((1, 1, 512), lambda t, order: (order[0, t], 0, 0)),
                pl.BlockSpec(start.shape, lambda t, order: (0, 0)),
                pl.BlockSpec((512, 256), lambda t, order: (order[0, t], 0)),
                pl.BlockSpec((512, 256), lambda t, order: (order[1, t], 0)),
                pl.BlockSpec((256, 256), lambda t, order: (order[0, t], 0)),
                pl.BlockSpec((256, 256), lambda t, order: (order[0, t], 0)),
            ],
            out_specs=[
                pl.BlockSpec(start.shape, lambda t, order: (0, 0)),
                pl.BlockSpec((256, 768), lambda t, order: (0, 0)),
            ],
        ),
        out_shape=[
            jax.ShapeDtypeStruct(start.shape, F32),
            jax.ShapeDtypeStruct((256, 768), F32),
        ],
        compiler_params=pltpu.CompilerParams(vmem_limit_bytes=48 * 1024 * 1024),
        cost_estimate=pl.CostEstimate(
            flops=2 * 8192 * start.shape[0] * 768, bytes_accessed=25_000_000, transcendentals=0
        ),
        name="scatter_rows",
    )(order, ids, start, *parts)


def product(left, right):
    return jnp.dot(left, right, preferred_element_type=F32)


def product_nt(left, right):
    return lax.dot_general(left, right, (((1,), (1,)), ((), ())), preferred_element_type=F32)


def product_tn(left, right):
    return lax.dot_general(left, right, (((0,), (0,)), ((), ())), preferred_element_type=F32)


def exact_mm(left, right):
    return jnp.dot(left, right, precision=exact_prec, preferred_element_type=F32)


def layer_norm(values_in, gain, shift):
    centre = jnp.mean(values_in, axis=-1, keepdims=True)
    cent = values_in - centre
    spread = jnp.mean(cent * cent, axis=-1, keepdims=True)
    return cent * lax.rsqrt(spread + 1e-05) * gain + shift


def layer_params(small_params, layer_idx):
    gain_rows = 2 * LAYERS + 1
    base_row = 2 * gain_rows + 8 * layer_idx
    model_width = small_params.shape[1]
    bias_qkv = jnp.concatenate(
        [small_params[base_row], jnp.zeros((model_width,), F32), small_params[base_row + 1]]
    )
    return (
        small_params[2 * layer_idx],
        small_params[2 * layer_idx + 1],
        small_params[gain_rows + 2 * layer_idx],
        small_params[gain_rows + 2 * layer_idx + 1],
        bias_qkv,
        small_params[base_row + 2],
        small_params[base_row + 3 : base_row + 7].reshape(-1),
        small_params[base_row + 7],
    )


def attend(queries_bf, key_values, doc_mask):
    model_width = queries_bf.shape[1]
    queries = queries_bf.reshape(-1, HEADS, HEAD_DIM)
    key_heads = key_values[:, :model_width].reshape(-1, HEADS, HEAD_DIM)
    scores = jnp.einsum("qhd,khd->hqk", queries, key_heads, preferred_element_type=F32) * 0.125
    scores = jnp.where(doc_mask[None], scores, -1e30)
    peak = jnp.max(scores, axis=-1, keepdims=True)
    expo = jnp.exp(scores - peak)
    return expo / jnp.sum(expo, axis=-1, keepdims=True)


def gather_pairs(own):
    core = swap(own, "c")
    far = z_flip(own)
    return jnp.concatenate([own, core, far, swap(far, "c")], axis=0)


def reduce_pairs(grad):
    span = grad.shape[0] // 4
    own, core, far, both = (grad[m * span : (m + 1) * span] for m in range(4))
    far = (far + swap(both, "c")).astype(BF)
    own = own + swap(core, "c")
    return own + wide(z_flip(far))


def layer_forward(residual, mats, params, doc_mask):
    w_qkv, w_proj, w_fc, w_out = mats
    gain_a, gain_b, shift_a, shift_b, bias_qkv, bias_proj, bias_fc, bias_out = params
    model_width = residual.shape[1]
    normed = layer_norm(residual, gain_a, shift_a).astype(BF)
    qkv_bf = (product(normed, w_qkv) + bias_qkv).astype(BF)
    key_values = gather_pairs(qkv_bf[:, model_width:])
    soft_probs = attend(qkv_bf[:, :model_width], key_values, doc_mask)
    value_heads = key_values[:, model_width:].reshape(-1, HEADS, HEAD_DIM)
    attended = jnp.einsum(
        "hqk,khd->qhd", soft_probs.astype(BF), value_heads, preferred_element_type=F32
    )
    attended = attended.reshape(-1, model_width).astype(BF)
    middle = residual + product(attended, w_proj) + bias_proj
    normed_b = layer_norm(middle, gain_b, shift_b).astype(BF)
    inner_pre = product(normed_b, w_fc) + bias_fc
    activated = jax.nn.gelu(inner_pre, approximate=True).astype(BF)
    result = middle + product(activated, w_out) + bias_out
    return (
        result,
        (residual, qkv_bf, key_values, attended, middle, normed_b, inner_pre, activated),
    )


def layer_backward(grad_in, kept_values, mats, params, doc_mask):
    residual, qkv_bf, key_values, attended, middle, normed_b, inner_pre, activated = kept_values
    w_qkv, w_proj, w_fc, w_out = mats
    gain_a, gain_b, shift_a, shift_b = params[:4]
    model_width = residual.shape[1]
    grad_out = grad_in.astype(BF)
    b_out = jnp.sum(wide(grad_out), axis=0)
    _, gelu_back = jax.vjp(lambda inner_in: jax.nn.gelu(inner_in, approximate=True), inner_pre)
    grad_inner = gelu_back(product_nt(grad_out, w_out))[0].astype(BF)
    b_fc = jnp.sum(wide(grad_inner), axis=0)
    _, norm_back_b = jax.vjp(layer_norm, middle, gain_b, shift_b)
    grad_mid, g_gain_b, g_shift_b = norm_back_b(product_nt(grad_inner, w_fc))
    grad_mid = grad_mid + grad_in
    grad_branch = grad_mid.astype(BF)
    b_proj = jnp.sum(wide(grad_branch), axis=0)
    grad_att = product_nt(grad_branch, w_proj).astype(BF)
    soft_probs = attend(qkv_bf[:, :model_width], key_values, doc_mask)
    seq_len = key_values.shape[0]
    queries = qkv_bf[:, :model_width].reshape(-1, HEADS, HEAD_DIM)
    key_heads = key_values[:, :model_width].reshape(seq_len, HEADS, HEAD_DIM)
    value_heads = key_values[:, model_width:].reshape(seq_len, HEADS, HEAD_DIM)
    grad_heads = grad_att.reshape(-1, HEADS, HEAD_DIM)
    grad_prob = jnp.einsum("qhd,khd->hqk", grad_heads, value_heads, preferred_element_type=F32)
    grad_score = soft_probs * (grad_prob - jnp.sum(soft_probs * grad_prob, axis=-1, keepdims=True))
    grad_score = grad_score.astype(BF)
    grad_query = (
        jnp.einsum("hqk,khd->qhd", grad_score, key_heads, preferred_element_type=F32).reshape(
            -1, model_width
        )
        * 0.125
    )
    grad_keys = (
        jnp.einsum("hqk,qhd->khd", grad_score, queries, preferred_element_type=F32).reshape(
            seq_len, model_width
        )
        * 0.125
    )
    grad_values = jnp.einsum(
        "hqk,qhd->khd", soft_probs.astype(BF), grad_heads, preferred_element_type=F32
    ).reshape(seq_len, model_width)
    grad_pairs = reduce_pairs(jnp.concatenate([grad_keys, grad_values], axis=1))
    grad_mixed = jnp.concatenate([grad_query, grad_pairs], axis=1).astype(BF)
    normed_a, norm_back_a = jax.vjp(layer_norm, residual, gain_a, shift_a)
    mixed_sums = jnp.sum(wide(grad_mixed), axis=0)
    grad_resid, g_gain_a, g_shift_a = norm_back_a(product_nt(grad_mixed, w_qkv))
    grad_resid = grad_resid + grad_mid
    bias_rows = jnp.concatenate(
        [
            jnp.stack([mixed_sums[:model_width], mixed_sums[2 * model_width :], b_proj]),
            b_fc.reshape(-1, model_width),
            b_out[None],
        ],
        axis=0,
    )
    return (
        grad_resid,
        (
            (normed_a.astype(BF), attended, normed_b, activated),
            (grad_mixed, grad_branch, grad_inner, grad_out),
        ),
        (g_gain_a, g_gain_b, g_shift_a, g_shift_b, bias_rows),
    )


def merge_stats(first_part, second_part):
    peak = jnp.maximum(first_part[0], second_part[0])
    summed = first_part[1] * jnp.exp(first_part[0] - peak) + second_part[1] * jnp.exp(
        second_part[0] - peak
    )
    return jnp.stack([peak, summed, first_part[2] + second_part[2]])


def adam_update(param, grad, first, second, rate, decay):
    first = first_decay * first + (1.0 - first_decay) * grad
    second = second_decay * second + (1.0 - second_decay) * grad * grad
    fixed_first = first / (1.0 - first_decay**STEP)
    fixed_second = second / (1.0 - second_decay**STEP)
    return (
        param - rate * (fixed_first / (jnp.sqrt(fixed_second) + adam_epsilon) + decay * param),
        first,
        second,
    )


def squared_blocks(flat):
    return flat.reshape(-1, BS, BS)


def gather_weights(packed, layer_idx, z_hi):
    from_there = permuted(packed, "zh", None, keep=lambda zh, c, y, zl, x: zh == layer_idx)
    mine = jnp.where(z_hi == layer_idx, packed, from_there)
    arrays = []
    for chunk in range(3):
        value = mine[chunk : chunk + 1]
        if chunk < 2:
            value = jnp.concatenate([value, swap(value, "zl")], axis=0)
            first, last = (("x", "y"), ("y", "x"))[chunk]
            value = jnp.concatenate(gather4(value, first), axis=0)
            arrays += gather4(value, last)
        else:
            value = jnp.concatenate(gather4(value, "x"), axis=0)
            value = jnp.concatenate(gather4(value, "y"), axis=0)
            arrays += [value, swap(value, "zl")]
    return arrays + [swap(value, "c") for value in arrays]


def reduce_weights(arrays, layer_idx, z_hi):
    blocks = []
    for chunk in range(3):
        mine, theirs = arrays[chunk], swap(arrays[3 + chunk], "c")
        axis, size, count = pieces_of(chunk)
        parts = [
            wide(mine[p * size : (p + 1) * size]) + wide(theirs[p * size : (p + 1) * size])
            for p in range(count)
        ]
        if chunk < 2:
            value = reduce4(parts, axis, BF)
            other = "x" if axis == "y" else "y"
            value = reduce4([value[2 * m : 2 * m + 2] for m in range(4)], other, BF)
            value = value[:1] + wide(swap(value[1:].astype(BF), "zl"))
        else:
            value = parts[0] + wide(swap(parts[1].astype(BF), "zl"))
            value = reduce4([value[4 * m : 4 * m + 4] for m in range(4)], "y", BF)
            value = reduce4([value[m : m + 1] for m in range(4)], "x", BF)
        blocks.append(value)
    value = jnp.concatenate(blocks, axis=0)
    from_there = permuted(value, "zh", None, keep=lambda zh, c, y, zl, x: zh != layer_idx)
    return value + from_there


def shards(
    token_ids,
    doc_ids,
    pick_slots,
    labels,
    vocab_table,
    vocab_first,
    vocab_second,
    positions,
    positions_first,
    positions_second,
    small_params,
    small_first,
    small_second,
    weights,
    stat_left,
    stat_right,
    root_left,
    root_right,
    anchor,
    fisher,
    owners,
):
    row_at = lax.axis_index("dp")
    seq_at = lax.axis_index("seq")
    z_hi, core = seq_at // 2, seq_at % 2
    y_at, zl_at, x_at = row_at // 8, (row_at // 4) % 2, row_at % 4
    span_len = token_ids.shape[1]
    model_width = small_params.shape[1]
    half_width = model_width // 2
    table_rows = vocab_table.shape[0]
    padded = -(-table_rows // 64) * 64
    vocab_start = row_at * 2 * table_rows
    shift_up, shift_down = jnp.array([0, 1, 2, 3]), jnp.array([0, 3, 2, 1])
    own_shift = jnp.where(core == 0, shift_up, shift_down)
    other_shift = jnp.where(core == 0, shift_down, shift_up)

    places = []
    for layer_idx in range(LAYERS):
        slots = []
        for kc in range(2):
            shift = own_shift if kc == 0 else other_shift
            for chunk in range(3):
                moves = jnp.array(inner_moves(chunk))
                at_y = (y_at + shift[moves[:, 0]]) % 4
                at_z = zl_at ^ moves[:, 1]
                at_x = (x_at + shift[moves[:, 2]]) % 4
                slots.append(((((core ^ kc) * 4 + at_y) * 2 + at_z) * 4 + at_x) * 3 + chunk)
        places.append(jnp.take(owners[layer_idx], jnp.concatenate(slots), axis=0))
    own_slots = (core * 32 + row_at) * 3 + jnp.arange(3)
    own_tiles = jnp.take(
        jnp.where(z_hi == 0, owners[0], owners[1]), own_slots, axis=0
    )
    own_odd = own_tiles % 2 == 1

    own_part = jnp.pad(vocab_table.astype(BF), ((0, padded - table_rows), (0, 0)))
    far_part = z_flip(own_part)
    both_parts = jnp.stack([own_part, far_part])
    near_parts = jnp.stack([swap(own_part, "c"), swap(far_part, "c")])
    table_bf = jnp.where(
        core == 0,
        jnp.concatenate([both_parts, near_parts], axis=2),
        jnp.concatenate([near_parts, both_parts], axis=2),
    ).reshape(2 * padded, model_width)
    vocab_rows = 2 * padded
    row_used = jnp.arange(vocab_rows) % padded < table_rows

    def local_row(ids):
        offset = ids - vocab_start
        inside = (offset >= 0) & (offset < 2 * table_rows)
        return jnp.where(inside, ((offset % 2) ^ z_hi) * padded + offset // 2, -1)

    packed = pack_blocks(squared_blocks(weights).astype(BF), own_odd)
    layer_weights = [
        assemble_layer(places[layer_idx], gather_weights(packed, layer_idx, z_hi))
        for layer_idx in range(LAYERS)
    ]
    all_params = [layer_params(small_params, layer_idx) for layer_idx in range(LAYERS)]

    far_y = (y_at + own_shift) % 4
    far_x = (x_at + own_shift) % 4
    far_z = zl_at ^ jnp.arange(2)
    rows_xyz = far_y[None, :, None] * 8 + far_z[None, None, :] * 4 + far_x[:, None, None]
    token_rows = local_row(jnp.take(token_ids, rows_xyz.reshape(-1), axis=0))
    spread_ids = jnp.broadcast_to(token_rows.reshape(-1, 1), (token_rows.size, LANES))
    found0, found1, found2, found3 = lookup(spread_ids, table_bf)

    def quarters(value):
        return jnp.split(value, 4, axis=0)

    def plain_reduce4(parts, axis):
        near = turn(parts[1] + turn(parts[2], axis, 1), axis, 1)
        return (parts[0] + near) + turn(parts[3], axis, -1)

    def last_pair(value):
        return value[:span_len] + swap(value[span_len:], "zl")

    looked = [
        last_pair(plain_reduce4(quarters(plain_reduce4(quarters(found0), "x")), "y")),
        last_pair(plain_reduce4(quarters(plain_reduce4(quarters(found1), "y")), "x")),
        plain_reduce4(quarters(plain_reduce4(quarters(found2 + swap(found3, "zl")), "x")), "y"),
    ]
    residual = wide(jnp.concatenate(looked, axis=1)) + positions

    doc_row = doc_ids[0]
    query_places = seq_at * span_len + jnp.arange(span_len)
    own_docs = lax.dynamic_slice_in_dim(doc_row, seq_at * span_len, span_len)
    part_order = seq_at ^ jnp.arange(4)
    key_places = (part_order[:, None] * span_len + jnp.arange(span_len)[None]).reshape(-1)
    key_docs = jnp.take(doc_row.reshape(4, span_len), part_order, axis=0).reshape(-1)
    doc_mask = (query_places[:, None] >= key_places[None, :]) & (
        own_docs[:, None] == key_docs[None, :]
    )
    kept_layers = []
    for layer_idx in range(LAYERS):
        residual, kept_values = layer_forward(
            residual, layer_weights[layer_idx], all_params[layer_idx], doc_mask
        )
        kept_layers.append(kept_values)
    gain_rows = 2 * LAYERS + 1
    final_norm, final_back = jax.vjp(
        layer_norm, residual, small_params[2 * LAYERS], small_params[gain_rows + 2 * LAYERS]
    )
    final_bf = final_norm.astype(BF)

    pick_dev = pick_slots.shape[1]
    half_picks = pick_dev // 2
    own_picks = lax.dynamic_index_in_dim(pick_slots, row_at, 0, keepdims=False)
    own_valid = own_picks >= 0
    pick_rows = jnp.maximum(own_picks, 0)
    chosen = jnp.where(own_valid[:, None], jnp.take(final_bf, pick_rows, axis=0), jnp.zeros((), BF))
    gathered = []
    for chunk in range(2):
        value = chosen[chunk * half_picks : (chunk + 1) * half_picks]
        value = jnp.concatenate([value, swap(value, "zl")], axis=0)
        first, last = (("x", "y"), ("y", "x"))[chunk]
        value = jnp.concatenate(gather4_direct(value, first), axis=0)
        gathered += gather4(value, last)
    gathered = jnp.concatenate(gathered, axis=0)
    rows_yxz = jnp.transpose(rows_xyz, (1, 0, 2)).reshape(-1)
    rows_xyz = rows_xyz.reshape(-1)

    def in_order(table):
        return jnp.concatenate(
            [
                jnp.take(table[:, :half_picks], rows_yxz, axis=0).reshape(-1),
                jnp.take(table[:, half_picks:], rows_xyz, axis=0).reshape(-1),
            ]
        )

    valid_all = in_order(pick_slots) >= 0
    label_rows = local_row(in_order(labels))
    logits = jnp.where(row_used[None, :], product_nt(gathered, table_bf), -1e30)
    hits = label_rows[:, None] == jnp.arange(vocab_rows)[None, :]
    peak = jnp.max(logits, axis=1)
    exp_total = jnp.sum(jnp.exp(logits - peak[:, None]), axis=1)
    target = jnp.sum(jnp.where(hits, logits, 0.0), axis=1)
    stats = jnp.stack([peak, exp_total, target])
    devices = jnp.arange(32)
    at_y = jnp.take(own_shift, (devices // 8 - y_at) % 4)
    at_x = jnp.take(own_shift, (devices % 4 - x_at) % 4)
    at_z = (devices // 4) % 2 ^ zl_at
    back_y = (at_y * 4 + at_x) * 2 + at_z
    back_x = (at_x * 4 + at_y) * 2 + at_z

    def reorder(value, first_order, second_order):
        value = value.reshape(value.shape[0], 2, 32, half_picks)
        return jnp.stack(
            [jnp.take(value[:, 0], first_order, axis=1), jnp.take(value[:, 1], second_order, axis=1)],
            axis=1,
        ).reshape(value.shape[0], -1)

    stats = reorder(stats, back_y, back_x)
    stats = merge_stats(stats, swap(stats, "zl"))
    for axis in ("x", "y"):
        one, two, three = (crossed(stats, axis, mask) for mask in (1, 2, 3))
        stats = merge_stats(merge_stats(stats, one), merge_stats(two, three))
    stats = reorder(stats, rows_yxz, rows_xyz)
    log_total = stats[0] + jnp.log(stats[1])
    losses = jnp.where(valid_all, log_total - stats[2], 0.0).reshape(2, 32, half_picks)
    loss_own = jnp.sum(losses[:, 0])
    count_own = jnp.sum(own_valid.astype(F32))
    grad_logits = jnp.where(
        valid_all[:, None], jnp.exp(logits - log_total[:, None]) - hits.astype(F32), 0.0
    ).astype(BF)
    head_grad = product_tn(grad_logits, gathered)
    grad_gathered = product(grad_logits, table_bf)
    grad_chosen = []
    for chunk in range(2):
        value = grad_gathered[chunk * 32 * half_picks : (chunk + 1) * 32 * half_picks]
        first, last = (("y", "x"), ("x", "y"))[chunk]
        value = reduce4(quarters(value), first, BF)
        value = reduce4_direct(quarters(value), last, F32)
        grad_chosen.append(value[:half_picks] + swap(value[half_picks:], "zl"))
    grad_chosen = jnp.concatenate(grad_chosen, axis=0)
    grad_final = (
        jnp.zeros((span_len, model_width), F32)
        .at[pick_rows]
        .add(jnp.where(own_valid[:, None], grad_chosen, 0.0))
    )
    grad_resid, g_final_gain, g_final_shift = final_back(grad_final)

    own_parts = [None] * LAYERS
    small_parts = [None] * LAYERS
    for layer_idx in reversed(range(LAYERS)):
        grad_resid, (lefts, rights), small_part = layer_backward(
            grad_resid,
            kept_layers[layer_idx],
            layer_weights[layer_idx],
            all_params[layer_idx],
            doc_mask,
        )
        own_parts[layer_idx] = reduce_weights(
            weight_grads(places[layer_idx], lefts, rights), layer_idx, z_hi
        )
        small_parts[layer_idx] = small_part
    own_blocks = unpack_blocks(jnp.where(z_hi == 0, own_parts[0], own_parts[1]), own_odd)

    grad_bf = grad_resid.astype(BF)
    columns = [grad_bf[:, at : at + 256] for at in range(0, model_width, 256)]

    def joined(parts):
        return jnp.concatenate(parts, axis=0)

    pair0 = joined([columns[0], swap(columns[0], "zl")])
    spread0 = joined(gather4(joined(gather4(pair0, "y")), "x"))
    pair1 = joined([columns[1], swap(columns[1], "zl")])
    spread1 = joined(gather4(joined(gather4(pair1, "x")), "y"))
    spread2 = joined(gather4(joined(gather4(columns[2], "y")), "x"))
    spread3 = swap(spread2, "zl")
    steps = jnp.arange(16)
    step_y = jnp.take(own_shift, (steps // 4 - y_at) % 4)
    step_x = jnp.take(own_shift, (steps % 4 - x_at) % 4)
    order = jnp.stack([step_x * 4 + step_y, step_y * 4 + step_x]).astype(jnp.int32)
    grad_table, pos_sum = scatter_rows(
        order, token_rows.reshape(16, 1, 512), head_grad, (spread0, spread1, spread2, spread3)
    )
    left_half, right_half = grad_table[:, :half_width], grad_table[:, half_width:]
    grad_half = jnp.where(core == 0, left_half, right_half) + swap(
        jnp.where(core == 0, right_half, left_half), "c"
    )
    far_grad = z_flip(grad_half[padded : padded + table_rows].astype(BF))
    grad_own = grad_half[:table_rows] + wide(far_grad)

    gain_list = []
    shift_list = []
    for layer_idx in range(LAYERS):
        gain_list += [small_parts[layer_idx][0], small_parts[layer_idx][1]]
        shift_list += [small_parts[layer_idx][2], small_parts[layer_idx][3]]
    scalars = jnp.zeros((model_width,), F32).at[0].set(loss_own).at[1].set(count_own)
    small_grad = jnp.concatenate(
        [jnp.stack(gain_list + [g_final_gain]), jnp.stack(shift_list + [g_final_shift])]
        + [small_parts[layer_idx][4] for layer_idx in range(LAYERS)]
        + [scalars[None]],
        axis=0,
    )
    small_all = sum_everywhere(small_grad)
    small_sum, ce_sum, pick_count = small_all[:-1], small_all[-1, 0], small_all[-1, 1]

    g_table = grad_own / pick_count
    g_pos = pos_sum / pick_count
    g_small = small_sum / pick_count
    g_ce = own_blocks.reshape(weights.shape) / pick_count
    g_blocks = g_ce + ewc_weight * fisher * (weights - anchor)
    first_row = row_at == 0
    first_seq = seq_at == 0
    local_squares = jnp.sum(g_table * g_table) + jnp.sum(g_blocks * g_blocks)
    local_squares = local_squares + jnp.where(first_row, jnp.sum(g_pos * g_pos), 0.0)
    local_squares = local_squares + jnp.where(
        first_row & first_seq, jnp.sum(g_small * g_small), 0.0
    )
    grad_norm = jnp.sqrt(sum_everywhere(jnp.broadcast_to(local_squares, (8, LANES)))[0, 0])
    factor = jnp.minimum(1.0, clip_bound / grad_norm)
    table_new, table_first, table_second = adam_update(
        vocab_table, factor * g_table, vocab_first, vocab_second, table_rate, decay_rate
    )
    pos_new, pos_first, pos_second = adam_update(
        positions, factor * g_pos, positions_first, positions_second, table_rate, 0.0
    )
    small_new, small_first_new, small_second_new = adam_update(
        small_params, factor * g_small, small_first, small_second, small_rate, 0.0
    )
    block_grad = factor * g_blocks

    def products(grad, root_l, root_r):
        return exact_mm(grad, grad.T), exact_mm(grad.T, grad), exact_mm(exact_mm(root_l, grad), root_r)

    left_mm, right_mm, direction = jax.vmap(products)(
        squared_blocks(g_blocks), squared_blocks(root_left), squared_blocks(root_right)
    )
    direction = (factor * direction).reshape(weights.shape)
    mean_square = jnp.mean(direction * direction, axis=1, keepdims=True)
    direction = direction * lax.rsqrt(mean_square + graft_epsilon)
    weights_new = weights - shampoo_rate * (direction + decay_rate * weights)
    square = factor * factor
    left_new = stat_decay * stat_left + (1.0 - stat_decay) * (
        square * left_mm.reshape(weights.shape)
    )
    right_new = stat_decay * stat_right + (1.0 - stat_decay) * (
        square * right_mm.reshape(weights.shape)
    )
    fisher_new = fisher_decay * fisher + (1.0 - fisher_decay) * g_ce * g_ce
    return (
        ce_sum,
        pick_count,
        grad_norm,
        table_new,
        table_first,
        table_second,
        pos_new,
        pos_first,
        pos_second,
        small_new,
        small_first_new,
        small_second_new,
        weights_new,
        left_new,
        right_new,
        block_grad,
        fisher_new,
    )


def solution(mesh):
    split = P(("seq", "dp"), None)
    table = P("dp", "seq")
    in_specs = (
        (P(None, "seq"), P("dp", None), P(None, "seq"), P(None, "seq"))
        + (table,) * 3
        + (P("seq", None),) * 3
        + (P(),) * 3
        + (split,) * 7
        + (P(),)
    )
    out_specs = (
        (P(),) * 3 + (table,) * 3 + (P("seq", None),) * 3 + (P(),) * 3 + (split,) * 5
    )
    return jax.shard_map(shards, mesh=mesh, in_specs=in_specs, out_specs=out_specs, check_vma=False)
```

time: 2880 us -> 1340 us (0.47)
  waiting for transfers between devices: 1200 us -> 296 us
  local copies, waits for them, and re-layouts: 782 us -> 123 us
  starting transfers between devices: 1.5 us -> 399 us
  blocking collectives: 327 us -> 0 us
  Pallas kernels: 0 us -> 179 us
  other arithmetic: 331 us -> 157 us
  matrix products: 195 us -> 162 us
    reduce_scatter x5 -> x0, waiting for transfers between devices: 523 us -> none  [the longest x1 210 us: shards(): lax.psum_scatter(product(grad_logits, table_bf), 'dp', scatter_dimension=...]
    all_gather x6 -> x0, waiting for transfers between devices: 432 us -> none  [the longest x1 270 us: shards(): lax.all_gather(weights.astype(jnp.bfloat16), ('seq', 'dp'), axis=0, tiled...]
    ppermute x0 -> x234, starting transfers between devices: none -> 399 us  [permuted(): return lax.ppermute(value, ('seq', 'dp'), pairs)]
    ppermute x0 -> x234, waiting for transfers between devices: none -> 296 us  [permuted(): return lax.ppermute(value, ('seq', 'dp'), pairs)]
    reshape x31 -> x4, local copies, waits for them, and re-layouts: 278 us -> 8.68 us  [the longest x2 7.02 us: layer_backward(): grad_values = jnp.einsum('hqk,qhd->khd', soft_probs.astype(BF), grad_head...]
    unnamed x13 -> x0, waiting for transfers between devices: 244 us -> none
    all_gather x3 -> x0, blocking collectives: 196 us -> none  [joined(): pieces = jax.tree.map(lambda part: lax.all_gather(part, axis), value)]
    pallas_call x0 -> x6, Pallas kernels: none -> 179 us  [the longest x2 62.5 us: weight_grads(): pl.pallas_call(weight_grad_kernel, grid_spec=pltpu.PrefetchScalarGridSpec...]
  transfers between devices with their start and end apart: 12 -> 234, of which waited for: 8 -> 86; matrix products, arithmetic and copies ran while one was open for 30% -> 12% of each run, Pallas kernels for 0% -> 14%
where the time goes in v1:
time: 1340 us; the launch traced here: 1330 us
  starting transfers between devices  399 us (30%)
  waiting for transfers between devices  296 us (22%)
  Pallas kernels  179 us (13%)
  matrix products  162 us (12%)
  other arithmetic  157 us (12%)
  local copies, waits for them, and re-layouts  123 us (9%)
    ppermute x234, starting transfers between devices, permuted(): return lax.ppermute(value, ('seq', 'dp'), pairs)  399 us
    ppermute x234, waiting for transfers between devices, permuted(): return lax.ppermute(value, ('seq', 'dp'), pairs)  296 us
    pallas_call x2, Pallas kernels, weight_grads(): pl.pallas_call(weight_grad_kernel, grid_spec=pltpu.PrefetchScalarGridSpec...  62.5 us
    pallas_call x2, Pallas kernels, assemble_layer(): pl.pallas_call(assemble_kernel, grid_spec=pltpu.PrefetchScalarGridSpec(nu...  58.6 us
    unnamed x542, local copies, waits for them, and re-layouts  37 us
    pallas_call x1, Pallas kernels, scatter_rows(): pl.pallas_call(scatter_kernel, grid_spec=pltpu.PrefetchScalarGridSpec(num...  30.8 us
    dot_general x9, matrix products, product_nt(): lax.dot_general(left, right, (((1,), (1,)), ((), ())), preferred_element_...  30.1 us
    pallas_call x1, Pallas kernels, lookup(): pl.pallas_call(lookup_kernel, grid=(steps,), in_specs=[pl.BlockSpec((512,...  27.6 us
  transfers between devices with their start and end apart: 234, of which 86 were waited for; matrix products, arithmetic and copies ran while one was open for 12% of the time, Pallas kernels for 14%

profile of v1, /device:TPU:1, one launch (start us, length us, event | category | flops | bytes accessed | tf_op | source)
XLA Modules:
  0.0 1328.4 jit_solution(11332654682618084809)
XLA Ops:
  10.4 6.3 collective-permute-start.25
  49.6 8.2 collective-permute-done.33
  98.9 27.6 %lookup.1 = (bf16[8192,256]{1,0:T(8,128)(2,1)S(1)}, bf16[8192,256]{1,0:T(8,128)(2,1)}, bf16[4096,256]{1,0:T(8,128)(2,1)S(1)}, bf16[4096,256]{1,0:T(8,128)(2,1)S(1)}) custom-call(s32[8192,128]{1,0:T(8,128)} %broadcast_in_dim.323.ids, bf16[1664,768]{1,0:T(8,128)(2,1)S(1)} %maximum_select_fusion.table), custom_call_target="tpu_custom_call" | custom-call | flops 20937965568 | bytes 20000000 | tf_op jit(solution)/shard_map/lookup/pallas_call | solution.py:290
  136.4 7.1 collective-permute-start.51
  147.6 7.8 collective-permute-start.47
  184.7 12.1 collective-permute-done.6
  202.6 8.8 collective-permute-start.50
  211.7 27.5 %collective-permute-done.18 = bf16[4096,256]{1,0:T(8,128)(2,1)S(1)} collective-permute-done((bf16[4096,256]{1,0:T(8,128)(2,1)S(1)}, bf16[4096,256]{1,0:T(8,128)(2,1)S(1)}, u32[]{:S(2)}, u32[]{:S(2)}) %collective-permute-start.18) | collective-permute-done | bytes 2097184 | tf_op jit(solution)/shard_map/ppermute | solution.py:73
  260.0 33.5 %assemble.2 = (bf16[768,2304]{1,0:T(8,128)(2,1)}, bf16[768,768]{1,0:T(8,128)(2,1)S(1)}, bf16[768,3072]{1,0:T(8,128)(2,1)}, bf16[3072,768]{1,0:T(8,128)(2,1)}) custom-call(s32[192]{0:T(256)S(1)} %get-tuple-element.361.places, bf16[8,288,128]{2,1,0:T(8,128)(2,1)S(1)} %constant_dynamic-update-slice_fusion.refs_0_, ...), custom_call_target="tpu_custom_call" | custom-call | bytes 29000000 | tf_op jit(solution)/shard_map/assemble/pallas_call | solution.py:198
  304.3 6.4 collective-permute-done.22
  335.0 9.9 collective-permute-start.84
  350.2 8.7 collective-permute-start.88
  363.9 9.1 collective-permute-start.92
  391.9 25.1 %assemble.3 = (bf16[768,2304]{1,0:T(8,128)(2,1)}, bf16[768,768]{1,0:T(8,128)(2,1)S(1)}, bf16[768,3072]{1,0:T(8,128)(2,1)}, bf16[3072,768]{1,0:T(8,128)(2,1)}) custom-call(s32[192]{0:T(256)S(1)} %get-tuple-element.360.places, bf16[8,288,128]{2,1,0:T(8,128)(2,1)S(1)} %copy-done.15, bf16[8,288,128]{2,1,0:T(8,128)(2,1)} %collective-permute-done.66.refs_1_, ...), custom_call_target="tpu_custom_call" | custom-call | bytes 29000000 | tf_op jit(solution)/shard_map/assemble/pallas_call | solution.py:198
  426.8 10.4 fusion.289
  437.3 7.2 fusion.58
  445.7 7.1 multiply_convert_fusion.3
  459.3 9.2 collective-permute-done.94
  471.5 8.8 collective-permute-done.95
  497.5 10.4 fusion.292
  507.9 7.2 fusion.61
  516.2 6.7 multiply_convert_fusion.2
  541.3 6.9 collective-permute-done.101
  566.0 8.0 collective-permute-done.108
  585.5 10.8 select_reduce_fusion.1
  596.4 8.1 exponential_reduce_fusion
  617.3 6.7 collective-permute-start.116
  632.0 8.2 select_convert_fusion
  640.2 6.4 fusion.295
  690.1 7.0 convert_reduce_fusion
  701.9 10.8 multiply_reduce_fusion.1
  712.7 8.0 fusion.26
  739.0 18.8 %collective-permute-start.133 = (f32[256,1536]{1,0:T(8,128)S(1)}, f32[256,1536]{1,0:T(8,128)S(1)}, u32[]{:S(2)}, u32[]{:S(2)}) collective-permute-start(f32[256,1536]{1,0:T(8,128)S(1)} %pad_maximum_fusion.3), channel_id=1, source_target_pairs={{0,32},{1,33},{2,34},{3,35},{4,36},{5,37},{6,38},{7,39},{8,40},{9,... | collective-permute-start | bytes 4718600 | tf_op jit(solution)/shard_map/ppermute | solution.py:73
  765.3 8.7 collective-permute-done.134
  802.3 10.6 multiply_reduce_fusion
  813.0 7.9 fusion.30
  846.0 31.1 %weight_grads.3 = (bf16[32,288,128]{2,1,0:T(8,128)(2,1)S(1)}, bf16[32,288,128]{2,1,0:T(8,128)(2,1)S(1)}, bf16[32,288,128]{2,1,0:T(8,128)(2,1)S(1)}, bf16[32,288,...) custom-call(s32[192]{0:T(256)S(1)} %get-tuple-element.360.places, ...), custom_call_target="tpu_custom_call" | custom-call | flops 3623878656 | bytes 21000000 | tf_op jit(solution)/shard_map/weight_grads/pallas_call | solution.py:255
  878.6 7.5 fusion.296.start
  888.9 6.2 fusion.67
  936.9 31.3 %weight_grads.2 = (bf16[32,288,128]{2,1,0:T(8,128)(2,1)S(1)}, bf16[32,288,128]{2,1,0:T(8,128)(2,1)S(1)}, bf16[32,288,128]{2,1,0:T(8,128)(2,1)S(1)}, bf16[32,288,...) custom-call(s32[192]{0:T(256)S(1)} %copy-done.47, ...), custom_call_target="tpu_custom_call" | custom-call | flops 3623878656 | bytes 21000000 | tf_op jit(solution)/shard_map/weight_grads/pallas_call | solution.py:255
  1053.2 13.1 collective-permute-start.182
  1069.6 6.8 collective-permute-start.190
  1082.5 13.1 collective-permute-done.161
  1102.7 8.8 collective-permute-done.162
  1120.8 8.9 collective-permute-done.175
  1137.3 30.8 %scatter_rows.1 = (f32[1664,768]{1,0:T(8,128)}, f32[256,768]{1,0:T(8,128)S(1)}) custom-call(s32[2,16]{1,0:T(2,128)S(1)} %pad_add_fusion.1.order, s32[16,1,512]{2,1,0:T(1,128)S(1)} %and_select_fusion.2.ids, f32[1664,768]{1,0:T(8,128)} %fusion.296.start, bf16[8192,256]{1,0:T(8,128)(2,1)} %copy-done.193, bf16[8192,256]{1,0:T(8,128)(2,1)} %copy-done.195, ...), custom_call_target="tpu_custom_call" | custom-call | flops 20937965568 | bytes 25000000 | tf_op jit(solution)/shard_map/scatter_rows/pallas_call | solution.py:336
  1170.9 23.5 %collective-permute-start.171 = (f32[1664,384]{1,0:T(8,128)S(1)}, f32[1664,384]{1,0:T(8,128)S(1)}, u32[]{:S(2)}, u32[]{:S(2)}) collective-permute-start(f32[1664,384]{1,0:T(8,128)S(1)} %slice_select_fusion), channel_id=1, source_target_pairs={{0,32},{1,33},{2,34},{3,35},{4,36},{5,37},{6,38},{7,39},{8,40},{9,... | collective-permute-start | bytes 7667720 | tf_op jit(solution)/shard_map/ppermute | solution.py:73
  1267.8 10.6 collective-permute-start.224
  (1413 shorter events, 733.8 us)
Async XLA Ops:
  10.4 29.6 %collective-permute-start.25 = (bf16[3,288,128]{2,1,0:T(8,128)(2,1)S(1)}, bf16[3,288,128]{2,1,0:T(8,128)(2,1)S(1)}, u32[]{:S(2)}, u32[]{:S(2)}) collective-permute-start(bf16[3,288,128]{2,1,0:T(8,128)(2,1)S(1)} %maximum_maximum_fusion.1), channel_id=1, source_target_pairs={{0,64},{1,65},{2,66},{3,67},{4,68},{5,69},{6,70},{7,71},{8,72},{9,... | collective-permute-start | bytes 663560 | tf_op jit(solution)/shard_map/ppermute | solution.py:73
  18.3 27.1 %collective-permute-start = (bf16[832,384]{1,0:T(8,128)(2,1)S(1)}, bf16[832,384]{1,0:T(8,128)(2,1)}, u32[]{:S(2)}, u32[]{:S(2)}) collective-permute-start(bf16[832,384]{1,0:T(8,128)(2,1)S(1)} %get-tuple-element.256), channel_id=1, source_target_pairs={{0,4},{1,5},{2,6},{3,7},{4,64},{5,65},{6,66},{7,67},{8,12},{9,13},... | collective-permute-start | bytes 1916936 | tf_op jit(solution)/shard_map/ppermute | solution.py:73
  89.5 40.0 %collective-permute-start.79 = (bf16[4,288,128]{2,1,0:T(8,128)(2,1)S(1)}, bf16[4,288,128]{2,1,0:T(8,128)(2,1)S(1)}, u32[]{:S(2)}, u32[]{:S(2)}) collective-permute-start(bf16[4,288,128]{2,1,0:T(8,128)(2,1)S(1)} %pad_maximum_fusion.13), channel_id=1, source_target_pairs={{0,24},{1,25},{2,26},{3,27},{4,28},{5,29},{6,30},{7,31},{8,0},{9,1... | collective-permute-start | bytes 884744 | tf_op jit(solution)/shard_map/ppermute | solution.py:73
  89.6 41.4 %collective-permute-start.43 = (bf16[4,288,128]{2,1,0:T(8,128)(2,1)S(1)}, bf16[4,288,128]{2,1,0:T(8,128)(2,1)S(1)}, u32[]{:S(2)}, u32[]{:S(2)}) collective-permute-start(bf16[4,288,128]{2,1,0:T(8,128)(2,1)S(1)} %pad_maximum_fusion.12), channel_id=1, source_target_pairs={{0,24},{1,25},{2,26},{3,27},{4,28},{5,29},{6,30},{7,31},{8,0},{9,1... | collective-permute-start | bytes 884744 | tf_op jit(solution)/shard_map/ppermute | solution.py:73
  90.7 35.9 %collective-permute-start.71 = (bf16[2,288,128]{2,1,0:T(8,128)(2,1)S(1)}, bf16[2,288,128]{2,1,0:T(8,128)(2,1)S(1)}, u32[]{:S(2)}, u32[]{:S(2)}) collective-permute-start(bf16[2,288,128]{2,1,0:T(8,128)(2,1)S(1)} %collective-permute-done.70), channel_id=1, source_target_pairs={{0,24},{1,25},{2,26},{3,27},{4,28},{5,29},{6,30},{7,31},{8,0},{9,1... | collective-permute-start | bytes 442376 | tf_op jit(solution)/shard_map/ppermute | solution.py:73
  90.7 36.1 %collective-permute-start.28 = (bf16[2,288,128]{2,1,0:T(8,128)(2,1)S(1)}, bf16[2,288,128]{2,1,0:T(8,128)(2,1)S(1)}, u32[]{:S(2)}, u32[]{:S(2)}) collective-permute-start(bf16[2,288,128]{2,1,0:T(8,128)(2,1)S(1)} %collective-permute-done.27), channel_id=1, source_target_pairs={{0,3},{1,0},{2,1},{3,2},{4,7},{5,4},{6,5},{7,6},{8,11},{9,8},{10,9... | collective-permute-start | bytes 442376 | tf_op jit(solution)/shard_map/ppermute | solution.py:73
  94.0 49.6 %collective-permute-start.37 = (bf16[8,288,128]{2,1,0:T(8,128)(2,1)S(1)}, bf16[8,288,128]{2,1,0:T(8,128)(2,1)S(1)}, u32[]{:S(2)}, u32[]{:S(2)}) collective-permute-start(bf16[8,288,128]{2,1,0:T(8,128)(2,1)S(1)} %constant_dynamic-update-slice_fusion.5.refs_4_), channel_id=1, source_target_pairs={{0,3},{1,0},{2,1},{3,2},{4,7},{5,4},{6,5},{7,6},{8,11},{9,8},{10,9... | collective-permute-start | bytes 1769480 | tf_op jit(solution)/shard_map/ppermute | solution.py:73
  126.8 33.6 %collective-permute-start.4 = (bf16[2048,256]{1,0:T(8,128)(2,1)S(1)}, bf16[2048,256]{1,0:T(8,128)(2,1)S(1)}, u32[]{:S(2)}, u32[]{:S(2)}) collective-permute-start(bf16[2048,256]{1,0:T(8,128)(2,1)S(1)} %split.126), channel_id=1, source_target_pairs={{0,1},{1,2},{2,3},{3,0},{4,5},{5,6},{6,7},{7,4},{8,9},{9,10},{10,1... | collective-permute-start | bytes 3145736 | tf_op jit(solution)/shard_map/ppermute | solution.py:73
  169.4 29.4 %collective-permute-start.46 = (bf16[16,288,128]{2,1,0:T(8,128)(2,1)S(1)}, bf16[16,288,128]{2,1,0:T(8,128)(2,1)S(1)}, u32[]{:S(2)}, u32[]{:S(2)}) collective-permute-start(bf16[16,288,128]{2,1,0:T(8,128)(2,1)S(1)} %constant_dynamic-update-slice_fusion.10.refs_8_), channel_id=1, source_target_pairs={{0,4},{1,5},{2,6},{3,7},{4,0},{5,1},{6,2},{7,3},{8,12},{9,13},{10,... | collective-permute-start | bytes 3538952 | tf_op jit(solution)/shard_map/ppermute | solution.py:73
  171.3 67.9 %collective-permute-start.18 = (bf16[4096,256]{1,0:T(8,128)(2,1)S(1)}, bf16[4096,256]{1,0:T(8,128)(2,1)S(1)}, u32[]{:S(2)}, u32[]{:S(2)}) collective-permute-start(bf16[4096,256]{1,0:T(8,128)(2,1)S(1)} %get-tuple-element.75), channel_id=1, source_target_pairs={{0,4},{1,5},{2,6},{3,7},{4,0},{5,1},{6,2},{7,3},{8,12},{9,13},{10,... | collective-permute-start | bytes 6291464 | tf_op jit(solution)/shard_map/ppermute | solution.py:73
  184.4 26.9 %collective-permute-start.13 = (bf16[2048,256]{1,0:T(8,128)(2,1)S(1)}, bf16[2048,256]{1,0:T(8,128)(2,1)S(1)}, u32[]{:S(2)}, u32[]{:S(2)}) collective-permute-start(bf16[2048,256]{1,0:T(8,128)(2,1)S(1)} %get-tuple-element.229), channel_id=1, source_target_pairs={{0,24},{1,25},{2,26},{3,27},{4,28},{5,29},{6,30},{7,31},{8,0},{9,1... | collective-permute-start | bytes 3145736 | tf_op jit(solution)/shard_map/ppermute | solution.py:73
  198.8 53.5 %collective-permute-start.55 = (bf16[16,288,128]{2,1,0:T(8,128)(2,1)S(1)}, bf16[16,288,128]{2,1,0:T(8,128)(2,1)S(1)}, u32[]{:S(2)}, u32[]{:S(2)}) collective-permute-start(bf16[16,288,128]{2,1,0:T(8,128)(2,1)S(1)} %constant_dynamic-update-slice_fusion.10.refs_8_), channel_id=1, source_target_pairs={{0,32},{1,33},{2,34},{3,35},{4,36},{5,37},{6,38},{7,39},{8,40},{9,... | collective-permute-start | bytes 3538952 | tf_op jit(solution)/shard_map/ppermute | solution.py:73
  202.6 37.7 %collective-permute-start.50 = (bf16[8,288,128]{2,1,0:T(8,128)(2,1)S(1)}, bf16[8,288,128]{2,1,0:T(8,128)(2,1)S(1)}, u32[]{:S(2)}, u32[]{:S(2)}) collective-permute-start(bf16[8,288,128]{2,1,0:T(8,128)(2,1)S(1)} %collective-permute-done.32.refs_3_), channel_id=1, source_target_pairs={{0,32},{1,33},{2,34},{3,35},{4,36},{5,37},{6,38},{7,39},{8,40},{9,... | collective-permute-start | bytes 1769480 | tf_op jit(solution)/shard_map/ppermute | solution.py:73
  211.3 45.4 %collective-permute-start.56 = (bf16[16,288,128]{2,1,0:T(8,128)(2,1)S(1)}, bf16[16,288,128]{2,1,0:T(8,128)(2,1)S(1)}, u32[]{:S(2)}, u32[]{:S(2)}) collective-permute-start(bf16[16,288,128]{2,1,0:T(8,128)(2,1)S(1)} %collective-permute-done.46.refs_9_), channel_id=1, source_target_pairs={{0,32},{1,33},{2,34},{3,35},{4,36},{5,37},{6,38},{7,39},{8,40},{9,... | collective-permute-start | bytes 3538952 | tf_op jit(solution)/shard_map/ppermute | solution.py:73
  211.6 33.9 %collective-permute-start.7 = (bf16[512,256]{1,0:T(8,128)(2,1)S(1)}, bf16[512,256]{1,0:T(8,128)(2,1)S(1)}, u32[]{:S(2)}, u32[]{:S(2)}) collective-permute-start(bf16[512,256]{1,0:T(8,128)(2,1)S(1)} %split.166), channel_id=1, source_target_pairs={{0,8},{1,9},{2,10},{3,11},{4,12},{5,13},{6,14},{7,15},{8,16},{9,17... | collective-permute-start | bytes 786440 | tf_op jit(solution)/shard_map/ppermute | solution.py:73
  254.3 39.1 %collective-permute-start.9 = (bf16[512,256]{1,0:T(8,128)(2,1)}, bf16[512,256]{1,0:T(8,128)(2,1)}, u32[]{:S(2)}, u32[]{:S(2)}) collective-permute-start(bf16[512,256]{1,0:T(8,128)(2,1)} %get-tuple-element.246), channel_id=1, source_target_pairs={{0,24},{1,25},{2,26},{3,27},{4,28},{5,29},{6,30},{7,31},{8,0},{9,1... | collective-permute-start | bytes 786440 | tf_op jit(solution)/shard_map/ppermute | solution.py:73
  255.2 40.9 %collective-permute-start.15 = (bf16[512,256]{1,0:T(8,128)(2,1)}, bf16[512,256]{1,0:T(8,128)(2,1)}, u32[]{:S(2)}, u32[]{:S(2)}) collective-permute-start(bf16[512,256]{1,0:T(8,128)(2,1)} %get-tuple-element.247), channel_id=1, source_target_pairs={{0,1},{1,2},{2,3},{3,0},{4,5},{5,6},{6,7},{7,4},{8,9},{9,10},{10,1... | collective-permute-start | bytes 786440 | tf_op jit(solution)/shard_map/ppermute | solution.py:73
  256.6 39.6 %collective-permute-start.16 = (bf16[512,256]{1,0:T(8,128)(2,1)}, bf16[512,256]{1,0:T(8,128)(2,1)}, u32[]{:S(2)}, u32[]{:S(2)}) collective-permute-start(bf16[512,256]{1,0:T(8,128)(2,1)} %get-tuple-element.248), channel_id=1, source_target_pairs={{0,3},{1,0},{2,1},{3,2},{4,7},{5,4},{6,5},{7,6},{8,11},{9,8},{10,9... | collective-permute-start | bytes 786440 | tf_op jit(solution)/shard_map/ppermute | solution.py:73
  256.8 43.2 %collective-permute-start.20 = (bf16[1024,256]{1,0:T(8,128)(2,1)S(1)}, bf16[1024,256]{1,0:T(8,128)(2,1)S(1)}, u32[]{:S(2)}, u32[]{:S(2)}) collective-permute-start(bf16[1024,256]{1,0:T(8,128)(2,1)S(1)} %get-tuple-element.238), channel_id=1, source_target_pairs={{0,1},{1,2},{2,3},{3,0},{4,5},{5,6},{6,7},{7,4},{8,9},{9,10},{10,1... | collective-permute-start | bytes 1572872 | tf_op jit(solution)/shard_map/ppermute | solution.py:73
  259.3 42.3 %collective-permute-start.21 = (bf16[1024,256]{1,0:T(8,128)(2,1)S(1)}, bf16[1024,256]{1,0:T(8,128)(2,1)S(1)}, u32[]{:S(2)}, u32[]{:S(2)}) collective-permute-start(bf16[1024,256]{1,0:T(8,128)(2,1)S(1)} %get-tuple-element.239), channel_id=1, source_target_pairs={{0,3},{1,0},{2,1},{3,2},{4,7},{5,4},{6,5},{7,6},{8,11},{9,8},{10,9... | collective-permute-start | bytes 1572872 | tf_op jit(solution)/shard_map/ppermute | solution.py:73
  293.5 29.6 %collective-permute-start.81 = (bf16[4,288,128]{2,1,0:T(8,128)(2,1)S(1)}, bf16[4,288,128]{2,1,0:T(8,128)(2,1)S(1)}, u32[]{:S(2)}, u32[]{:S(2)}) collective-permute-start(bf16[4,288,128]{2,1,0:T(8,128)(2,1)S(1)} %copy-done.128), channel_id=1, source_target_pairs={{0,8},{1,9},{2,10},{3,11},{4,12},{5,13},{6,14},{7,15},{8,16},{9,17... | collective-permute-start | bytes 884744 | tf_op jit(solution)/shard_map/ppermute | solution.py:73
  296.1 31.0 %collective-permute-start.66 = (bf16[8,288,128]{2,1,0:T(8,128)(2,1)S(1)}, bf16[8,288,128]{2,1,0:T(8,128)(2,1)}, u32[]{:S(2)}, u32[]{:S(2)}) collective-permute-start(bf16[8,288,128]{2,1,0:T(8,128)(2,1)S(1)} %constant_dynamic-update-slice_fusion.17.refs_0_), channel_id=1, source_target_pairs={{0,24},{1,25},{2,26},{3,27},{4,28},{5,29},{6,30},{7,31},{8,0},{9,1... | collective-permute-start | bytes 1769480 | tf_op jit(solution)/shard_map/ppermute | solution.py:73
  296.2 32.6 %collective-permute-start.68 = (bf16[8,288,128]{2,1,0:T(8,128)(2,1)S(1)}, bf16[8,288,128]{2,1,0:T(8,128)(2,1)}, u32[]{:S(2)}, u32[]{:S(2)}) collective-permute-start(bf16[8,288,128]{2,1,0:T(8,128)(2,1)S(1)} %constant_dynamic-update-slice_fusion.17.refs_0_), channel_id=1, source_target_pairs={{0,8},{1,9},{2,10},{3,11},{4,12},{5,13},{6,14},{7,15},{8,16},{9,17... | collective-permute-start | bytes 1769480 | tf_op jit(solution)/shard_map/ppermute | solution.py:73
  334.1 29.8 %collective-permute-start.82 = (bf16[16,288,128]{2,1,0:T(8,128)(2,1)S(1)}, bf16[16,288,128]{2,1,0:T(8,128)(2,1)}, u32[]{:S(2)}, u32[]{:S(2)}) collective-permute-start(bf16[16,288,128]{2,1,0:T(8,128)(2,1)S(1)} %constant_dynamic-update-slice_fusion.27.refs_8_), channel_id=1, source_target_pairs={{0,4},{1,5},{2,6},{3,7},{4,0},{5,1},{6,2},{7,3},{8,12},{9,13},{10,... | collective-permute-start | bytes 3538952 | tf_op jit(solution)/shard_map/ppermute | solution.py:73
  346.2 31.3 %collective-permute-start.91 = (bf16[16,288,128]{2,1,0:T(8,128)(2,1)S(1)}, bf16[16,288,128]{2,1,0:T(8,128)(2,1)}, u32[]{:S(2)}, u32[]{:S(2)}) collective-permute-start(bf16[16,288,128]{2,1,0:T(8,128)(2,1)S(1)} %constant_dynamic-update-slice_fusion.27.refs_8_), channel_id=1, source_target_pairs={{0,32},{1,33},{2,34},{3,35},{4,36},{5,37},{6,38},{7,39},{8,40},{9,... | collective-permute-start | bytes 3538952 | tf_op jit(solution)/shard_map/ppermute | solution.py:73
  348.6 27.8 %collective-permute-start.59 = (bf16[256,1536]{1,0:T(8,128)(2,1)}, bf16[256,1536]{1,0:T(8,128)(2,1)}, u32[]{:S(2)}, u32[]{:S(2)}) collective-permute-start(bf16[256,1536]{1,0:T(8,128)(2,1)} %collective-permute-done.58), channel_id=1, source_target_pairs={{0,4},{1,5},{2,6},{3,7},{4,64},{5,65},{6,66},{7,67},{8,12},{9,13},... | collective-permute-start | bytes 2359304 | tf_op jit(solution)/shard_map/ppermute | solution.py:73
  374.8 42.4 %collective-permute-start.57 = (bf16[256,1536]{1,0:T(8,128)(2,1)}, bf16[256,1536]{1,0:T(8,128)(2,1)}, u32[]{:S(2)}, u32[]{:S(2)}) collective-permute-start(bf16[256,1536]{1,0:T(8,128)(2,1)} %copy-done.86), channel_id=1, source_target_pairs={{0,32},{1,33},{2,34},{3,35},{4,36},{5,37},{6,38},{7,39},{8,40},{9,... | collective-permute-start | bytes 2359304 | tf_op jit(solution)/shard_map/ppermute | solution.py:73
  376.3 40.9 %collective-permute-start.60 = (bf16[256,1536]{1,0:T(8,128)(2,1)}, bf16[256,1536]{1,0:T(8,128)(2,1)}, u32[]{:S(2)}, u32[]{:S(2)}) collective-permute-start(bf16[256,1536]{1,0:T(8,128)(2,1)} %collective-permute-done.59), channel_id=1, source_target_pairs={{0,32},{1,33},{2,34},{3,35},{4,36},{5,37},{6,38},{7,39},{8,40},{9,... | collective-permute-start | bytes 2359304 | tf_op jit(solution)/shard_map/ppermute | solution.py:73
  841.5 53.7 %collective-permute-start.137 = (f32[256,1536]{1,0:T(8,128)}, f32[256,1536]{1,0:T(8,128)}, u32[]{:S(2)}, u32[]{:S(2)}) collective-permute-start(f32[256,1536]{1,0:T(8,128)} %pad_maximum_fusion.2), channel_id=1, source_target_pairs={{0,32},{1,33},{2,34},{3,35},{4,36},{5,37},{6,38},{7,39},{8,40},{9,... | collective-permute-start | bytes 4718600 | tf_op jit(solution)/shard_map/ppermute | solution.py:73
  878.1 26.3 %collective-permute-start.207 = (bf16[32,288,128]{2,1,0:T(8,128)(2,1)}, bf16[32,288,128]{2,1,0:T(8,128)(2,1)}, u32[]{:S(2)}, u32[]{:S(2)}) collective-permute-start(bf16[32,288,128]{2,1,0:T(8,128)(2,1)} %get-tuple-element.94), channel_id=1, source_target_pairs={{0,32},{1,33},{2,34},{3,35},{4,36},{5,37},{6,38},{7,39},{8,40},{9,... | collective-permute-start | bytes 7077896 | tf_op jit(solution)/shard_map/ppermute | solution.py:73
  878.2 32.9 %collective-permute-start.215 = (bf16[32,288,128]{2,1,0:T(8,128)(2,1)}, bf16[32,288,128]{2,1,0:T(8,128)(2,1)}, u32[]{:S(2)}, u32[]{:S(2)}) collective-permute-start(bf16[32,288,128]{2,1,0:T(8,128)(2,1)} %get-tuple-element.96), channel_id=1, source_target_pairs={{0,32},{1,33},{2,34},{3,35},{4,36},{5,37},{6,38},{7,39},{8,40},{9,... | collective-permute-start | bytes 7077896 | tf_op jit(solution)/shard_map/ppermute | solution.py:73
  916.8 82.9 %collective-permute-start.201 = (bf16[8,288,128]{2,1,0:T(8,128)(2,1)}, bf16[8,288,128]{2,1,0:T(8,128)(2,1)}, u32[]{:S(2)}, u32[]{:S(2)}) collective-permute-start(bf16[8,288,128]{2,1,0:T(8,128)(2,1)} %get-tuple-element.222), channel_id=1, source_target_pairs={{0,8},{1,9},{2,10},{3,11},{4,12},{5,13},{6,14},{7,15},{8,16},{9,17... | collective-permute-start | bytes 1769480 | tf_op jit(solution)/shard_map/ppermute | solution.py:73
  918.6 83.3 %collective-permute-start.202 = (bf16[8,288,128]{2,1,0:T(8,128)(2,1)}, bf16[8,288,128]{2,1,0:T(8,128)(2,1)}, u32[]{:S(2)}, u32[]{:S(2)}) collective-permute-start(bf16[8,288,128]{2,1,0:T(8,128)(2,1)} %get-tuple-element.223), channel_id=1, source_target_pairs={{0,24},{1,25},{2,26},{3,27},{4,28},{5,29},{6,30},{7,31},{8,0},{9,1... | collective-permute-start | bytes 1769480 | tf_op jit(solution)/shard_map/ppermute | solution.py:73
  927.5 40.7 %collective-permute-start.140 = (f32[27,768]{1,0:T(8,128)S(1)}, f32[27,768]{1,0:T(8,128)S(1)}, u32[]{:S(2)}, u32[]{:S(2)}) collective-permute-start(f32[27,768]{1,0:T(8,128)S(1)} %concatenate.246), channel_id=1, source_target_pairs={{0,32},{1,33},{2,34},{3,35},{4,36},{5,37},{6,38},{7,39},{8,40},{9,... | collective-permute-start | bytes 248840 | tf_op jit(solution)/shard_map/ppermute | solution.py:73
  934.0 34.4 %collective-permute-start.157 = (bf16[256,256]{1,0:T(8,128)(2,1)S(1)}, bf16[256,256]{1,0:T(8,128)(2,1)S(1)}, u32[]{:S(2)}, u32[]{:S(2)}) collective-permute-start(bf16[256,256]{1,0:T(8,128)(2,1)S(1)} %get-tuple-element.277), channel_id=1, source_target_pairs={{0,4},{1,5},{2,6},{3,7},{4,0},{5,1},{6,2},{7,3},{8,12},{9,13},{10,... | collective-permute-start | bytes 393224 | tf_op jit(solution)/shard_map/ppermute | solution.py:73
  934.0 37.5 %collective-permute-start.150 = (bf16[256,256]{1,0:T(8,128)(2,1)S(1)}, bf16[256,256]{1,0:T(8,128)(2,1)S(1)}, u32[]{:S(2)}, u32[]{:S(2)}) collective-permute-start(bf16[256,256]{1,0:T(8,128)(2,1)S(1)} %get-tuple-element.278), channel_id=1, source_target_pairs={{0,4},{1,5},{2,6},{3,7},{4,0},{5,1},{6,2},{7,3},{8,12},{9,13},{10,... | collective-permute-start | bytes 393224 | tf_op jit(solution)/shard_map/ppermute | solution.py:73
  999.7 97.6 %collective-permute-start.174 = (bf16[32,288,128]{2,1,0:T(8,128)(2,1)S(1)}, bf16[32,288,128]{2,1,0:T(8,128)(2,1)S(1)}, u32[]{:S(2)}, u32[]{:S(2)}) collective-permute-start(bf16[32,288,128]{2,1,0:T(8,128)(2,1)S(1)} %copy-done.222), channel_id=1, source_target_pairs={{0,32},{1,33},{2,34},{3,35},{4,36},{5,37},{6,38},{7,39},{8,40},{9,... | collective-permute-start | bytes 7077896 | tf_op jit(solution)/shard_map/ppermute | solution.py:73
  1042.4 27.2 %collective-permute-start.169 = (bf16[1024,256]{1,0:T(8,128)(2,1)S(1)}, bf16[1024,256]{1,0:T(8,128)(2,1)S(1)}, u32[]{:S(2)}, u32[]{:S(2)}) collective-permute-start(bf16[1024,256]{1,0:T(8,128)(2,1)S(1)} %pad_maximum_fusion.9), channel_id=1, source_target_pairs={{0,1},{1,2},{2,3},{3,0},{4,5},{5,6},{6,7},{7,4},{8,9},{9,10},{10,1... | collective-permute-start | bytes 1572872 | tf_op jit(solution)/shard_map/ppermute | solution.py:73
  1053.2 45.2 %collective-permute-start.182 = (bf16[32,288,128]{2,1,0:T(8,128)(2,1)S(1)}, bf16[32,288,128]{2,1,0:T(8,128)(2,1)S(1)}, u32[]{:S(2)}, u32[]{:S(2)}) collective-permute-start(bf16[32,288,128]{2,1,0:T(8,128)(2,1)S(1)} %copy-done.221), channel_id=1, source_target_pairs={{0,32},{1,33},{2,34},{3,35},{4,36},{5,37},{6,38},{7,39},{8,40},{9,... | collective-permute-start | bytes 7077896 | tf_op jit(solution)/shard_map/ppermute | solution.py:73
  1069.6 29.6 %collective-permute-start.190 = (bf16[32,288,128]{2,1,0:T(8,128)(2,1)S(1)}, bf16[32,288,128]{2,1,0:T(8,128)(2,1)S(1)}, u32[]{:S(2)}, u32[]{:S(2)}) collective-permute-start(bf16[32,288,128]{2,1,0:T(8,128)(2,1)S(1)} %copy-done.220), channel_id=1, source_target_pairs={{0,32},{1,33},{2,34},{3,35},{4,36},{5,37},{6,38},{7,39},{8,40},{9,... | collective-permute-start | bytes 7077896 | tf_op jit(solution)/shard_map/ppermute | solution.py:73
  1097.3 40.0 %collective-permute-start.170 = (bf16[4096,256]{1,0:T(8,128)(2,1)S(1)}, bf16[4096,256]{1,0:T(8,128)(2,1)S(1)}, u32[]{:S(2)}, u32[]{:S(2)}) collective-permute-start(bf16[4096,256]{1,0:T(8,128)(2,1)S(1)} %constant_dynamic-update-slice_fusion.86.part2), channel_id=1, source_target_pairs={{0,4},{1,5},{2,6},{3,7},{4,0},{5,1},{6,2},{7,3},{8,12},{9,13},{10,... | collective-permute-start | bytes 6291464 | tf_op jit(solution)/shard_map/ppermute | solution.py:73
  1119.5 81.3 %collective-permute-start.191 = (bf16[16,288,128]{2,1,0:T(8,128)(2,1)}, bf16[16,288,128]{2,1,0:T(8,128)(2,1)}, u32[]{:S(2)}, u32[]{:S(2)}) collective-permute-start(bf16[16,288,128]{2,1,0:T(8,128)(2,1)} %add_convert_fusion.1), channel_id=1, source_target_pairs={{0,4},{1,5},{2,6},{3,7},{4,0},{5,1},{6,2},{7,3},{8,12},{9,13},{10,... | collective-permute-start | bytes 3538952 | tf_op jit(solution)/shard_map/ppermute | solution.py:73
  1131.1 39.8 %collective-permute-start.176 = (bf16[8,288,128]{2,1,0:T(8,128)(2,1)}, bf16[8,288,128]{2,1,0:T(8,128)(2,1)S(1)}, u32[]{:S(2)}, u32[]{:S(2)}) collective-permute-start(bf16[8,288,128]{2,1,0:T(8,128)(2,1)} %get-tuple-element.218), channel_id=1, source_target_pairs={{0,8},{1,9},{2,10},{3,11},{4,12},{5,13},{6,14},{7,15},{8,16},{9,17... | collective-permute-start | bytes 1769480 | tf_op jit(solution)/shard_map/ppermute | solution.py:73
  1131.1 63.3 %collective-permute-start.177 = (bf16[8,288,128]{2,1,0:T(8,128)(2,1)}, bf16[8,288,128]{2,1,0:T(8,128)(2,1)}, u32[]{:S(2)}, u32[]{:S(2)}) collective-permute-start(bf16[8,288,128]{2,1,0:T(8,128)(2,1)} %get-tuple-element.219), channel_id=1, source_target_pairs={{0,24},{1,25},{2,26},{3,27},{4,28},{5,29},{6,30},{7,31},{8,0},{9,1... | collective-permute-start | bytes 1769480 | tf_op jit(solution)/shard_map/ppermute | solution.py:73
  1134.0 62.3 %collective-permute-start.184 = (bf16[8,288,128]{2,1,0:T(8,128)(2,1)}, bf16[8,288,128]{2,1,0:T(8,128)(2,1)}, u32[]{:S(2)}, u32[]{:S(2)}) collective-permute-start(bf16[8,288,128]{2,1,0:T(8,128)(2,1)} %get-tuple-element.220), channel_id=1, source_target_pairs={{0,1},{1,2},{2,3},{3,0},{4,5},{5,6},{6,7},{7,4},{8,9},{9,10},{10,1... | collective-permute-start | bytes 1769480 | tf_op jit(solution)/shard_map/ppermute | solution.py:73
  1137.3 60.5 %collective-permute-start.185 = (bf16[8,288,128]{2,1,0:T(8,128)(2,1)}, bf16[8,288,128]{2,1,0:T(8,128)(2,1)}, u32[]{:S(2)}, u32[]{:S(2)}) collective-permute-start(bf16[8,288,128]{2,1,0:T(8,128)(2,1)} %get-tuple-element.221), channel_id=1, source_target_pairs={{0,3},{1,0},{2,1},{3,2},{4,7},{5,4},{6,5},{7,6},{8,11},{9,8},{10,9... | collective-permute-start | bytes 1769480 | tf_op jit(solution)/shard_map/ppermute | solution.py:73
  1170.9 65.5 %collective-permute-start.171 = (f32[1664,384]{1,0:T(8,128)S(1)}, f32[1664,384]{1,0:T(8,128)S(1)}, u32[]{:S(2)}, u32[]{:S(2)}) collective-permute-start(f32[1664,384]{1,0:T(8,128)S(1)} %slice_select_fusion), channel_id=1, source_target_pairs={{0,32},{1,33},{2,34},{3,35},{4,36},{5,37},{6,38},{7,39},{8,40},{9,... | collective-permute-start | bytes 7667720 | tf_op jit(solution)/shard_map/ppermute | solution.py:73
  1218.1 28.5 %collective-permute-start.223 = (f32[3,288,128]{2,1,0:T(8,128)}, f32[3,288,128]{2,1,0:T(8,128)}, u32[]{:S(2)}, u32[]{:S(2)}) collective-permute-start(f32[3,288,128]{2,1,0:T(8,128)} %pad_maximum_fusion.11), channel_id=1, source_target_pairs={{0,64},{1,65},{2,66},{3,67},{4,68},{5,69},{6,70},{7,71},{8,72},{9,... | collective-permute-start | bytes 1327112 | tf_op jit(solution)/shard_map/ppermute | solution.py:73
  (431 other events, 6418.5 us)

commit v2 on v1

--- a/solution.py
+++ b/solution.py
@@ -15,6 +15,7 @@
 PACK = 288
 LANES = 128
 HALF = 96
+SLOTS = 64
 
 exact_prec = lax.Precision.HIGHEST
 clip_bound = 0.02
@@ -81,10 +82,6 @@
     return permuted(value, axis, None)
 
 
-def crossed(value, axis, mask):
-    return permuted(value, axis, lambda at, c: at ^ mask)
-
-
 def z_flip(value):
     return turn(turn(value, "z", 1), "z", 1)
 
@@ -93,10 +90,6 @@
     near = turn(value, axis, -1)
     other = turn(value, axis, 1)
     return [value, near, turn(near, axis, -1), other]
-
-
-def gather4_direct(value, axis):
-    return [value, turn(value, axis, -1), turn(value, axis, 2), turn(value, axis, 1)]
 
 
 def wide(value):
@@ -111,19 +104,16 @@
     return wide(parts[0]) + wide(near) + wide(other)
 
 
-def reduce4_direct(parts, axis, kind):
-    near = turn(parts[1].astype(kind), axis, 1)
-    far = turn(parts[2].astype(kind), axis, 2)
-    other = turn(parts[3].astype(kind), axis, -1)
-    return wide(parts[0]) + wide(near) + wide(far) + wide(other)
-
-
 def sum_everywhere(value):
-    value = value + swap(value, "c")
-    for axis in ("z", "y", "x"):
-        one, two, three = (crossed(value, axis, mask) for mask in (1, 2, 3))
-        value = (value + one) + (two + three)
-    return value
+    shape, share = value.shape, value.size // len(COORDS)
+    parts = exchanged(value.reshape(len(COORDS), share), ("seq", "dp"))
+    total = jnp.sum(parts, axis=0, keepdims=True)
+    spread = jnp.broadcast_to(total, (len(COORDS), share))
+    return exchanged(spread, ("seq", "dp")).reshape(shape)
+
+
+def exchanged(value, axes):
+    return lax.all_to_all(value, axes, 0, 0, tiled=True)
 
 
 def pack_blocks(blocks, odd):
@@ -135,14 +125,10 @@
     return jnp.concatenate([main, rest], axis=1)
 
 
-def unpack_blocks(packed, odd):
-    odd = odd[:, None, None]
+def unpack_blocks(packed):
     main, rest = packed[:, :BS], packed[:, BS:]
-    left, right = rest[:, :, : LANES // 2], rest[:, :, LANES // 2 :]
-    half = jnp.concatenate([jnp.where(odd, right, left), jnp.where(odd, left, right)], axis=1)
-    return jnp.where(
-        odd, jnp.concatenate([half, main], axis=2), jnp.concatenate([main, half], axis=2)
-    )
+    half = jnp.concatenate([rest[:, :, : LANES // 2], rest[:, :, LANES // 2 :]], axis=1)
+    return jnp.concatenate([main, half], axis=2)
 
 
 def pieces_of(chunk):
@@ -161,36 +147,46 @@
 
 
 def assemble_kernel(places, *refs):
-    arrays, outs, (natural, sem) = refs[:20], refs[20:24], refs[24:]
+    arrays, outs, (halves, sems) = refs[:20], refs[20:24], refs[24:]
     at = 0
     for array in arrays:
-        count = array.shape[0]
 
         def fetch(q, carry, array=array, at=at):
-            pltpu.make_async_copy(array.at[q], natural.at[places[at + q]], sem).start()
+            tile = places[at + q]
+            pltpu.make_async_copy(array.at[q, pl.ds(BS, HALF)], halves.at[tile], sems.at[4]).start()
+            for which, out in enumerate(outs):
+                base, tall, across = MATRICES[which]
+
+                @pl.when((tile >= base) & (tile < base + tall * across))
+                def _(out=out, base=base, across=across, which=which):
+                    row, col = (tile - base) // across, (tile - base) % across
+                    left = pl.multiple_of((col // 2) * 2 * BS + (col % 2) * 2 * LANES, LANES)
+                    target = out.at[pl.ds(pl.multiple_of(row * BS, HALF), BS), pl.ds(left, LANES)]
+                    pltpu.make_async_copy(array.at[q, pl.ds(0, BS)], target, sems.at[which]).start()
+
             return carry
 
-        lax.fori_loop(0, count, fetch, 0)
-        at += count
-    pltpu.make_async_copy(natural, natural, sem).wait()
-    left = lax.broadcasted_iota(jnp.int32, (HALF, LANES), 1) < LANES // 2
+        lax.fori_loop(0, array.shape[0], fetch, 0)
+        at += array.shape[0]
+    pltpu.make_async_copy(halves, halves, sems.at[4]).wait()
+    for which, out in enumerate(outs):
+        most = out.at[:, pl.ds(0, 2 * out.shape[1] // 3)]
+        pltpu.make_async_copy(most, most, sems.at[which]).wait()
+    left_lanes = lax.broadcasted_iota(jnp.int32, (HALF, LANES), 1) < LANES // 2
     for out, (base, tall, across) in zip(outs, MATRICES, strict=True):
         pairs = across // 2
 
         def place(t, carry, out=out, base=base, pairs=pairs):
             row = pl.multiple_of((t // pairs) * BS, HALF)
-            col = pl.multiple_of((t % pairs) * 2 * BS, LANES)
-            even, odd = base + 2 * t, base + 2 * t + 1
-            out[pl.ds(row, BS), pl.ds(col, LANES)] = natural[even, :BS]
-            out[pl.ds(row, BS), pl.ds(col + 2 * LANES, LANES)] = natural[odd, :BS]
-            he, ho = wide(natural[even, BS:]), wide(natural[odd, BS:])
-            out[pl.ds(row, HALF), pl.ds(col + LANES, LANES)] = jnp.where(left, he, ho).astype(BF)
-            out[pl.ds(row + HALF, HALF), pl.ds(col + LANES, LANES)] = pltpu.roll(
-                jnp.where(left, ho, he), LANES // 2, 1
+            col = pl.multiple_of((t % pairs) * 2 * BS + LANES, LANES)
+            he, ho = wide(halves[base + 2 * t]), wide(halves[base + 2 * t + 1])
+            out[pl.ds(row, HALF), pl.ds(col, LANES)] = jnp.where(left_lanes, he, ho).astype(BF)
+            out[pl.ds(row + HALF, HALF), pl.ds(col, LANES)] = pltpu.roll(
+                jnp.where(left_lanes, ho, he), LANES // 2, 1
             ).astype(BF)
             return carry
 
-        lax.fori_loop(0, tall * pairs, place, 0)
+        lax.fori_loop(0, tall * pairs, place, 0, unroll=2)
 
 
 def assemble_layer(places, arrays):
@@ -202,7 +198,7 @@
             grid=(),
             in_specs=[pl.BlockSpec(memory_space=pl.ANY)] * len(arrays),
             out_specs=[pl.BlockSpec(memory_space=pltpu.VMEM)] * 4,
-            scratch_shapes=[pltpu.VMEM((BS, PACK, LANES), BF), pltpu.SemaphoreType.DMA],
+            scratch_shapes=[pltpu.VMEM((BS, HALF, LANES), BF), pltpu.SemaphoreType.DMA((5,))],
         ),
         out_shape=shapes,
         compiler_params=pltpu.CompilerParams(vmem_limit_bytes=40 * 1024 * 1024),
@@ -211,63 +207,78 @@
     )(places, *arrays)
 
 
-def weight_grad_kernel(places, *refs):
-    lefts, rights, outs, (natural, sem) = refs[:4], refs[4:8], refs[8:14], refs[14:]
-    left = lax.broadcasted_iota(jnp.int32, (HALF, LANES), 1) < LANES // 2
-    for lhs, rhs, (base, tall, across) in zip(lefts, rights, MATRICES, strict=True):
-        pairs = across // 2
-
-        def unit(t, carry, lhs=lhs, rhs=rhs, base=base, across=across, pairs=pairs):
-            rows, cols = t // pairs, t % pairs
-            span = 2 * BS
-            piece = lax.dot_general(
-                lhs[:, pl.ds(pl.multiple_of(rows * span, LANES), span)],
-                rhs[:, pl.ds(pl.multiple_of(cols * span, LANES), span)],
-                (((0,), (0,)), ((), ())),
-                preferred_element_type=F32,
+LEFT_ROWS = (768, 768, 768, 3072)
+RIGHT_ROWS = (2304, 768, 3072, 768)
+
+
+def tile_rows(tiles):
+    matrix = sum((tiles >= base).astype(jnp.int32) for base, _, _ in MATRICES[1:])
+    offset = tiles - jnp.take(jnp.array([m[0] for m in MATRICES]), matrix)
+    across = jnp.take(jnp.array([m[2] for m in MATRICES]), matrix)
+    left_base = jnp.take(jnp.array([0, 768, 1536, 2304]), matrix)
+    right_base = jnp.take(jnp.array([0, 2304, 3072, 6144]), matrix)
+    return jnp.stack(
+        [left_base + BS * (offset // across), right_base + BS * (offset % across)]
+    ).astype(jnp.int32)
+
+
+def weight_grad_kernel(rows, *refs):
+    sources, outs, (lefts, rights, sems) = refs[:16], refs[16:19], refs[19:]
+    for part in range(2):
+        for stack, sizes, first in ((lefts, LEFT_ROWS, 0), (rights, RIGHT_ROWS, 4)):
+            at = 0
+            for index, size in enumerate(sizes):
+                pltpu.make_async_copy(
+                    sources[8 * part + first + index],
+                    stack.at[pl.ds(at, size), pl.ds(256 * part, 256)],
+                    sems.at[first // 4],
+                ).start()
+                at += size
+    rights[pl.ds(sum(RIGHT_ROWS), 64)] = jnp.zeros((64, 512), BF)
+    pltpu.make_async_copy(lefts, lefts, sems.at[0]).wait()
+    filled = rights.at[pl.ds(0, sum(RIGHT_ROWS))]
+    pltpu.make_async_copy(filled, filled, sems.at[1]).wait()
+    left_lanes = lax.broadcasted_iota(jnp.int32, (HALF, LANES), 1) < LANES // 2
+    for chunk, out in enumerate(outs):
+
+        def tile(q, carry, chunk=chunk, out=out):
+            left = lefts[pl.ds(pl.multiple_of(rows[0, 32 * chunk + q], 64), BS)]
+            right = rights[pl.ds(pl.multiple_of(rows[1, 32 * chunk + q], 64), 256)]
+            value = lax.dot_general(
+                left, right, (((1,), (1,)), ((), ())), preferred_element_type=F32
             )
-            for r in range(2):
-                even = base + (2 * rows + r) * across + 2 * cols
-                strip = piece[r * BS : (r + 1) * BS]
-                natural[even, :BS] = strip[:, :LANES].astype(BF)
-                natural[even + 1, :BS] = strip[:, 2 * LANES :].astype(BF)
-                mid = strip[:, LANES : 2 * LANES]
-                top = mid[:HALF]
-                low = pltpu.roll(mid[HALF:], LANES // 2, 1)
-                natural[even, BS:] = jnp.where(left, top, low).astype(BF)
-                natural[even + 1, BS:] = jnp.where(left, low, top).astype(BF)
+            out[q, :BS] = value[:, :LANES].astype(BF)
+            rest = value[:, LANES:]
+            low = pltpu.roll(rest[HALF:], LANES // 2, 1)
+            out[q, BS:] = jnp.where(left_lanes, rest[:HALF], low).astype(BF)
             return carry
 
-        lax.fori_loop(0, (tall // 2) * pairs, unit, 0)
-    at = 0
-    for out in outs:
-
-        def put(q, carry, out=out, at=at):
-            pltpu.make_async_copy(natural.at[places[at + q]], out.at[q], sem).start()
-            return carry
-
-        lax.fori_loop(0, 32, put, 0)
-        at += 32
-    pltpu.make_async_copy(natural, natural, sem).wait()
-
-
-def weight_grads(places, lefts, rights):
+        lax.fori_loop(0, 32, tile, 0, unroll=2)
+
+
+def weight_grads(tiles, lefts, rights):
+    own = [value.T for value in (*lefts, *rights)]
+    other = [swap(value, "c") for value in own]
     return pl.pallas_call(
         weight_grad_kernel,
         grid_spec=pltpu.PrefetchScalarGridSpec(
             num_scalar_prefetch=1,
             grid=(),
-            in_specs=[pl.BlockSpec(memory_space=pltpu.VMEM)] * 8,
-            out_specs=[pl.BlockSpec(memory_space=pl.ANY)] * 6,
-            scratch_shapes=[pltpu.VMEM((BS, PACK, LANES), BF), pltpu.SemaphoreType.DMA],
+            in_specs=[pl.BlockSpec(memory_space=pl.ANY)] * 16,
+            out_specs=[pl.BlockSpec(memory_space=pltpu.VMEM)] * 3,
+            scratch_shapes=[
+                pltpu.VMEM((sum(LEFT_ROWS), 512), BF),
+                pltpu.VMEM((sum(RIGHT_ROWS) + 64, 512), BF),
+                pltpu.SemaphoreType.DMA((2,)),
+            ],
         ),
-        out_shape=[jax.ShapeDtypeStruct((32, PACK, LANES), BF)] * 6,
+        out_shape=[jax.ShapeDtypeStruct((32, PACK, LANES), BF)] * 3,
         compiler_params=pltpu.CompilerParams(vmem_limit_bytes=40 * 1024 * 1024),
         cost_estimate=pl.CostEstimate(
-            flops=2 * 256 * 7_077_888, bytes_accessed=21_000_000, transcendentals=0
+            flops=2 * 512 * 96 * BS * BS, bytes_accessed=20_000_000, transcendentals=0
         ),
         name="weight_grads",
-    )(places, *lefts, *rights)
+    )(tile_rows(tiles), *own, *other)
 
 
 def lookup_kernel(ids, table, out0, out1, out2, out3):
@@ -314,13 +325,10 @@
     )(ids, table)
 
 
-def scatter_kernel(order, ids, start, part0, part1, part2, part3, out, sums):
-    step = pl.program_id(0)
-
-    @pl.when(step == 0)
+def scatter_kernel(ids, start, part0, part1, part2, part3, out):
+    @pl.when(pl.program_id(0) == 0)
     def _():
         out[...] = start[...]
-        sums[...] = jnp.zeros(sums.shape, F32)
 
     rows, tokens = out.shape[0], ids.shape[2]
     place = lax.broadcasted_iota(jnp.int32, (rows, tokens), 0)
@@ -329,38 +337,89 @@
     for at, part in enumerate((part0[...], part1[...], last)):
         cols = slice(at * 256, (at + 1) * 256)
         out[:, cols] += jnp.dot(hot, part, preferred_element_type=F32)
-        sums[:, cols] += wide(part[:256]) + wide(part[256:])
-
-
-def scatter_rows(order, ids, start, parts):
+
+
+def scatter_rows(ids, start, parts):
     return pl.pallas_call(
         scatter_kernel,
-        grid_spec=pltpu.PrefetchScalarGridSpec(
-            num_scalar_prefetch=1,
-            grid=(16,),
-            in_specs=[
-                pl.BlockSpec((1, 1, 512), lambda t, order: (order[0, t], 0, 0)),
-                pl.BlockSpec(start.shape, lambda t, order: (0, 0)),
-                pl.BlockSpec((512, 256), lambda t, order: (order[0, t], 0)),
-                pl.BlockSpec((512, 256), lambda t, order: (order[1, t], 0)),
-                pl.BlockSpec((256, 256), lambda t, order: (order[0, t], 0)),
-                pl.BlockSpec((256, 256), lambda t, order: (order[0, t], 0)),
-            ],
-            out_specs=[
-                pl.BlockSpec(start.shape, lambda t, order: (0, 0)),
-                pl.BlockSpec((256, 768), lambda t, order: (0, 0)),
-            ],
-        ),
-        out_shape=[
-            jax.ShapeDtypeStruct(start.shape, F32),
-            jax.ShapeDtypeStruct((256, 768), F32),
+        grid=(16,),
+        in_specs=[
+            pl.BlockSpec((1, 1, 512), lambda t: (t, 0, 0)),
+            pl.BlockSpec(start.shape, lambda t: (0, 0)),
+            pl.BlockSpec((512, 256), lambda t: (t, 0)),
+            pl.BlockSpec((512, 256), lambda t: ((t % 4) * 4 + t // 4, 0)),
+            pl.BlockSpec((256, 256), lambda t: (t, 0)),
+            pl.BlockSpec((256, 256), lambda t: (t, 0)),
         ],
+        out_specs=pl.BlockSpec(start.shape, lambda t: (0, 0)),
+        out_shape=jax.ShapeDtypeStruct(start.shape, F32),
         compiler_params=pltpu.CompilerParams(vmem_limit_bytes=48 * 1024 * 1024),
         cost_estimate=pl.CostEstimate(
             flops=2 * 8192 * start.shape[0] * 768, bytes_accessed=25_000_000, transcendentals=0
         ),
         name="scatter_rows",
-    )(order, ids, start, *parts)
+    )(ids, start, *parts)
+
+
+def pick_rows_kernel(ids, table, out):
+    rows = table.shape[0]
+    lane = lax.broadcasted_iota(jnp.int32, (ids.shape[0], LANES), 1)
+    held = ids[...]
+    hot = jnp.concatenate(
+        [jnp.where(held == lane + at, 1.0, 0.0).astype(BF) for at in range(0, rows, LANES)], axis=1
+    )
+    out[...] = jnp.dot(hot, table[...], preferred_element_type=F32).astype(BF)
+
+
+def pick_table_rows(ids, table):
+    count, width = ids.size, table.shape[1]
+    spread = jnp.broadcast_to(ids.reshape(-1, 1), (count, LANES))
+    tall = min(512, count)
+    return pl.pallas_call(
+        pick_rows_kernel,
+        grid=(count // tall,),
+        in_specs=[
+            pl.BlockSpec((tall, LANES), lambda t: (t, 0)),
+            pl.BlockSpec(table.shape, lambda t: (0, 0)),
+        ],
+        out_specs=pl.BlockSpec((tall, width), lambda t: (t, 0)),
+        out_shape=jax.ShapeDtypeStruct((count, width), BF),
+        compiler_params=pltpu.CompilerParams(vmem_limit_bytes=40 * 1024 * 1024),
+        cost_estimate=pl.CostEstimate(
+            flops=2 * count * table.shape[0] * width, bytes_accessed=8_000_000, transcendentals=0
+        ),
+        name="pick_table_rows",
+    )(spread, table)
+
+
+def add_rows_kernel(ids, start, rows, out):
+    @pl.when(pl.program_id(0) == 0)
+    def _():
+        out[...] = start[...]
+
+    place = lax.broadcasted_iota(jnp.int32, (out.shape[0], ids.shape[2]), 0)
+    hot = jnp.where(place == ids[0], 1.0, 0.0).astype(BF)
+    out[...] += jnp.dot(hot, rows[...], preferred_element_type=F32)
+
+
+def add_table_rows(ids, start, rows):
+    count, width = rows.shape
+    return pl.pallas_call(
+        add_rows_kernel,
+        grid=(count // 512,),
+        in_specs=[
+            pl.BlockSpec((1, 1, 512), lambda t: (t, 0, 0)),
+            pl.BlockSpec(start.shape, lambda t: (0, 0)),
+            pl.BlockSpec((512, width), lambda t: (t, 0)),
+        ],
+        out_specs=pl.BlockSpec(start.shape, lambda t: (0, 0)),
+        out_shape=jax.ShapeDtypeStruct(start.shape, F32),
+        compiler_params=pltpu.CompilerParams(vmem_limit_bytes=48 * 1024 * 1024),
+        cost_estimate=pl.CostEstimate(
+            flops=2 * count * start.shape[0] * width, bytes_accessed=14_000_000, transcendentals=0
+        ),
+        name="add_table_rows",
+    )(ids.reshape(-1, 1, 512), start, rows)
 
 
 def product(left, right):
@@ -518,14 +577,6 @@
     )
 
 
-def merge_stats(first_part, second_part):
-    peak = jnp.maximum(first_part[0], second_part[0])
-    summed = first_part[1] * jnp.exp(first_part[0] - peak) + second_part[1] * jnp.exp(
-        second_part[0] - peak
-    )
-    return jnp.stack([peak, summed, first_part[2] + second_part[2]])
-
-
 def adam_update(param, grad, first, second, rate, decay):
     first = first_decay * first + (1.0 - first_decay) * grad
     second = second_decay * second + (1.0 - second_decay) * grad * grad
@@ -563,19 +614,15 @@
 def reduce_weights(arrays, layer_idx, z_hi):
     blocks = []
     for chunk in range(3):
-        mine, theirs = arrays[chunk], swap(arrays[3 + chunk], "c")
         axis, size, count = pieces_of(chunk)
-        parts = [
-            wide(mine[p * size : (p + 1) * size]) + wide(theirs[p * size : (p + 1) * size])
-            for p in range(count)
-        ]
+        parts = [arrays[chunk][p * size : (p + 1) * size] for p in range(count)]
         if chunk < 2:
             value = reduce4(parts, axis, BF)
             other = "x" if axis == "y" else "y"
             value = reduce4([value[2 * m : 2 * m + 2] for m in range(4)], other, BF)
             value = value[:1] + wide(swap(value[1:].astype(BF), "zl"))
         else:
-            value = parts[0] + wide(swap(parts[1].astype(BF), "zl"))
+            value = wide(parts[0]) + wide(swap(parts[1], "zl"))
             value = reduce4([value[4 * m : 4 * m + 4] for m in range(4)], "y", BF)
             value = reduce4([value[m : m + 1] for m in range(4)], "x", BF)
         blocks.append(value)
@@ -657,36 +704,67 @@
         return jnp.where(inside, ((offset % 2) ^ z_hi) * padded + offset // 2, -1)
 
     packed = pack_blocks(squared_blocks(weights).astype(BF), own_odd)
-    layer_weights = [
-        assemble_layer(places[layer_idx], gather_weights(packed, layer_idx, z_hi))
-        for layer_idx in range(LAYERS)
-    ]
+    layer_weights = []
+    for layer_idx in range(LAYERS):
+        arrays = gather_weights(packed, layer_idx, z_hi)
+        packed, arrays[2], arrays[6], arrays[9] = lax.optimization_barrier(
+            (packed, arrays[2], arrays[6], arrays[9])
+        )
+        layer_weights.append(assemble_layer(places[layer_idx], arrays))
     all_params = [layer_params(small_params, layer_idx) for layer_idx in range(LAYERS)]
+
+    sequences = token_ids.shape[0]
+    shard_of = token_ids // (2 * table_rows)
+    held_by = (shard_of[:, None, :] == jnp.arange(sequences)[None, :, None]).astype(BF)
+    before = (jnp.arange(span_len)[:, None] <= jnp.arange(span_len)[None, :]).astype(BF)
+    ranks = product(held_by.reshape(-1, span_len), before).reshape(held_by.shape).astype(jnp.int32) - 1
+    crowded = jnp.max(ranks[:, :, -1]) >= SLOTS
+    crowded = jnp.broadcast_to(crowded.astype(F32), (8, LANES))
+    crowded = jnp.maximum(crowded, swap(crowded, "c"))
+    crowded = jnp.maximum(crowded, swap(crowded, "zh"))[0, 0] > 0.0
+    all_rows = local_row(token_ids)
+    own_ranks = lax.dynamic_index_in_dim(ranks, row_at, 1, keepdims=False)
+    slots = jnp.arange(SLOTS)
+    in_slot = (own_ranks[:, None, :] == slots[None, :, None]) & (all_rows >= 0)[:, None, :]
+    slot_rows = jnp.sum(jnp.where(in_slot, all_rows[:, None, :] + 1, 0), axis=2) - 1
+    arrived = exchanged(pick_table_rows(slot_rows, table_bf), "dp")
+    my_shards = lax.dynamic_index_in_dim(shard_of, row_at, 0, keepdims=False)
+    my_ranks = lax.dynamic_index_in_dim(ranks, row_at, 0, keepdims=False)
+    my_rank = jnp.sum(jnp.where(my_shards[None, :] == jnp.arange(sequences)[:, None], my_ranks, 0), axis=0)
+    my_slots = jnp.where(my_rank < SLOTS, my_shards * SLOTS + my_rank, -1)
+    slot_hot = my_slots[:, None] == jnp.arange(sequences * SLOTS)[None, :]
+    looked = product(slot_hot.astype(BF), arrived)
 
     far_y = (y_at + own_shift) % 4
     far_x = (x_at + own_shift) % 4
     far_z = zl_at ^ jnp.arange(2)
     rows_xyz = far_y[None, :, None] * 8 + far_z[None, None, :] * 4 + far_x[:, None, None]
-    token_rows = local_row(jnp.take(token_ids, rows_xyz.reshape(-1), axis=0))
-    spread_ids = jnp.broadcast_to(token_rows.reshape(-1, 1), (token_rows.size, LANES))
-    found0, found1, found2, found3 = lookup(spread_ids, table_bf)
+    crowd_rows = jnp.where(own_ranks >= SLOTS, all_rows, -1)
+    crowd_rows = jnp.take(crowd_rows, rows_xyz.reshape(-1), axis=0)
 
     def quarters(value):
         return jnp.split(value, 4, axis=0)
 
-    def plain_reduce4(parts, axis):
-        near = turn(parts[1] + turn(parts[2], axis, 1), axis, 1)
-        return (parts[0] + near) + turn(parts[3], axis, -1)
-
-    def last_pair(value):
-        return value[:span_len] + swap(value[span_len:], "zl")
-
-    looked = [
-        last_pair(plain_reduce4(quarters(plain_reduce4(quarters(found0), "x")), "y")),
-        last_pair(plain_reduce4(quarters(plain_reduce4(quarters(found1), "y")), "x")),
-        plain_reduce4(quarters(plain_reduce4(quarters(found2 + swap(found3, "zl")), "x")), "y"),
-    ]
-    residual = wide(jnp.concatenate(looked, axis=1)) + positions
+    def dense_rows():
+        spread_ids = jnp.broadcast_to(crowd_rows.reshape(-1, 1), (crowd_rows.size, LANES))
+        found0, found1, found2, found3 = lookup(spread_ids, table_bf)
+
+        def plain_reduce4(parts, axis):
+            near = turn(parts[1] + turn(parts[2], axis, 1), axis, 1)
+            return (parts[0] + near) + turn(parts[3], axis, -1)
+
+        def last_pair(value):
+            return value[:span_len] + swap(value[span_len:], "zl")
+
+        parts = [
+            last_pair(plain_reduce4(quarters(plain_reduce4(quarters(found0), "x")), "y")),
+            last_pair(plain_reduce4(quarters(plain_reduce4(quarters(found1), "y")), "x")),
+            plain_reduce4(quarters(plain_reduce4(quarters(found2 + swap(found3, "zl")), "x")), "y"),
+        ]
+        return wide(jnp.concatenate(parts, axis=1))
+
+    looked = looked + lax.cond(crowded, dense_rows, lambda: jnp.zeros((span_len, model_width), F32))
+    residual = looked + positions
 
     doc_row = doc_ids[0]
     query_places = seq_at * span_len + jnp.arange(span_len)
@@ -710,75 +788,31 @@
     final_bf = final_norm.astype(BF)
 
     pick_dev = pick_slots.shape[1]
-    half_picks = pick_dev // 2
     own_picks = lax.dynamic_index_in_dim(pick_slots, row_at, 0, keepdims=False)
     own_valid = own_picks >= 0
     pick_rows = jnp.maximum(own_picks, 0)
     chosen = jnp.where(own_valid[:, None], jnp.take(final_bf, pick_rows, axis=0), jnp.zeros((), BF))
-    gathered = []
-    for chunk in range(2):
-        value = chosen[chunk * half_picks : (chunk + 1) * half_picks]
-        value = jnp.concatenate([value, swap(value, "zl")], axis=0)
-        first, last = (("x", "y"), ("y", "x"))[chunk]
-        value = jnp.concatenate(gather4_direct(value, first), axis=0)
-        gathered += gather4(value, last)
-    gathered = jnp.concatenate(gathered, axis=0)
-    rows_yxz = jnp.transpose(rows_xyz, (1, 0, 2)).reshape(-1)
-    rows_xyz = rows_xyz.reshape(-1)
-
-    def in_order(table):
-        return jnp.concatenate(
-            [
-                jnp.take(table[:, :half_picks], rows_yxz, axis=0).reshape(-1),
-                jnp.take(table[:, half_picks:], rows_xyz, axis=0).reshape(-1),
-            ]
-        )
-
-    valid_all = in_order(pick_slots) >= 0
-    label_rows = local_row(in_order(labels))
+    gathered = exchanged(jnp.tile(chosen, (sequences, 1)), "dp")
+    valid_all = pick_slots.reshape(-1) >= 0
+    label_rows = local_row(labels.reshape(-1))
     logits = jnp.where(row_used[None, :], product_nt(gathered, table_bf), -1e30)
     hits = label_rows[:, None] == jnp.arange(vocab_rows)[None, :]
     peak = jnp.max(logits, axis=1)
     exp_total = jnp.sum(jnp.exp(logits - peak[:, None]), axis=1)
     target = jnp.sum(jnp.where(hits, logits, 0.0), axis=1)
-    stats = jnp.stack([peak, exp_total, target])
-    devices = jnp.arange(32)
-    at_y = jnp.take(own_shift, (devices // 8 - y_at) % 4)
-    at_x = jnp.take(own_shift, (devices % 4 - x_at) % 4)
-    at_z = (devices // 4) % 2 ^ zl_at
-    back_y = (at_y * 4 + at_x) * 2 + at_z
-    back_x = (at_x * 4 + at_y) * 2 + at_z
-
-    def reorder(value, first_order, second_order):
-        value = value.reshape(value.shape[0], 2, 32, half_picks)
-        return jnp.stack(
-            [jnp.take(value[:, 0], first_order, axis=1), jnp.take(value[:, 1], second_order, axis=1)],
-            axis=1,
-        ).reshape(value.shape[0], -1)
-
-    stats = reorder(stats, back_y, back_x)
-    stats = merge_stats(stats, swap(stats, "zl"))
-    for axis in ("x", "y"):
-        one, two, three = (crossed(stats, axis, mask) for mask in (1, 2, 3))
-        stats = merge_stats(merge_stats(stats, one), merge_stats(two, three))
-    stats = reorder(stats, rows_yxz, rows_xyz)
-    log_total = stats[0] + jnp.log(stats[1])
-    losses = jnp.where(valid_all, log_total - stats[2], 0.0).reshape(2, 32, half_picks)
-    loss_own = jnp.sum(losses[:, 0])
+    stats = jnp.stack([peak, exp_total, target]).reshape(1, -1)
+    stats = exchanged(jnp.tile(stats, (sequences, 1)), "dp").reshape(sequences, 3, -1)
+    top = jnp.max(stats[:, 0], axis=0)
+    log_total = top + jnp.log(jnp.sum(stats[:, 1] * jnp.exp(stats[:, 0] - top[None]), axis=0))
+    losses = jnp.where(valid_all, log_total - jnp.sum(stats[:, 2], axis=0), 0.0)
+    loss_own = jnp.sum(lax.dynamic_slice_in_dim(losses, row_at * pick_dev, pick_dev))
     count_own = jnp.sum(own_valid.astype(F32))
     grad_logits = jnp.where(
         valid_all[:, None], jnp.exp(logits - log_total[:, None]) - hits.astype(F32), 0.0
     ).astype(BF)
     head_grad = product_tn(grad_logits, gathered)
-    grad_gathered = product(grad_logits, table_bf)
-    grad_chosen = []
-    for chunk in range(2):
-        value = grad_gathered[chunk * 32 * half_picks : (chunk + 1) * 32 * half_picks]
-        first, last = (("y", "x"), ("x", "y"))[chunk]
-        value = reduce4(quarters(value), first, BF)
-        value = reduce4_direct(quarters(value), last, F32)
-        grad_chosen.append(value[:half_picks] + swap(value[half_picks:], "zl"))
-    grad_chosen = jnp.concatenate(grad_chosen, axis=0)
+    grad_chosen = exchanged(product(grad_logits, table_bf).astype(BF), "dp")
+    grad_chosen = jnp.sum(wide(grad_chosen.reshape(sequences, pick_dev, model_width)), axis=0)
     grad_final = (
         jnp.zeros((span_len, model_width), F32)
         .at[pick_rows]
@@ -796,31 +830,37 @@
             all_params[layer_idx],
             doc_mask,
         )
-        own_parts[layer_idx] = reduce_weights(
-            weight_grads(places[layer_idx], lefts, rights), layer_idx, z_hi
+        tiles = weight_grads(places[layer_idx][:96], lefts, rights)
+        if layer_idx:
+            grad_resid, tiles = lax.optimization_barrier((grad_resid, tiles))
+        own_parts[layer_idx] = reduce_weights(tiles, layer_idx, z_hi)
+        small_parts[layer_idx] = small_part
+    own_blocks = unpack_blocks(jnp.where(z_hi == 0, own_parts[0], own_parts[1]))
+
+    grad_bf = grad_resid.astype(BF)
+    slot_grads = product_tn(slot_hot.astype(BF), grad_bf).astype(BF)
+    grad_table = add_table_rows(slot_rows, head_grad, exchanged(slot_grads, "dp"))
+
+    def dense_grads():
+        columns = [grad_bf[:, at : at + 256] for at in range(0, model_width, 256)]
+
+        def joined(parts):
+            return jnp.concatenate(parts, axis=0)
+
+        pair0 = joined([columns[0], swap(columns[0], "zl")])
+        spread0 = joined(gather4(joined(gather4(pair0, "y")), "x"))
+        pair1 = joined([columns[1], swap(columns[1], "zl")])
+        spread1 = joined(gather4(joined(gather4(pair1, "x")), "y"))
+        spread2 = joined(gather4(joined(gather4(columns[2], "y")), "x"))
+        spread3 = swap(spread2, "zl")
+        return scatter_rows(
+            crowd_rows.reshape(16, 1, 512), grad_table, (spread0, spread1, spread2, spread3)
         )
-        small_parts[layer_idx] = small_part
-    own_blocks = unpack_blocks(jnp.where(z_hi == 0, own_parts[0], own_parts[1]), own_odd)
-
-    grad_bf = grad_resid.astype(BF)
-    columns = [grad_bf[:, at : at + 256] for at in range(0, model_width, 256)]
-
-    def joined(parts):
-        return jnp.concatenate(parts, axis=0)
-
-    pair0 = joined([columns[0], swap(columns[0], "zl")])
-    spread0 = joined(gather4(joined(gather4(pair0, "y")), "x"))
-    pair1 = joined([columns[1], swap(columns[1], "zl")])
-    spread1 = joined(gather4(joined(gather4(pair1, "x")), "y"))
-    spread2 = joined(gather4(joined(gather4(columns[2], "y")), "x"))
-    spread3 = swap(spread2, "zl")
-    steps = jnp.arange(16)
-    step_y = jnp.take(own_shift, (steps // 4 - y_at) % 4)
-    step_x = jnp.take(own_shift, (steps % 4 - x_at) % 4)
-    order = jnp.stack([step_x * 4 + step_y, step_y * 4 + step_x]).astype(jnp.int32)
-    grad_table, pos_sum = scatter_rows(
-        order, token_rows.reshape(16, 1, 512), head_grad, (spread0, spread1, spread2, spread3)
-    )
+
+    grad_table = lax.cond(crowded, dense_grads, lambda: grad_table)
+    pos_parts = exchanged(grad_resid, "dp").reshape(sequences, -1, model_width)
+    pos_own = jnp.sum(pos_parts, axis=0)
+    pos_sum = exchanged(jnp.tile(pos_own, (sequences, 1)), "dp")
     left_half, right_half = grad_table[:, :half_width], grad_table[:, half_width:]
     grad_half = jnp.where(core == 0, left_half, right_half) + swap(
         jnp.where(core == 0, right_half, left_half), "c"
@@ -837,25 +877,26 @@
     small_grad = jnp.concatenate(
         [jnp.stack(gain_list + [g_final_gain]), jnp.stack(shift_list + [g_final_shift])]
         + [small_parts[layer_idx][4] for layer_idx in range(LAYERS)]
-        + [scalars[None]],
+        + [scalars[None], jnp.zeros((5, model_width), F32)],
         axis=0,
     )
     small_all = sum_everywhere(small_grad)
-    small_sum, ce_sum, pick_count = small_all[:-1], small_all[-1, 0], small_all[-1, 1]
+    rows = small_params.shape[0]
+    small_sum, ce_sum, pick_count = small_all[:rows], small_all[rows, 0], small_all[rows, 1]
 
     g_table = grad_own / pick_count
     g_pos = pos_sum / pick_count
     g_small = small_sum / pick_count
     g_ce = own_blocks.reshape(weights.shape) / pick_count
     g_blocks = g_ce + ewc_weight * fisher * (weights - anchor)
-    first_row = row_at == 0
-    first_seq = seq_at == 0
+    g_pos_own = pos_own / pick_count
     local_squares = jnp.sum(g_table * g_table) + jnp.sum(g_blocks * g_blocks)
-    local_squares = local_squares + jnp.where(first_row, jnp.sum(g_pos * g_pos), 0.0)
+    local_squares = local_squares + jnp.sum(g_pos_own * g_pos_own)
     local_squares = local_squares + jnp.where(
-        first_row & first_seq, jnp.sum(g_small * g_small), 0.0
-    )
-    grad_norm = jnp.sqrt(sum_everywhere(jnp.broadcast_to(local_squares, (8, LANES)))[0, 0])
+        (row_at == 0) & (seq_at == 0), jnp.sum(g_small * g_small), 0.0
+    )
+    all_squares = exchanged(jnp.broadcast_to(local_squares, (len(COORDS), LANES)), ("seq", "dp"))
+    grad_norm = jnp.sqrt(jnp.sum(all_squares[:, 0]))
     factor = jnp.minimum(1.0, clip_bound / grad_norm)
     table_new, table_first, table_second = adam_update(
         vocab_table, factor * g_table, vocab_first, vocab_second, table_rate, decay_rate

time: 1340 us -> 1200 us (0.90)
  starting transfers between devices: 399 us -> 286 us
  Pallas kernels: 179 us -> 119 us
  waiting for transfers between devices: 296 us -> 238 us
  blocking collectives: 0 us -> 40.8 us
  other arithmetic: 157 us -> 179 us
  local copies, waits for them, and re-layouts: 123 us -> 144 us
    ppermute x234 -> x149, starting transfers between devices: 399 us -> 224 us  [permuted(): return lax.ppermute(value, ('seq', 'dp'), pairs)]
    ppermute x234 -> x149, waiting for transfers between devices: 296 us -> 147 us  [permuted(): return lax.ppermute(value, ('seq', 'dp'), pairs)]
    all_to_all x0 -> x9, waiting for transfers between devices: none -> 90.6 us  [exchanged(): return lax.all_to_all(value, axes, 0, 0, tiled=True)]
    all_to_all x0 -> x9, starting transfers between devices: none -> 62.4 us  [exchanged(): return lax.all_to_all(value, axes, 0, 0, tiled=True)]
    all_to_all x0 -> x1, blocking collectives: none -> 40.8 us  [exchanged(): return lax.all_to_all(value, axes, 0, 0, tiled=True)]
    pallas_call x2, Pallas kernels: 58.4 us -> 20.2 us  [the longest x1 11.1 us: add_table_rows(): pl.pallas_call(add_rows_kernel, grid=(count // 512,), in_specs=[pl.BlockS...]
    unnamed x542 -> x511, local copies, waits for them, and re-layouts: 37 us -> 32.8 us
    dot_general x9 -> x11, matrix products: 26.5 us -> 29.3 us  [product(): return jnp.dot(left, right, preferred_element_type=F32)]
  transfers between devices with their start and end apart: 234 -> 158, of which waited for: 86 -> 38; matrix products, arithmetic and copies ran while one was open for 12% -> 20% of each run, Pallas kernels for 14% -> 7%
where the time goes in v2:
time: 1200 us; the launch traced here: 1190 us
  starting transfers between devices  286 us (24%)
  waiting for transfers between devices  238 us (20%)
  other arithmetic  179 us (15%)
  matrix products  163 us (14%)
  local copies, waits for them, and re-layouts  144 us (12%)
  Pallas kernels  119 us (10%)
  blocking collectives  40.8 us (3%)
    ppermute x149, starting transfers between devices, permuted(): return lax.ppermute(value, ('seq', 'dp'), pairs)  224 us
    ppermute x149, waiting for transfers between devices, permuted(): return lax.ppermute(value, ('seq', 'dp'), pairs)  147 us
    all_to_all x9, waiting for transfers between devices, exchanged(): return lax.all_to_all(value, axes, 0, 0, tiled=True)  90.6 us
    all_to_all x9, starting transfers between devices, exchanged(): return lax.all_to_all(value, axes, 0, 0, tiled=True)  62.4 us
    pallas_call x2, Pallas kernels, weight_grads(): pl.pallas_call(weight_grad_kernel, grid_spec=pltpu.PrefetchScalarGridSpec...  49.7 us
    pallas_call x2, Pallas kernels, assemble_layer(): pl.pallas_call(assemble_kernel, grid_spec=pltpu.PrefetchScalarGridSpec(nu...  49.6 us
    all_to_all x1, blocking collectives, exchanged(): return lax.all_to_all(value, axes, 0, 0, tiled=True)  40.8 us
    dot_general x9, matrix products, product_nt(): lax.dot_general(left, right, (((1,), (1,)), ((), ())), preferred_element_...  36.5 us
  transfers between devices with their start and end apart: 158, of which 38 were waited for; matrix products, arithmetic and copies ran while one was open for 20% of the time, Pallas kernels for 7%

profile of v2, /device:TPU:1, one launch (start us, length us, event | category | flops | bytes accessed | tf_op | source)
XLA Modules:
  0.0 1191.1 jit_solution(345738866097879207)
XLA Ops:
  40.6 9.8 conditional.2
  94.9 9.1 pick_table_rows.1
  104.0 8.4 all-to-all-start
  119.5 7.6 collective-permute-start.74
  127.0 22.5 %collective-permute-done.84 = bf16[3,288,128]{2,1,0:T(8,128)(2,1)S(1)} collective-permute-done((bf16[3,288,128]{2,1,0:T(8,128)(2,1)S(1)}, bf16[3,288,128]{2,1,0:T(8,128)(2,1)S(1)}, u32[]{:S(2)}, u32[]{:S(2)}) %collective-permute-start.84) | collective-permute-done | bytes 221216 | tf_op jit(solution)/shard_map/ppermute | solution.py:74
  210.0 24.9 %assemble.2 = (bf16[768,2304]{1,0:T(8,128)(2,1)}, bf16[768,768]{1,0:T(8,128)(2,1)S(1)}, bf16[768,3072]{1,0:T(8,128)(2,1)}, bf16[3072,768]{1,0:T(8,128)(2,1)}) custom-call(s32[192]{0:T(256)S(1)} %get-tuple-element.368.places, bf16[8,288,128]{2,1,0:T(8,128)(2,1)S(1)} %copy-done.7, bf16[8,288,128]{2,1,0:T(8,128)(2,1)} %collective-permute-done.53.refs_1_, ...), custom_call_target="tpu_custom_call" | custom-call | bytes 29000000 | tf_op jit(solution)/shard_map/assemble/pallas_call | solution.py:194
  250.7 6.1 collective-permute-start.111
  259.5 12.6 %collective-permute-start.107 = (bf16[8,288,128]{2,1,0:T(8,128)(2,1)}, bf16[8,288,128]{2,1,0:T(8,128)(2,1)}, u32[]{:S(2)}, u32[]{:S(2)}) collective-permute-start(bf16[8,288,128]{2,1,0:T(8,128)(2,1)} %collective-permute-done.89.refs_1_), channel_id=1, source_target_pairs={{0,32},{1,33},{2,34},{3,35},{4,36},{5,37},{6,38},{7,39},{8,40},{9,... | collective-permute-start | bytes 1769480 | tf_op jit(solution)/shard_map/ppermute | solution.py:74
  277.1 7.6 collective-permute-start.115
  313.8 24.6 %assemble.3 = (bf16[768,2304]{1,0:T(8,128)(2,1)}, bf16[768,768]{1,0:T(8,128)(2,1)S(1)}, bf16[768,3072]{1,0:T(8,128)(2,1)}, bf16[3072,768]{1,0:T(8,128)(2,1)}) custom-call(s32[192]{0:T(256)S(1)} %get-tuple-element.367.places, bf16[8,288,128]{2,1,0:T(8,128)(2,1)S(1)} %copy-done.9, bf16[8,288,128]{2,1,0:T(8,128)(2,1)} %collective-permute-done.89.refs_1_, ...), custom_call_target="tpu_custom_call" | custom-call | bytes 29000000 | tf_op jit(solution)/shard_map/assemble/pallas_call | solution.py:194
  347.8 10.5 fusion.322
  358.3 7.3 fusion.102
  375.1 10.9 collective-permute-done.117
  388.7 8.5 collective-permute-done.118
  414.6 10.5 fusion.325
  425.1 8.0 fusion.105
  449.6 40.7 %all-to-all-done.1 = bf16[32,64,768]{2,1,0:T(8,128)(2,1)} async-done(((bf16[32,64,768]{2,1,0:T(8,128)(2,1)}), bf16[32,64,768]{2,1,0:T(8,128)(2,1)}, u32[]{:S(2)}, u32[]{:S(2)}) %all-to-all-start.1) | async-done | bytes 3145760 | tf_op jit(solution)/shard_map/all_to_all | solution.py:116
  490.3 8.4 select_reduce_fusion.1
  498.8 5.9 exponential_reduce_fusion
  506.1 8.0 all-to-all-start.2
  514.2 12.2 %all-to-all-done.2 = f32[32,1,6144]{2,1,0:T(1,128)S(1)} async-done(((f32[32,1,6144]{2,1,0:T(1,128)}), f32[32,1,6144]{2,1,0:T(1,128)S(1)}, u32[]{:S(2)}, u32[]{:S(2)}) %all-to-all-start.2) | async-done | bytes 786464 | tf_op jit(solution)/shard_map/all_to_all | solution.py:116
  532.4 8.0 select_convert_fusion
  540.5 9.9 convolution_convert_fusion.1
  550.4 40.8 %all_to_all.87 = bf16[32,64,768]{2,1,0:T(8,128)(2,1)S(1)} all-to-all(bf16[32,64,768]{2,1,0:T(8,128)(2,1)S(1)} %bitcast.364), channel_id=1, replica_groups=mesh['seq'=4,'dp'=32] {'dp'}, dimensions={0} | all-to-all | bytes 6291456 | tf_op jit(solution)/shard_map/all_to_all | solution.py:116
  598.8 8.1 convert_reduce_fusion.1
  618.0 10.8 multiply_reduce_fusion.1
  634.9 5.9 multiply_convert_fusion.1
  651.5 9.3 collective-permute-done.122
  695.7 26.2 %weight_grads.2 = (bf16[32,288,128]{2,1,0:T(8,128)(2,1)}, bf16[32,288,128]{2,1,0:T(8,128)(2,1)}, bf16[32,288,128]{2,1,0:T(8,128)(2,1)}) custom-call(s32[2,96]{1,0:T(2,128)S(1)} %pad_add_fusion.rows, bf16[768,256]{1,0:T(8,128)(2,1)S(1)} %get-tuple-element.315.refs_0_, bf16[768,256]{1,0:T(8,128)(2,1)} %bitcast.62.refs_1_, bf16[768,256]{1,0:T(8,128)(2,1)S(1)} %copy-done.32, ...), custom_call_target="tpu_custom_call" | custom-call | flops 3623878656 | bytes 20000000 | tf_op jit(solution)/shard_map/weight_grads/pallas_call | solution.py:262
  721.9 8.0 convert_reduce_fusion.2
  738.9 10.6 multiply_reduce_fusion
  755.5 5.9 multiply_convert_fusion
  767.3 10.7 collective-permute-done.134
  781.1 8.2 collective-permute-done.135
  806.5 10.1 fusion.332.start
  817.7 26.3 %all-to-all-done.6 = bf16[32,64,768]{2,1,0:T(8,128)(2,1)S(1)} async-done(((bf16[32,64,768]{2,1,0:T(8,128)(2,1)}), bf16[32,64,768]{2,1,0:T(8,128)(2,1)S(1)}, u32[]{:S(2)}, u32[]{:S(2)}) %all-to-all-start.6) | async-done | bytes 3145760 | tf_op jit(solution)/shard_map/all_to_all | solution.py:116
  844.0 11.1 add_table_rows.1
  924.4 6.0 collective-permute-start.144
  930.4 6.2 collective-permute-start.141
  958.0 23.5 %weight_grads.3 = (bf16[32,288,128]{2,1,0:T(8,128)(2,1)}, bf16[32,288,128]{2,1,0:T(8,128)(2,1)}, bf16[32,288,128]{2,1,0:T(8,128)(2,1)}) custom-call(s32[2,96]{1,0:T(2,128)S(1)} %pad_add_fusion.1.rows, bf16[768,256]{1,0:T(8,128)(2,1)S(1)} %copy-done.25, bf16[768,256]{1,0:T(8,128)(2,1)S(1)} %bitcast.328, bf16[768,256]{1,0:T(8,128)(2,1)S(1)} %copy-done.31, ...), custom_call_target="tpu_custom_call" | custom-call | flops 3623878656 | bytes 20000000 | tf_op jit(solution)/shard_map/weight_grads/pallas_call | solution.py:262
  988.7 12.1 %all-to-all-start.4 = ((f32[128,1,192]{2,1,0:T(1,128)}), f32[128,1,192]{2,1,0:T(1,128)}, u32[]{:S(2)}, u32[]{:S(2)}) async-start(f32[128,1,192]{2,1,0:T(1,128)} %all_to_all.76), calls=%async_computation.4 | async-start | bytes 262144 | tf_op jit(solution)/shard_map/all_to_all | solution.py:116
  1012.5 6.4 all-to-all-start.5
  1045.3 11.9 collective-permute-done.161
  1074.8 6.1 collective-permute-start.190
  1083.3 6.5 collective-permute-done.153
  1113.3 5.9 collective-permute-start.138
  1133.4 7.1 all-to-all-start.8
  1143.2 7.2 all-to-all-done.8
  (1152 shorter events, 607.6 us)
Async XLA Ops:
  8.0 29.5 %collective-permute-start.44 = (bf16[832,384]{1,0:T(8,128)(2,1)}, bf16[832,384]{1,0:T(8,128)(2,1)}, u32[]{:S(2)}, u32[]{:S(2)}) collective-permute-start(bf16[832,384]{1,0:T(8,128)(2,1)} %get-tuple-element.320), channel_id=1, source_target_pairs={{0,32},{1,33},{2,34},{3,35},{4,36},{5,37},{6,38},{7,39},{8,40},{9,... | collective-permute-start | bytes 1916936 | tf_op jit(solution)/shard_map/ppermute | solution.py:74
  9.7 25.8 %collective-permute-start.48 = (bf16[3,288,128]{2,1,0:T(8,128)(2,1)S(1)}, bf16[3,288,128]{2,1,0:T(8,128)(2,1)S(1)}, u32[]{:S(2)}, u32[]{:S(2)}) collective-permute-start(bf16[3,288,128]{2,1,0:T(8,128)(2,1)S(1)} %maximum_maximum_fusion), channel_id=1, source_target_pairs={{0,64},{1,65},{2,66},{3,67},{4,68},{5,69},{6,70},{7,71},{8,72},{9,... | collective-permute-start | bytes 663560 | tf_op jit(solution)/shard_map/ppermute | solution.py:74
  87.3 28.4 %collective-permute-start.67 = (bf16[16,288,128]{2,1,0:T(8,128)(2,1)S(1)}, bf16[16,288,128]{2,1,0:T(8,128)(2,1)S(1)}, u32[]{:S(2)}, u32[]{:S(2)}) collective-permute-start(bf16[16,288,128]{2,1,0:T(8,128)(2,1)S(1)} %constant_dynamic-update-slice_fusion.43.refs_8_), channel_id=1, source_target_pairs={{0,4},{1,5},{2,6},{3,7},{4,0},{5,1},{6,2},{7,3},{8,12},{9,13},{10,... | collective-permute-start | bytes 3538952 | tf_op jit(solution)/shard_map/ppermute | solution.py:74
  104.0 131.0 %all-to-all-start = ((bf16[32,64,768]{2,1,0:T(8,128)(2,1)}), bf16[32,64,768]{2,1,0:T(8,128)(2,1)}, u32[]{:S(2)}, u32[]{:S(2)}) async-start(bf16[32,64,768]{2,1,0:T(8,128)(2,1)} %bitcast.9), calls=%async_computation | async-start | bytes 6291456 | tf_op jit(solution)/shard_map/all_to_all | solution.py:116
  115.7 33.8 %collective-permute-start.84 = (bf16[3,288,128]{2,1,0:T(8,128)(2,1)S(1)}, bf16[3,288,128]{2,1,0:T(8,128)(2,1)S(1)}, u32[]{:S(2)}, u32[]{:S(2)}) collective-permute-start(bf16[3,288,128]{2,1,0:T(8,128)(2,1)S(1)} %copy-done.101), channel_id=1, source_target_pairs={{64,0},{65,1},{66,2},{67,3},{68,4},{69,5},{70,6},{71,7},{72,8},{73... | collective-permute-start | bytes 663560 | tf_op jit(solution)/shard_map/ppermute | solution.py:74
  117.0 41.2 %collective-permute-start.69 = (bf16[8,288,128]{2,1,0:T(8,128)(2,1)}, bf16[8,288,128]{2,1,0:T(8,128)(2,1)}, u32[]{:S(2)}, u32[]{:S(2)}) collective-permute-start(bf16[8,288,128]{2,1,0:T(8,128)(2,1)} %constant_dynamic-update-slice_fusion.38.refs_4_), channel_id=1, source_target_pairs={{0,1},{1,2},{2,3},{3,0},{4,5},{5,6},{6,7},{7,4},{8,9},{9,10},{10,1... | collective-permute-start | bytes 1769480 | tf_op jit(solution)/shard_map/ppermute | solution.py:74
  119.5 39.6 %collective-permute-start.74 = (bf16[8,288,128]{2,1,0:T(8,128)(2,1)}, bf16[8,288,128]{2,1,0:T(8,128)(2,1)S(1)}, u32[]{:S(2)}, u32[]{:S(2)}) collective-permute-start(bf16[8,288,128]{2,1,0:T(8,128)(2,1)} %constant_dynamic-update-slice_fusion.38.refs_4_), channel_id=1, source_target_pairs={{0,32},{1,33},{2,34},{3,35},{4,36},{5,37},{6,38},{7,39},{8,40},{9,... | collective-permute-start | bytes 1769480 | tf_op jit(solution)/shard_map/ppermute | solution.py:74
  181.5 22.4 %collective-permute-start.78 = (bf16[16,288,128]{2,1,0:T(8,128)(2,1)S(1)}, bf16[16,288,128]{2,1,0:T(8,128)(2,1)S(1)}, u32[]{:S(2)}, u32[]{:S(2)}) collective-permute-start(bf16[16,288,128]{2,1,0:T(8,128)(2,1)S(1)} %constant_dynamic-update-slice_fusion.43.refs_8_), channel_id=1, source_target_pairs={{0,32},{1,33},{2,34},{3,35},{4,36},{5,37},{6,38},{7,39},{8,40},{9,... | collective-permute-start | bytes 3538952 | tf_op jit(solution)/shard_map/ppermute | solution.py:74
  183.7 24.1 %collective-permute-start.79 = (bf16[16,288,128]{2,1,0:T(8,128)(2,1)S(1)}, bf16[16,288,128]{2,1,0:T(8,128)(2,1)S(1)}, u32[]{:S(2)}, u32[]{:S(2)}) collective-permute-start(bf16[16,288,128]{2,1,0:T(8,128)(2,1)S(1)} %collective-permute-done.67.refs_9_), channel_id=1, source_target_pairs={{0,32},{1,33},{2,34},{3,35},{4,36},{5,37},{6,38},{7,39},{8,40},{9,... | collective-permute-start | bytes 3538952 | tf_op jit(solution)/shard_map/ppermute | solution.py:74
  203.1 36.4 %collective-permute-start.102 = (bf16[4,288,128]{2,1,0:T(8,128)(2,1)}, bf16[4,288,128]{2,1,0:T(8,128)(2,1)}, u32[]{:S(2)}, u32[]{:S(2)}) collective-permute-start(bf16[4,288,128]{2,1,0:T(8,128)(2,1)} %pad_maximum_fusion.16), channel_id=1, source_target_pairs={{0,8},{1,9},{2,10},{3,11},{4,12},{5,13},{6,14},{7,15},{8,16},{9,17... | collective-permute-start | bytes 884744 | tf_op jit(solution)/shard_map/ppermute | solution.py:74
  203.9 37.6 %collective-permute-start.95 = (bf16[8,288,128]{2,1,0:T(8,128)(2,1)}, bf16[8,288,128]{2,1,0:T(8,128)(2,1)}, u32[]{:S(2)}, u32[]{:S(2)}) collective-permute-start(bf16[8,288,128]{2,1,0:T(8,128)(2,1)} %constant_dynamic-update-slice_fusion.55.refs_4_), channel_id=1, source_target_pairs={{0,3},{1,0},{2,1},{3,2},{4,7},{5,4},{6,5},{7,6},{8,11},{9,8},{10,9... | collective-permute-start | bytes 1769480 | tf_op jit(solution)/shard_map/ppermute | solution.py:74
  204.0 40.1 %collective-permute-start.105 = (bf16[8,288,128]{2,1,0:T(8,128)(2,1)}, bf16[8,288,128]{2,1,0:T(8,128)(2,1)}, u32[]{:S(2)}, u32[]{:S(2)}) collective-permute-start(bf16[8,288,128]{2,1,0:T(8,128)(2,1)} %constant_dynamic-update-slice_fusion.55.refs_4_), channel_id=1, source_target_pairs={{0,1},{1,2},{2,3},{3,0},{4,5},{5,6},{6,7},{7,4},{8,9},{9,10},{10,1... | collective-permute-start | bytes 1769480 | tf_op jit(solution)/shard_map/ppermute | solution.py:74
  206.6 37.5 %collective-permute-start.110 = (bf16[8,288,128]{2,1,0:T(8,128)(2,1)}, bf16[8,288,128]{2,1,0:T(8,128)(2,1)}, u32[]{:S(2)}, u32[]{:S(2)}) collective-permute-start(bf16[8,288,128]{2,1,0:T(8,128)(2,1)} %constant_dynamic-update-slice_fusion.55.refs_4_), channel_id=1, source_target_pairs={{0,32},{1,33},{2,34},{3,35},{4,36},{5,37},{6,38},{7,39},{8,40},{9,... | collective-permute-start | bytes 1769480 | tf_op jit(solution)/shard_map/ppermute | solution.py:74
  207.8 36.3 %collective-permute-start.89 = (bf16[8,288,128]{2,1,0:T(8,128)(2,1)}, bf16[8,288,128]{2,1,0:T(8,128)(2,1)}, u32[]{:S(2)}, u32[]{:S(2)}) collective-permute-start(bf16[8,288,128]{2,1,0:T(8,128)(2,1)} %constant_dynamic-update-slice_fusion.50.refs_0_), channel_id=1, source_target_pairs={{0,24},{1,25},{2,26},{3,27},{4,28},{5,29},{6,30},{7,31},{8,0},{9,1... | collective-permute-start | bytes 1769480 | tf_op jit(solution)/shard_map/ppermute | solution.py:74
  248.7 28.4 %collective-permute-start.103 = (bf16[16,288,128]{2,1,0:T(8,128)(2,1)S(1)}, bf16[16,288,128]{2,1,0:T(8,128)(2,1)S(1)}, u32[]{:S(2)}, u32[]{:S(2)}) collective-permute-start(bf16[16,288,128]{2,1,0:T(8,128)(2,1)S(1)} %constant_dynamic-update-slice_fusion.60.refs_8_), channel_id=1, source_target_pairs={{0,4},{1,5},{2,6},{3,7},{4,0},{5,1},{6,2},{7,3},{8,12},{9,13},{10,... | collective-permute-start | bytes 3538952 | tf_op jit(solution)/shard_map/ppermute | solution.py:74
  258.2 37.4 %collective-permute-start.114 = (bf16[16,288,128]{2,1,0:T(8,128)(2,1)S(1)}, bf16[16,288,128]{2,1,0:T(8,128)(2,1)}, u32[]{:S(2)}, u32[]{:S(2)}) collective-permute-start(bf16[16,288,128]{2,1,0:T(8,128)(2,1)S(1)} %constant_dynamic-update-slice_fusion.60.refs_8_), channel_id=1, source_target_pairs={{0,32},{1,33},{2,34},{3,35},{4,36},{5,37},{6,38},{7,39},{8,40},{9,... | collective-permute-start | bytes 3538952 | tf_op jit(solution)/shard_map/ppermute | solution.py:74
  258.3 32.2 %collective-permute-start.82 = (bf16[256,1536]{1,0:T(8,128)(2,1)}, bf16[256,1536]{1,0:T(8,128)(2,1)}, u32[]{:S(2)}, u32[]{:S(2)}) collective-permute-start(bf16[256,1536]{1,0:T(8,128)(2,1)} %collective-permute-done.81), channel_id=1, source_target_pairs={{0,4},{1,5},{2,6},{3,7},{4,64},{5,65},{6,66},{7,67},{8,12},{9,13},... | collective-permute-start | bytes 2359304 | tf_op jit(solution)/shard_map/ppermute | solution.py:74
  259.5 30.9 %collective-permute-start.107 = (bf16[8,288,128]{2,1,0:T(8,128)(2,1)}, bf16[8,288,128]{2,1,0:T(8,128)(2,1)}, u32[]{:S(2)}, u32[]{:S(2)}) collective-permute-start(bf16[8,288,128]{2,1,0:T(8,128)(2,1)} %collective-permute-done.89.refs_1_), channel_id=1, source_target_pairs={{0,32},{1,33},{2,34},{3,35},{4,36},{5,37},{6,38},{7,39},{8,40},{9,... | collective-permute-start | bytes 1769480 | tf_op jit(solution)/shard_map/ppermute | solution.py:74
  277.1 28.0 %collective-permute-start.115 = (bf16[16,288,128]{2,1,0:T(8,128)(2,1)S(1)}, bf16[16,288,128]{2,1,0:T(8,128)(2,1)}, u32[]{:S(2)}, u32[]{:S(2)}) collective-permute-start(bf16[16,288,128]{2,1,0:T(8,128)(2,1)S(1)} %collective-permute-done.103.refs_9_), channel_id=1, source_target_pairs={{0,32},{1,33},{2,34},{3,35},{4,36},{5,37},{6,38},{7,39},{8,40},{9,... | collective-permute-start | bytes 3538952 | tf_op jit(solution)/shard_map/ppermute | solution.py:74
  290.4 48.1 %collective-permute-start.80 = (bf16[256,1536]{1,0:T(8,128)(2,1)}, bf16[256,1536]{1,0:T(8,128)(2,1)}, u32[]{:S(2)}, u32[]{:S(2)}) collective-permute-start(bf16[256,1536]{1,0:T(8,128)(2,1)} %copy-done.68), channel_id=1, source_target_pairs={{0,32},{1,33},{2,34},{3,35},{4,36},{5,37},{6,38},{7,39},{8,40},{9,... | collective-permute-start | bytes 2359304 | tf_op jit(solution)/shard_map/ppermute | solution.py:74
  290.5 48.0 %collective-permute-start.83 = (bf16[256,1536]{1,0:T(8,128)(2,1)}, bf16[256,1536]{1,0:T(8,128)(2,1)}, u32[]{:S(2)}, u32[]{:S(2)}) collective-permute-start(bf16[256,1536]{1,0:T(8,128)(2,1)} %collective-permute-done.82), channel_id=1, source_target_pairs={{0,32},{1,33},{2,34},{3,35},{4,36},{5,37},{6,38},{7,39},{8,40},{9,... | collective-permute-start | bytes 2359304 | tf_op jit(solution)/shard_map/ppermute | solution.py:74
  444.1 46.2 %all-to-all-start.1 = ((bf16[32,64,768]{2,1,0:T(8,128)(2,1)}), bf16[32,64,768]{2,1,0:T(8,128)(2,1)}, u32[]{:S(2)}, u32[]{:S(2)}) async-start(bf16[32,64,768]{2,1,0:T(8,128)(2,1)} %tile.8), calls=%async_computation.1 | async-start | bytes 6291456 | tf_op jit(solution)/shard_map/all_to_all | solution.py:116
  649.7 26.8 %collective-permute-start.120 = (f32[256,1536]{0,1:T(8,128)S(1)}, f32[256,1536]{0,1:T(8,128)S(1)}, u32[]{:S(2)}, u32[]{:S(2)}) collective-permute-start(f32[256,1536]{0,1:T(8,128)S(1)} %get-tuple-element.284), channel_id=1, source_target_pairs={{0,32},{1,33},{2,34},{3,35},{4,36},{5,37},{6,38},{7,39},{8,40},{9,... | collective-permute-start | bytes 4718600 | tf_op jit(solution)/shard_map/ppermute | solution.py:74
  651.5 37.5 %collective-permute-start.125 = (bf16[768,256]{1,0:T(8,128)(2,1)}, bf16[768,256]{1,0:T(8,128)(2,1)}, u32[]{:S(2)}, u32[]{:S(2)}) collective-permute-start(bf16[768,256]{1,0:T(8,128)(2,1)} %bitcast.62.refs_1_), channel_id=1, source_target_pairs={{0,32},{1,33},{2,34},{3,35},{4,36},{5,37},{6,38},{7,39},{8,40},{9,... | collective-permute-start | bytes 1179656 | tf_op jit(solution)/shard_map/ppermute | solution.py:74
  664.0 31.6 %collective-permute-start.127 = (bf16[3072,256]{1,0:T(8,128)(2,1)S(1)}, bf16[3072,256]{1,0:T(8,128)(2,1)}, u32[]{:S(2)}, u32[]{:S(2)}) collective-permute-start(bf16[3072,256]{1,0:T(8,128)(2,1)S(1)} %get-tuple-element.292.refs_3_), channel_id=1, source_target_pairs={{0,32},{1,33},{2,34},{3,35},{4,36},{5,37},{6,38},{7,39},{8,40},{9,... | collective-permute-start | bytes 4718600 | tf_op jit(solution)/shard_map/ppermute | solution.py:74
  665.6 30.0 %collective-permute-start.130 = (bf16[3072,256]{1,0:T(8,128)(2,1)S(1)}, bf16[3072,256]{1,0:T(8,128)(2,1)}, u32[]{:S(2)}, u32[]{:S(2)}) collective-permute-start(bf16[3072,256]{1,0:T(8,128)(2,1)S(1)} %get-tuple-element.291.refs_6_), channel_id=1, source_target_pairs={{0,32},{1,33},{2,34},{3,35},{4,36},{5,37},{6,38},{7,39},{8,40},{9,... | collective-permute-start | bytes 4718600 | tf_op jit(solution)/shard_map/ppermute | solution.py:74
  766.9 22.4 %collective-permute-start.132 = (f32[256,1536]{0,1:T(8,128)S(1)}, f32[256,1536]{0,1:T(8,128)S(1)}, u32[]{:S(2)}, u32[]{:S(2)}) collective-permute-start(f32[256,1536]{0,1:T(8,128)S(1)} %get-tuple-element.282), channel_id=1, source_target_pairs={{0,32},{1,33},{2,34},{3,35},{4,36},{5,37},{6,38},{7,39},{8,40},{9,... | collective-permute-start | bytes 4718600 | tf_op jit(solution)/shard_map/ppermute | solution.py:74
  801.4 42.7 %all-to-all-start.6 = ((bf16[32,64,768]{2,1,0:T(8,128)(2,1)}), bf16[32,64,768]{2,1,0:T(8,128)(2,1)S(1)}, u32[]{:S(2)}, u32[]{:S(2)}) async-start(bf16[32,64,768]{2,1,0:T(8,128)(2,1)} %bitcast.347), calls=%async_computation.6 | async-start | bytes 6291456 | tf_op jit(solution)/shard_map/all_to_all | solution.py:116
  855.6 27.8 %collective-permute-start.169 = (bf16[8,288,128]{2,1,0:T(8,128)(2,1)}, bf16[8,288,128]{2,1,0:T(8,128)(2,1)S(1)}, u32[]{:S(2)}, u32[]{:S(2)}) collective-permute-start(bf16[8,288,128]{2,1,0:T(8,128)(2,1)} %get-tuple-element.301), channel_id=1, source_target_pairs={{0,8},{1,9},{2,10},{3,11},{4,12},{5,13},{6,14},{7,15},{8,16},{9,17... | collective-permute-start | bytes 1769480 | tf_op jit(solution)/shard_map/ppermute | solution.py:74
  858.1 29.2 %collective-permute-start.176 = (bf16[8,288,128]{2,1,0:T(8,128)(2,1)}, bf16[8,288,128]{2,1,0:T(8,128)(2,1)S(1)}, u32[]{:S(2)}, u32[]{:S(2)}) collective-permute-start(bf16[8,288,128]{2,1,0:T(8,128)(2,1)} %get-tuple-element.303), channel_id=1, source_target_pairs={{0,1},{1,2},{2,3},{3,0},{4,5},{5,6},{6,7},{7,4},{8,9},{9,10},{10,1... | collective-permute-start | bytes 1769480 | tf_op jit(solution)/shard_map/ppermute | solution.py:74
  879.5 25.4 %collective-permute-start.178 = (bf16[8,288,128]{2,1,0:T(8,128)(2,1)}, bf16[8,288,128]{2,1,0:T(8,128)(2,1)}, u32[]{:S(2)}, u32[]{:S(2)}) collective-permute-start(bf16[8,288,128]{2,1,0:T(8,128)(2,1)} %get-tuple-element.304), channel_id=1, source_target_pairs={{0,3},{1,0},{2,1},{3,2},{4,7},{5,4},{6,5},{7,6},{8,11},{9,8},{10,9... | collective-permute-start | bytes 1769480 | tf_op jit(solution)/shard_map/ppermute | solution.py:74
  883.3 25.0 %collective-permute-start.183 = (bf16[16,288,128]{2,1,0:T(8,128)(2,1)}, bf16[16,288,128]{2,1,0:T(8,128)(2,1)}, u32[]{:S(2)}, u32[]{:S(2)}) collective-permute-start(bf16[16,288,128]{2,1,0:T(8,128)(2,1)} %slice.749), channel_id=1, source_target_pairs={{0,4},{1,5},{2,6},{3,7},{4,0},{5,1},{6,2},{7,3},{8,12},{9,13},{10,... | collective-permute-start | bytes 3538952 | tf_op jit(solution)/shard_map/ppermute | solution.py:74
  899.5 37.1 %collective-permute-start.140 = (bf16[768,256]{1,0:T(8,128)(2,1)}, bf16[768,256]{1,0:T(8,128)(2,1)S(1)}, u32[]{:S(2)}, u32[]{:S(2)}) collective-permute-start(bf16[768,256]{1,0:T(8,128)(2,1)} %bitcast.327), channel_id=1, source_target_pairs={{0,32},{1,33},{2,34},{3,35},{4,36},{5,37},{6,38},{7,39},{8,40},{9,... | collective-permute-start | bytes 1179656 | tf_op jit(solution)/shard_map/ppermute | solution.py:74
  900.9 55.5 %collective-permute-start.142 = (bf16[3072,256]{1,0:T(8,128)(2,1)S(1)}, bf16[3072,256]{1,0:T(8,128)(2,1)S(1)}, u32[]{:S(2)}, u32[]{:S(2)}) collective-permute-start(bf16[3072,256]{1,0:T(8,128)(2,1)S(1)} %get-tuple-element.290.refs_3_), channel_id=1, source_target_pairs={{0,32},{1,33},{2,34},{3,35},{4,36},{5,37},{6,38},{7,39},{8,40},{9,... | collective-permute-start | bytes 4718600 | tf_op jit(solution)/shard_map/ppermute | solution.py:74
  904.9 51.9 %collective-permute-start.145 = (bf16[3072,256]{1,0:T(8,128)(2,1)S(1)}, bf16[3072,256]{1,0:T(8,128)(2,1)S(1)}, u32[]{:S(2)}, u32[]{:S(2)}) collective-permute-start(bf16[3072,256]{1,0:T(8,128)(2,1)S(1)} %get-tuple-element.289.refs_6_), channel_id=1, source_target_pairs={{0,32},{1,33},{2,34},{3,35},{4,36},{5,37},{6,38},{7,39},{8,40},{9,... | collective-permute-start | bytes 4718600 | tf_op jit(solution)/shard_map/ppermute | solution.py:74
  956.5 27.7 %collective-permute-start.187 = (bf16[1,288,128]{2,1,0:T(8,128)(2,1)S(1)}, bf16[1,288,128]{2,1,0:T(8,128)(2,1)S(1)}, u32[]{:S(2)}, u32[]{:S(2)}) collective-permute-start(bf16[1,288,128]{2,1,0:T(8,128)(2,1)S(1)} %get-tuple-element.333), channel_id=1, source_target_pairs={{0,1},{1,2},{2,3},{3,0},{4,5},{5,6},{6,7},{7,4},{8,9},{9,10},{10,1... | collective-permute-start | bytes 221192 | tf_op jit(solution)/shard_map/ppermute | solution.py:74
  956.8 48.8 %collective-permute-start.189 = (bf16[1,288,128]{2,1,0:T(8,128)(2,1)}, bf16[1,288,128]{2,1,0:T(8,128)(2,1)}, u32[]{:S(2)}, u32[]{:S(2)}) collective-permute-start(bf16[1,288,128]{2,1,0:T(8,128)(2,1)} %get-tuple-element.334), channel_id=1, source_target_pairs={{0,3},{1,0},{2,1},{3,2},{4,7},{5,4},{6,5},{7,6},{8,11},{9,8},{10,9... | collective-permute-start | bytes 221192 | tf_op jit(solution)/shard_map/ppermute | solution.py:74
  987.2 36.9 %collective-permute-start.154 = (bf16[8,288,128]{2,1,0:T(8,128)(2,1)}, bf16[8,288,128]{2,1,0:T(8,128)(2,1)}, u32[]{:S(2)}, u32[]{:S(2)}) collective-permute-start(bf16[8,288,128]{2,1,0:T(8,128)(2,1)} %get-tuple-element.299), channel_id=1, source_target_pairs={{0,1},{1,2},{2,3},{3,0},{4,5},{5,6},{6,7},{7,4},{8,9},{9,10},{10,1... | collective-permute-start | bytes 1769480 | tf_op jit(solution)/shard_map/ppermute | solution.py:74
  1000.8 35.9 %collective-permute-start.149 = (bf16[8,288,128]{2,1,0:T(8,128)(2,1)}, bf16[8,288,128]{2,1,0:T(8,128)(2,1)}, u32[]{:S(2)}, u32[]{:S(2)}) collective-permute-start(bf16[8,288,128]{2,1,0:T(8,128)(2,1)} %get-tuple-element.298), channel_id=1, source_target_pairs={{0,24},{1,25},{2,26},{3,27},{4,28},{5,29},{6,30},{7,31},{8,0},{9,1... | collective-permute-start | bytes 1769480 | tf_op jit(solution)/shard_map/ppermute | solution.py:74
  1004.3 32.4 %collective-permute-start.148 = (bf16[8,288,128]{2,1,0:T(8,128)(2,1)}, bf16[8,288,128]{2,1,0:T(8,128)(2,1)}, u32[]{:S(2)}, u32[]{:S(2)}) collective-permute-start(bf16[8,288,128]{2,1,0:T(8,128)(2,1)} %add_convert_fusion.3), channel_id=1, source_target_pairs={{0,8},{1,9},{2,10},{3,11},{4,12},{5,13},{6,14},{7,15},{8,16},{9,17... | collective-permute-start | bytes 1769480 | tf_op jit(solution)/shard_map/ppermute | solution.py:74
  1022.8 34.4 %collective-permute-start.161 = (bf16[16,288,128]{2,1,0:T(8,128)(2,1)}, bf16[16,288,128]{2,1,0:T(8,128)(2,1)}, u32[]{:S(2)}, u32[]{:S(2)}) collective-permute-start(bf16[16,288,128]{2,1,0:T(8,128)(2,1)} %slice.719), channel_id=1, source_target_pairs={{0,4},{1,5},{2,6},{3,7},{4,0},{5,1},{6,2},{7,3},{8,12},{9,13},{10,... | collective-permute-start | bytes 3538952 | tf_op jit(solution)/shard_map/ppermute | solution.py:74
  1029.6 78.3 %all-to-all-start.7 = ((f32[32,8,768]{2,1,0:T(8,128)}), f32[32,8,768]{2,1,0:T(8,128)}, u32[]{:S(2)}, u32[]{:S(2)}) async-start(f32[32,8,768]{2,1,0:T(8,128)} %bitcast.99), calls=%async_computation.7 | async-start | bytes 1572864 | tf_op jit(solution)/shard_map/all_to_all | solution.py:116
  1038.6 22.5 %collective-permute-start.150 = (bf16[2,288,128]{2,1,0:T(8,128)(2,1)S(1)}, bf16[2,288,128]{2,1,0:T(8,128)(2,1)S(1)}, u32[]{:S(2)}, u32[]{:S(2)}) collective-permute-start(bf16[2,288,128]{2,1,0:T(8,128)(2,1)S(1)} %get-tuple-element.321), channel_id=1, source_target_pairs={{0,1},{1,2},{2,3},{3,0},{4,5},{5,6},{6,7},{7,4},{8,9},{9,10},{10,1... | collective-permute-start | bytes 442376 | tf_op jit(solution)/shard_map/ppermute | solution.py:74
  1041.1 25.9 %collective-permute-start.152 = (bf16[2,288,128]{2,1,0:T(8,128)(2,1)S(1)}, bf16[2,288,128]{2,1,0:T(8,128)(2,1)S(1)}, u32[]{:S(2)}, u32[]{:S(2)}) collective-permute-start(bf16[2,288,128]{2,1,0:T(8,128)(2,1)S(1)} %get-tuple-element.322), channel_id=1, source_target_pairs={{0,3},{1,0},{2,1},{3,2},{4,7},{5,4},{6,5},{7,6},{8,11},{9,8},{10,9... | collective-permute-start | bytes 442376 | tf_op jit(solution)/shard_map/ppermute | solution.py:74
  1045.3 29.4 %collective-permute-start.159 = (bf16[2,288,128]{2,1,0:T(8,128)(2,1)S(1)}, bf16[2,288,128]{2,1,0:T(8,128)(2,1)S(1)}, u32[]{:S(2)}, u32[]{:S(2)}) collective-permute-start(bf16[2,288,128]{2,1,0:T(8,128)(2,1)S(1)} %get-tuple-element.324), channel_id=1, source_target_pairs={{0,24},{1,25},{2,26},{3,27},{4,28},{5,29},{6,30},{7,31},{8,0},{9,1... | collective-permute-start | bytes 442376 | tf_op jit(solution)/shard_map/ppermute | solution.py:74
  1061.1 37.3 %collective-permute-start.136 = (f32[1664,384]{1,0:T(8,128)S(1)}, f32[1664,384]{1,0:T(8,128)S(1)}, u32[]{:S(2)}, u32[]{:S(2)}) collective-permute-start(f32[1664,384]{1,0:T(8,128)S(1)} %slice_select_fusion), channel_id=1, source_target_pairs={{0,32},{1,33},{2,34},{3,35},{4,36},{5,37},{6,38},{7,39},{8,40},{9,... | collective-permute-start | bytes 7667720 | tf_op jit(solution)/shard_map/ppermute | solution.py:74
  1074.8 37.0 %collective-permute-start.190 = (f32[3,288,128]{2,1,0:T(8,128)}, f32[3,288,128]{2,1,0:T(8,128)}, u32[]{:S(2)}, u32[]{:S(2)}) collective-permute-start(f32[3,288,128]{2,1,0:T(8,128)} %pad_maximum_fusion.12), channel_id=1, source_target_pairs={{0,64},{1,65},{2,66},{3,67},{4,68},{5,69},{6,70},{7,71},{8,72},{9,... | collective-permute-start | bytes 1327112 | tf_op jit(solution)/shard_map/ppermute | solution.py:74
  1151.3 33.9 %all-to-all-start.9 = ((f32[32,8,768]{2,1,0:T(8,128)}), f32[32,8,768]{2,1,0:T(8,128)}, u32[]{:S(2)}, u32[]{:S(2)}) async-start(f32[32,8,768]{2,1,0:T(8,128)} %tile.11), calls=%async_computation.9 | async-start | bytes 1572864 | tf_op jit(solution)/shard_map/all_to_all | solution.py:116
  (352 other events, 3934.9 us)

commit v3 on v2

--- a/solution.py
+++ b/solution.py
@@ -12,7 +12,6 @@
 LAYERS = 2
 BS = 192
 STEP = 10
-PACK = 288
 LANES = 128
 HALF = 96
 SLOTS = 64
@@ -96,189 +95,96 @@
     return value.astype(F32)
 
 
-def reduce4(parts, axis, kind):
-    first = turn(parts[2].astype(kind), axis, 1)
-    onward = (wide(parts[1]) + wide(first)).astype(kind)
-    near = turn(onward, axis, 1)
-    other = turn(parts[3].astype(kind), axis, -1)
-    return wide(parts[0]) + wide(near) + wide(other)
-
-
-def sum_everywhere(value):
-    shape, share = value.shape, value.size // len(COORDS)
-    parts = exchanged(value.reshape(len(COORDS), share), ("seq", "dp"))
-    total = jnp.sum(parts, axis=0, keepdims=True)
-    spread = jnp.broadcast_to(total, (len(COORDS), share))
-    return exchanged(spread, ("seq", "dp")).reshape(shape)
-
-
 def exchanged(value, axes):
     return lax.all_to_all(value, axes, 0, 0, tiled=True)
 
 
-def pack_blocks(blocks, odd):
-    odd = odd[:, None, None]
-    main = jnp.where(odd, blocks[:, :, BS - LANES :], blocks[:, :, :LANES])
-    half = jnp.where(odd, blocks[:, :, : BS - LANES], blocks[:, :, LANES:])
-    top, low = half[:, :HALF], half[:, HALF:]
-    rest = jnp.concatenate([jnp.where(odd, low, top), jnp.where(odd, top, low)], axis=2)
-    return jnp.concatenate([main, rest], axis=1)
-
-
-def unpack_blocks(packed):
-    main, rest = packed[:, :BS], packed[:, BS:]
-    half = jnp.concatenate([rest[:, :, : LANES // 2], rest[:, :, LANES // 2 :]], axis=1)
-    return jnp.concatenate([main, half], axis=2)
-
-
-def pieces_of(chunk):
-    return (("y", 8, 4), ("x", 8, 4), ("zl", 16, 2))[chunk]
-
-
-def inner_moves(chunk):
-    if chunk == 0:
-        return [(my, kz, mx) for my in range(4) for mx in range(4) for kz in range(2)]
-    if chunk == 1:
-        return [(my, kz, mx) for mx in range(4) for my in range(4) for kz in range(2)]
-    return [(my, kz, mx) for kz in range(2) for my in range(4) for mx in range(4)]
+def joined(*parts):
+    return jnp.concatenate(parts, axis=0)
 
 
 MATRICES = ((0, 4, 12), (48, 4, 4), (64, 4, 16), (128, 16, 4))
-
-
-def assemble_kernel(places, *refs):
-    arrays, outs, (halves, sems) = refs[:20], refs[20:24], refs[24:]
-    at = 0
-    for array in arrays:
-
-        def fetch(q, carry, array=array, at=at):
-            tile = places[at + q]
-            pltpu.make_async_copy(array.at[q, pl.ds(BS, HALF)], halves.at[tile], sems.at[4]).start()
-            for which, out in enumerate(outs):
-                base, tall, across = MATRICES[which]
-
-                @pl.when((tile >= base) & (tile < base + tall * across))
-                def _(out=out, base=base, across=across, which=which):
-                    row, col = (tile - base) // across, (tile - base) % across
-                    left = pl.multiple_of((col // 2) * 2 * BS + (col % 2) * 2 * LANES, LANES)
-                    target = out.at[pl.ds(pl.multiple_of(row * BS, HALF), BS), pl.ds(left, LANES)]
-                    pltpu.make_async_copy(array.at[q, pl.ds(0, BS)], target, sems.at[which]).start()
-
+SHAPES = [(tall * BS, across * BS) for _, tall, across in MATRICES]
+
+
+def tile_places(tiles):
+    matrix = sum((tiles >= base).astype(jnp.int32) for base, _, _ in MATRICES[1:])
+    offset = tiles - jnp.take(jnp.array([m[0] for m in MATRICES]), matrix)
+    across = jnp.take(jnp.array([m[2] for m in MATRICES]), matrix)
+    odd = tiles % 2
+    column = BS * (offset % across) - odd * (LANES // 2)
+    return jnp.stack([matrix, BS * (offset // across), column, odd]).astype(jnp.int32)
+
+
+def spread_kernel(places, tiles, *outs):
+    for out in outs:
+
+        def clear(at, carry, out=out):
+            out[pl.ds(pl.multiple_of(at * HALF, HALF), HALF)] = jnp.zeros((HALF, out.shape[1]), BF)
             return carry
 
-        lax.fori_loop(0, array.shape[0], fetch, 0)
-        at += array.shape[0]
-    pltpu.make_async_copy(halves, halves, sems.at[4]).wait()
-    for which, out in enumerate(outs):
-        most = out.at[:, pl.ds(0, 2 * out.shape[1] // 3)]
-        pltpu.make_async_copy(most, most, sems.at[which]).wait()
-    left_lanes = lax.broadcasted_iota(jnp.int32, (HALF, LANES), 1) < LANES // 2
-    for out, (base, tall, across) in zip(outs, MATRICES, strict=True):
-        pairs = across // 2
-
-        def place(t, carry, out=out, base=base, pairs=pairs):
-            row = pl.multiple_of((t // pairs) * BS, HALF)
-            col = pl.multiple_of((t % pairs) * 2 * BS + LANES, LANES)
-            he, ho = wide(halves[base + 2 * t]), wide(halves[base + 2 * t + 1])
-            out[pl.ds(row, HALF), pl.ds(col, LANES)] = jnp.where(left_lanes, he, ho).astype(BF)
-            out[pl.ds(row + HALF, HALF), pl.ds(col, LANES)] = pltpu.roll(
-                jnp.where(left_lanes, ho, he), LANES // 2, 1
-            ).astype(BF)
-            return carry
-
-        lax.fori_loop(0, tall * pairs, place, 0, unroll=2)
-
-
-def assemble_layer(places, arrays):
-    shapes = [jax.ShapeDtypeStruct((t * BS, a * BS), BF) for _, t, a in MATRICES]
+        lax.fori_loop(0, out.shape[0] // HALF, clear, 0)
+    for k in range(3):
+        for which, out in enumerate(outs):
+
+            @pl.when(places[0, k] == which)
+            def _(out=out, k=k):
+                row = pl.ds(pl.multiple_of(places[1, k], 64), BS)
+                col = pl.ds(pl.multiple_of(places[2, k], LANES), 2 * LANES)
+                value = tiles[k]
+                value = jnp.where(places[3, k] == 1, pltpu.roll(value, LANES // 2, 1), value)
+                out[row, col] = (wide(out[row, col]) + value).astype(BF)
+
+
+def spread_tiles(places, tiles):
     return pl.pallas_call(
-        assemble_kernel,
+        spread_kernel,
         grid_spec=pltpu.PrefetchScalarGridSpec(
             num_scalar_prefetch=1,
             grid=(),
-            in_specs=[pl.BlockSpec(memory_space=pl.ANY)] * len(arrays),
+            in_specs=[pl.BlockSpec(memory_space=pltpu.VMEM)],
             out_specs=[pl.BlockSpec(memory_space=pltpu.VMEM)] * 4,
-            scratch_shapes=[pltpu.VMEM((BS, HALF, LANES), BF), pltpu.SemaphoreType.DMA((5,))],
         ),
-        out_shape=shapes,
-        compiler_params=pltpu.CompilerParams(vmem_limit_bytes=40 * 1024 * 1024),
-        cost_estimate=pl.CostEstimate(flops=0, bytes_accessed=29_000_000, transcendentals=0),
-        name="assemble",
-    )(places, *arrays)
-
-
-LEFT_ROWS = (768, 768, 768, 3072)
-RIGHT_ROWS = (2304, 768, 3072, 768)
-
-
-def tile_rows(tiles):
-    matrix = sum((tiles >= base).astype(jnp.int32) for base, _, _ in MATRICES[1:])
-    offset = tiles - jnp.take(jnp.array([m[0] for m in MATRICES]), matrix)
-    across = jnp.take(jnp.array([m[2] for m in MATRICES]), matrix)
-    left_base = jnp.take(jnp.array([0, 768, 1536, 2304]), matrix)
-    right_base = jnp.take(jnp.array([0, 2304, 3072, 6144]), matrix)
-    return jnp.stack(
-        [left_base + BS * (offset // across), right_base + BS * (offset % across)]
-    ).astype(jnp.int32)
-
-
-def weight_grad_kernel(rows, *refs):
-    sources, outs, (lefts, rights, sems) = refs[:16], refs[16:19], refs[19:]
-    for part in range(2):
-        for stack, sizes, first in ((lefts, LEFT_ROWS, 0), (rights, RIGHT_ROWS, 4)):
-            at = 0
-            for index, size in enumerate(sizes):
-                pltpu.make_async_copy(
-                    sources[8 * part + first + index],
-                    stack.at[pl.ds(at, size), pl.ds(256 * part, 256)],
-                    sems.at[first // 4],
-                ).start()
-                at += size
-    rights[pl.ds(sum(RIGHT_ROWS), 64)] = jnp.zeros((64, 512), BF)
-    pltpu.make_async_copy(lefts, lefts, sems.at[0]).wait()
-    filled = rights.at[pl.ds(0, sum(RIGHT_ROWS))]
-    pltpu.make_async_copy(filled, filled, sems.at[1]).wait()
-    left_lanes = lax.broadcasted_iota(jnp.int32, (HALF, LANES), 1) < LANES // 2
-    for chunk, out in enumerate(outs):
-
-        def tile(q, carry, chunk=chunk, out=out):
-            left = lefts[pl.ds(pl.multiple_of(rows[0, 32 * chunk + q], 64), BS)]
-            right = rights[pl.ds(pl.multiple_of(rows[1, 32 * chunk + q], 64), 256)]
-            value = lax.dot_general(
-                left, right, (((1,), (1,)), ((), ())), preferred_element_type=F32
-            )
-            out[q, :BS] = value[:, :LANES].astype(BF)
-            rest = value[:, LANES:]
-            low = pltpu.roll(rest[HALF:], LANES // 2, 1)
-            out[q, BS:] = jnp.where(left_lanes, rest[:HALF], low).astype(BF)
-            return carry
-
-        lax.fori_loop(0, 32, tile, 0, unroll=2)
-
-
-def weight_grads(tiles, lefts, rights):
-    own = [value.T for value in (*lefts, *rights)]
-    other = [swap(value, "c") for value in own]
+        out_shape=[jax.ShapeDtypeStruct(shape, BF) for shape in SHAPES],
+        compiler_params=pltpu.CompilerParams(vmem_limit_bytes=32 * 1024 * 1024),
+        cost_estimate=pl.CostEstimate(flops=0, bytes_accessed=15_000_000, transcendentals=0),
+        name="spread_tiles",
+    )(places, tiles)
+
+
+def cut_kernel(places, *refs):
+    matrices, out, (held, sem) = refs[:8], refs[8], refs[9:]
+    for k in range(3):
+        for which, matrix in enumerate(matrices):
+
+            @pl.when(places[0, k] == which)
+            def _(matrix=matrix, k=k):
+                row = pl.ds(pl.multiple_of(places[1, k], 64), BS)
+                col = pl.ds(pl.multiple_of(places[2, k], LANES), 2 * LANES)
+                pltpu.make_async_copy(matrix.at[row, col], held.at[k], sem).start()
+
+    pltpu.make_async_copy(held, held, sem).wait()
+    for k in range(3):
+        value = held[k]
+        value = jnp.where(places[3, k] == 1, pltpu.roll(value, 2 * LANES - LANES // 2, 1), value)
+        out[k] = value[:, :BS]
+
+
+def cut_tiles(places, matrices):
     return pl.pallas_call(
-        weight_grad_kernel,
+        cut_kernel,
         grid_spec=pltpu.PrefetchScalarGridSpec(
             num_scalar_prefetch=1,
             grid=(),
-            in_specs=[pl.BlockSpec(memory_space=pl.ANY)] * 16,
-            out_specs=[pl.BlockSpec(memory_space=pltpu.VMEM)] * 3,
-            scratch_shapes=[
-                pltpu.VMEM((sum(LEFT_ROWS), 512), BF),
-                pltpu.VMEM((sum(RIGHT_ROWS) + 64, 512), BF),
-                pltpu.SemaphoreType.DMA((2,)),
-            ],
+            in_specs=[pl.BlockSpec(memory_space=pl.ANY)] * 8,
+            out_specs=pl.BlockSpec(memory_space=pltpu.VMEM),
+            scratch_shapes=[pltpu.VMEM((3, BS, 2 * LANES), F32), pltpu.SemaphoreType.DMA],
         ),
-        out_shape=[jax.ShapeDtypeStruct((32, PACK, LANES), BF)] * 3,
-        compiler_params=pltpu.CompilerParams(vmem_limit_bytes=40 * 1024 * 1024),
-        cost_estimate=pl.CostEstimate(
-            flops=2 * 512 * 96 * BS * BS, bytes_accessed=20_000_000, transcendentals=0
-        ),
-        name="weight_grads",
-    )(tile_rows(tiles), *own, *other)
+        out_shape=jax.ShapeDtypeStruct((3, BS, BS), F32),
+        compiler_params=pltpu.CompilerParams(vmem_limit_bytes=16 * 1024 * 1024),
+        cost_estimate=pl.CostEstimate(flops=0, bytes_accessed=1_000_000, transcendentals=0),
+        name="cut_tiles",
+    )(places, *matrices)
 
 
 def lookup_kernel(ids, table, out0, out1, out2, out3):
@@ -475,27 +381,17 @@
     return expo / jnp.sum(expo, axis=-1, keepdims=True)
 
 
-def gather_pairs(own):
-    core = swap(own, "c")
-    far = z_flip(own)
-    return jnp.concatenate([own, core, far, swap(far, "c")], axis=0)
-
-
-def reduce_pairs(grad):
-    span = grad.shape[0] // 4
-    own, core, far, both = (grad[m * span : (m + 1) * span] for m in range(4))
-    far = (far + swap(both, "c")).astype(BF)
-    own = own + swap(core, "c")
-    return own + wide(z_flip(far))
-
-
 def layer_forward(residual, mats, params, doc_mask):
     w_qkv, w_proj, w_fc, w_out = mats
     gain_a, gain_b, shift_a, shift_b, bias_qkv, bias_proj, bias_fc, bias_out = params
     model_width = residual.shape[1]
     normed = layer_norm(residual, gain_a, shift_a).astype(BF)
     qkv_bf = (product(normed, w_qkv) + bias_qkv).astype(BF)
-    key_values = gather_pairs(qkv_bf[:, model_width:])
+    own_pairs = qkv_bf[:, model_width:]
+    core_pairs = swap(own_pairs, "c")
+    far_pairs = z_flip(own_pairs)
+    both_pairs = swap(far_pairs, "c")
+    key_values = jnp.concatenate([own_pairs, core_pairs, far_pairs, both_pairs], axis=0)
     soft_probs = attend(qkv_bf[:, :model_width], key_values, doc_mask)
     value_heads = key_values[:, model_width:].reshape(-1, HEADS, HEAD_DIM)
     attended = jnp.einsum(
@@ -509,12 +405,14 @@
     result = middle + product(activated, w_out) + bias_out
     return (
         result,
-        (residual, qkv_bf, key_values, attended, middle, normed_b, inner_pre, activated),
-    )
-
-
-def layer_backward(grad_in, kept_values, mats, params, doc_mask):
-    residual, qkv_bf, key_values, attended, middle, normed_b, inner_pre, activated = kept_values
+        (residual, normed, qkv_bf, key_values, attended, middle, normed_b, inner_pre, activated),
+    )
+
+
+def layer_backward(grad_in, kept_values, mats, params, doc_mask, earlier):
+    residual, normed, qkv_bf, key_values, attended, middle, normed_b, inner_pre, activated = (
+        kept_values
+    )
     w_qkv, w_proj, w_fc, w_out = mats
     gain_a, gain_b, shift_a, shift_b = params[:4]
     model_width = residual.shape[1]
@@ -523,12 +421,18 @@
     _, gelu_back = jax.vjp(lambda inner_in: jax.nn.gelu(inner_in, approximate=True), inner_pre)
     grad_inner = gelu_back(product_nt(grad_out, w_out))[0].astype(BF)
     b_fc = jnp.sum(wide(grad_inner), axis=0)
+    early = product_tn(normed_b, grad_inner), product_tn(activated, grad_out)
+    grad_inner, early = lax.optimization_barrier((grad_inner, early))
+    if earlier is not None:
+        early, first_earlier = lax.optimization_barrier((early, earlier[0]))
+    early = lax.psum(early, ("seq", "dp"))
     _, norm_back_b = jax.vjp(layer_norm, middle, gain_b, shift_b)
     grad_mid, g_gain_b, g_shift_b = norm_back_b(product_nt(grad_inner, w_fc))
     grad_mid = grad_mid + grad_in
     grad_branch = grad_mid.astype(BF)
     b_proj = jnp.sum(wide(grad_branch), axis=0)
     grad_att = product_nt(grad_branch, w_proj).astype(BF)
+    d_proj = product_tn(attended, grad_branch)
     soft_probs = attend(qkv_bf[:, :model_width], key_values, doc_mask)
     seq_len = key_values.shape[0]
     queries = qkv_bf[:, :model_width].reshape(-1, HEADS, HEAD_DIM)
@@ -553,12 +457,24 @@
     grad_values = jnp.einsum(
         "hqk,qhd->khd", soft_probs.astype(BF), grad_heads, preferred_element_type=F32
     ).reshape(seq_len, model_width)
-    grad_pairs = reduce_pairs(jnp.concatenate([grad_keys, grad_values], axis=1))
+    if earlier is not None:
+        grad_query, first_earlier = lax.optimization_barrier((grad_query, first_earlier))
+    grad_pairs = jnp.concatenate([grad_keys, grad_values], axis=1)
+    own, core, far, both = jnp.split(grad_pairs, 4, axis=0)
+    far = far + swap(both, "c")
+    own = own + swap(core, "c")
+    grad_pairs = own + wide(z_flip(far.astype(BF)))
     grad_mixed = jnp.concatenate([grad_query, grad_pairs], axis=1).astype(BF)
-    normed_a, norm_back_a = jax.vjp(layer_norm, residual, gain_a, shift_a)
+    late = product_tn(normed, grad_mixed), d_proj
+    _, norm_back_a = jax.vjp(layer_norm, residual, gain_a, shift_a)
     mixed_sums = jnp.sum(wide(grad_mixed), axis=0)
     grad_resid, g_gain_a, g_shift_a = norm_back_a(product_nt(grad_mixed, w_qkv))
     grad_resid = grad_resid + grad_mid
+    grad_resid, late = lax.optimization_barrier((grad_resid, late))
+    if earlier is not None:
+        late, second_earlier, grad_resid = lax.optimization_barrier((late, earlier[1], grad_resid))
+        earlier = first_earlier, second_earlier
+    late = lax.psum(late, ("dp", "seq"))
     bias_rows = jnp.concatenate(
         [
             jnp.stack([mixed_sums[:model_width], mixed_sums[2 * model_width :], b_proj]),
@@ -569,10 +485,8 @@
     )
     return (
         grad_resid,
-        (
-            (normed_a.astype(BF), attended, normed_b, activated),
-            (grad_mixed, grad_branch, grad_inner, grad_out),
-        ),
+        (early, late),
+        earlier,
         (g_gain_a, g_gain_b, g_shift_a, g_shift_b, bias_rows),
     )
 
@@ -591,44 +505,6 @@
 
 def squared_blocks(flat):
     return flat.reshape(-1, BS, BS)
-
-
-def gather_weights(packed, layer_idx, z_hi):
-    from_there = permuted(packed, "zh", None, keep=lambda zh, c, y, zl, x: zh == layer_idx)
-    mine = jnp.where(z_hi == layer_idx, packed, from_there)
-    arrays = []
-    for chunk in range(3):
-        value = mine[chunk : chunk + 1]
-        if chunk < 2:
-            value = jnp.concatenate([value, swap(value, "zl")], axis=0)
-            first, last = (("x", "y"), ("y", "x"))[chunk]
-            value = jnp.concatenate(gather4(value, first), axis=0)
-            arrays += gather4(value, last)
-        else:
-            value = jnp.concatenate(gather4(value, "x"), axis=0)
-            value = jnp.concatenate(gather4(value, "y"), axis=0)
-            arrays += [value, swap(value, "zl")]
-    return arrays + [swap(value, "c") for value in arrays]
-
-
-def reduce_weights(arrays, layer_idx, z_hi):
-    blocks = []
-    for chunk in range(3):
-        axis, size, count = pieces_of(chunk)
-        parts = [arrays[chunk][p * size : (p + 1) * size] for p in range(count)]
-        if chunk < 2:
-            value = reduce4(parts, axis, BF)
-            other = "x" if axis == "y" else "y"
-            value = reduce4([value[2 * m : 2 * m + 2] for m in range(4)], other, BF)
-            value = value[:1] + wide(swap(value[1:].astype(BF), "zl"))
-        else:
-            value = wide(parts[0]) + wide(swap(parts[1], "zl"))
-            value = reduce4([value[4 * m : 4 * m + 4] for m in range(4)], "y", BF)
-            value = reduce4([value[m : m + 1] for m in range(4)], "x", BF)
-        blocks.append(value)
-    value = jnp.concatenate(blocks, axis=0)
-    from_there = permuted(value, "zh", None, keep=lambda zh, c, y, zl, x: zh != layer_idx)
-    return value + from_there
 
 
 def shards(
@@ -664,32 +540,39 @@
     table_rows = vocab_table.shape[0]
     padded = -(-table_rows // 64) * 64
     vocab_start = row_at * 2 * table_rows
-    shift_up, shift_down = jnp.array([0, 1, 2, 3]), jnp.array([0, 3, 2, 1])
-    own_shift = jnp.where(core == 0, shift_up, shift_down)
-    other_shift = jnp.where(core == 0, shift_down, shift_up)
-
-    places = []
-    for layer_idx in range(LAYERS):
-        slots = []
-        for kc in range(2):
-            shift = own_shift if kc == 0 else other_shift
-            for chunk in range(3):
-                moves = jnp.array(inner_moves(chunk))
-                at_y = (y_at + shift[moves[:, 0]]) % 4
-                at_z = zl_at ^ moves[:, 1]
-                at_x = (x_at + shift[moves[:, 2]]) % 4
-                slots.append(((((core ^ kc) * 4 + at_y) * 2 + at_z) * 4 + at_x) * 3 + chunk)
-        places.append(jnp.take(owners[layer_idx], jnp.concatenate(slots), axis=0))
+    own_shift = jnp.where(core == 0, jnp.array([0, 1, 2, 3]), jnp.array([0, 3, 2, 1]))
+
     own_slots = (core * 32 + row_at) * 3 + jnp.arange(3)
     own_tiles = jnp.take(
         jnp.where(z_hi == 0, owners[0], owners[1]), own_slots, axis=0
     )
-    own_odd = own_tiles % 2 == 1
+    own_places = tile_places(own_tiles)
+
+    own_weights = jnp.pad(squared_blocks(weights), ((0, 0), (0, 0), (0, 2 * LANES - BS)))
+    layer_weights = []
+    for layer_idx in range(LAYERS):
+        here = jnp.where(z_hi == layer_idx, own_places[0], -1)
+        matrices = spread_tiles(own_places.at[0].set(here), own_weights.astype(BF).astype(F32))
+        if layer_idx:
+            matrices, layer_weights[-1] = lax.optimization_barrier((matrices, layer_weights[-1]))
+        layer_weights.append(lax.psum(matrices, ("seq", "dp")))
+
+    sequences = token_ids.shape[0]
+    shard_of = token_ids // (2 * table_rows)
+    held_by = (shard_of[:, None, :] == jnp.arange(sequences)[None, :, None]).astype(BF)
+    before = (jnp.arange(span_len)[:, None] <= jnp.arange(span_len)[None, :]).astype(BF)
+    ranks = product(held_by.reshape(-1, span_len), before).reshape(held_by.shape).astype(jnp.int32) - 1
+    crowds = jnp.sum((ranks[:, :, -1] >= SLOTS).astype(F32))
+    counts = jnp.stack([crowds, jnp.sum((pick_slots >= 0).astype(F32))])
+    counts = jnp.broadcast_to(counts[:, None], (2, LANES))
 
     own_part = jnp.pad(vocab_table.astype(BF), ((0, padded - table_rows), (0, 0)))
-    far_part = z_flip(own_part)
+    near_part, far_part = swap(own_part, "c"), z_flip(own_part)
+    counts = counts + swap(counts, "c")
+    counts = counts + swap(counts, "zh")
+    crowded, pick_count = counts[0, 0] > 0.0, counts[1, 0]
     both_parts = jnp.stack([own_part, far_part])
-    near_parts = jnp.stack([swap(own_part, "c"), swap(far_part, "c")])
+    near_parts = jnp.stack([near_part, swap(far_part, "c")])
     table_bf = jnp.where(
         core == 0,
         jnp.concatenate([both_parts, near_parts], axis=2),
@@ -703,25 +586,8 @@
         inside = (offset >= 0) & (offset < 2 * table_rows)
         return jnp.where(inside, ((offset % 2) ^ z_hi) * padded + offset // 2, -1)
 
-    packed = pack_blocks(squared_blocks(weights).astype(BF), own_odd)
-    layer_weights = []
-    for layer_idx in range(LAYERS):
-        arrays = gather_weights(packed, layer_idx, z_hi)
-        packed, arrays[2], arrays[6], arrays[9] = lax.optimization_barrier(
-            (packed, arrays[2], arrays[6], arrays[9])
-        )
-        layer_weights.append(assemble_layer(places[layer_idx], arrays))
     all_params = [layer_params(small_params, layer_idx) for layer_idx in range(LAYERS)]
 
-    sequences = token_ids.shape[0]
-    shard_of = token_ids // (2 * table_rows)
-    held_by = (shard_of[:, None, :] == jnp.arange(sequences)[None, :, None]).astype(BF)
-    before = (jnp.arange(span_len)[:, None] <= jnp.arange(span_len)[None, :]).astype(BF)
-    ranks = product(held_by.reshape(-1, span_len), before).reshape(held_by.shape).astype(jnp.int32) - 1
-    crowded = jnp.max(ranks[:, :, -1]) >= SLOTS
-    crowded = jnp.broadcast_to(crowded.astype(F32), (8, LANES))
-    crowded = jnp.maximum(crowded, swap(crowded, "c"))
-    crowded = jnp.maximum(crowded, swap(crowded, "zh"))[0, 0] > 0.0
     all_rows = local_row(token_ids)
     own_ranks = lax.dynamic_index_in_dim(ranks, row_at, 1, keepdims=False)
     slots = jnp.arange(SLOTS)
@@ -806,7 +672,6 @@
     log_total = top + jnp.log(jnp.sum(stats[:, 1] * jnp.exp(stats[:, 0] - top[None]), axis=0))
     losses = jnp.where(valid_all, log_total - jnp.sum(stats[:, 2], axis=0), 0.0)
     loss_own = jnp.sum(lax.dynamic_slice_in_dim(losses, row_at * pick_dev, pick_dev))
-    count_own = jnp.sum(own_valid.astype(F32))
     grad_logits = jnp.where(
         valid_all[:, None], jnp.exp(logits - log_total[:, None]) - hits.astype(F32), 0.0
     ).astype(BF)
@@ -820,82 +685,118 @@
     )
     grad_resid, g_final_gain, g_final_shift = final_back(grad_final)
 
-    own_parts = [None] * LAYERS
+    summed = None
+    layer_grads = []
     small_parts = [None] * LAYERS
     for layer_idx in reversed(range(LAYERS)):
-        grad_resid, (lefts, rights), small_part = layer_backward(
+        grad_resid, matrix_grads, earlier, small_parts[layer_idx] = layer_backward(
             grad_resid,
             kept_layers[layer_idx],
             layer_weights[layer_idx],
             all_params[layer_idx],
             doc_mask,
+            summed,
         )
-        tiles = weight_grads(places[layer_idx][:96], lefts, rights)
-        if layer_idx:
-            grad_resid, tiles = lax.optimization_barrier((grad_resid, tiles))
-        own_parts[layer_idx] = reduce_weights(tiles, layer_idx, z_hi)
-        small_parts[layer_idx] = small_part
-    own_blocks = unpack_blocks(jnp.where(z_hi == 0, own_parts[0], own_parts[1]))
-
-    grad_bf = grad_resid.astype(BF)
-    slot_grads = product_tn(slot_hot.astype(BF), grad_bf).astype(BF)
-    grad_table = add_table_rows(slot_rows, head_grad, exchanged(slot_grads, "dp"))
-
-    def dense_grads():
-        columns = [grad_bf[:, at : at + 256] for at in range(0, model_width, 256)]
-
-        def joined(parts):
-            return jnp.concatenate(parts, axis=0)
-
-        pair0 = joined([columns[0], swap(columns[0], "zl")])
-        spread0 = joined(gather4(joined(gather4(pair0, "y")), "x"))
-        pair1 = joined([columns[1], swap(columns[1], "zl")])
-        spread1 = joined(gather4(joined(gather4(pair1, "x")), "y"))
-        spread2 = joined(gather4(joined(gather4(columns[2], "y")), "x"))
-        spread3 = swap(spread2, "zl")
-        return scatter_rows(
-            crowd_rows.reshape(16, 1, 512), grad_table, (spread0, spread1, spread2, spread3)
-        )
-
-    grad_table = lax.cond(crowded, dense_grads, lambda: grad_table)
-    pos_parts = exchanged(grad_resid, "dp").reshape(sequences, -1, model_width)
-    pos_own = jnp.sum(pos_parts, axis=0)
-    pos_sum = exchanged(jnp.tile(pos_own, (sequences, 1)), "dp")
-    left_half, right_half = grad_table[:, :half_width], grad_table[:, half_width:]
-    grad_half = jnp.where(core == 0, left_half, right_half) + swap(
-        jnp.where(core == 0, right_half, left_half), "c"
-    )
-    far_grad = z_flip(grad_half[padded : padded + table_rows].astype(BF))
-    grad_own = grad_half[:table_rows] + wide(far_grad)
+        if earlier is not None:
+            layer_grads.append(earlier)
+        summed = matrix_grads
+    layer_grads.append(summed)
 
     gain_list = []
     shift_list = []
     for layer_idx in range(LAYERS):
         gain_list += [small_parts[layer_idx][0], small_parts[layer_idx][1]]
         shift_list += [small_parts[layer_idx][2], small_parts[layer_idx][3]]
-    scalars = jnp.zeros((model_width,), F32).at[0].set(loss_own).at[1].set(count_own)
+    first_term = loss_own.astype(BF)
+    second_term = (loss_own - wide(first_term)).astype(BF)
+    third_term = (loss_own - wide(first_term) - wide(second_term)).astype(BF)
+    scalars = jnp.stack([wide(first_term), wide(second_term), wide(third_term)])
     small_grad = jnp.concatenate(
         [jnp.stack(gain_list + [g_final_gain]), jnp.stack(shift_list + [g_final_shift])]
         + [small_parts[layer_idx][4] for layer_idx in range(LAYERS)]
-        + [scalars[None], jnp.zeros((5, model_width), F32)],
+        + [jnp.pad(scalars, (0, model_width - 3))[None]],
         axis=0,
     )
-    small_all = sum_everywhere(small_grad)
-    rows = small_params.shape[0]
-    small_sum, ce_sum, pick_count = small_all[:rows], small_all[rows, 0], small_all[rows, 1]
+    small_grad = jnp.pad(small_grad, ((0, sequences - small_grad.shape[0]), (0, 0)))
+
+    grad_bf = grad_resid.astype(BF)
+    slot_grads = product_tn(slot_hot.astype(BF), grad_bf).astype(BF)
+    own_rows = span_len // sequences
+    spare = 16 - own_rows - 1
+    outgoing = jnp.concatenate(
+        [
+            slot_grads.reshape(sequences, SLOTS, model_width),
+            grad_bf.reshape(sequences, own_rows, model_width),
+            small_grad.astype(BF)[:, None],
+            jnp.zeros((sequences, spare, model_width), BF),
+        ],
+        axis=1,
+    )
+    arrived = exchanged(outgoing.reshape(-1, model_width), "dp").reshape(sequences, -1, model_width)
+    pos_own = jnp.sum(wide(arrived[:, SLOTS : SLOTS + own_rows]), axis=0)
+    small_own = jnp.sum(wide(arrived[:, SLOTS + own_rows]), axis=0)
+    small_own = jnp.broadcast_to(small_own[None], (8, model_width))
+    grad_table = add_table_rows(
+        slot_rows, head_grad, arrived[:, :SLOTS].reshape(-1, model_width)
+    )
+
+    def dense_grads():
+        columns = [grad_bf[:, at : at + 256] for at in range(0, model_width, 256)]
+
+        pair0 = joined(columns[0], swap(columns[0], "zl"))
+        spread0 = joined(*gather4(joined(*gather4(pair0, "y")), "x"))
+        pair1 = joined(columns[1], swap(columns[1], "zl"))
+        spread1 = joined(*gather4(joined(*gather4(pair1, "x")), "y"))
+        spread2 = joined(*gather4(joined(*gather4(columns[2], "y")), "x"))
+        spread3 = swap(spread2, "zl")
+        return scatter_rows(
+            crowd_rows.reshape(16, 1, 512), grad_table, (spread0, spread1, spread2, spread3)
+        )
+
+    grad_table = lax.cond(crowded, dense_grads, lambda: grad_table)
+    left_half, right_half = grad_table[:, :half_width], grad_table[:, half_width:]
+    mine = jnp.where(core == 0, left_half, right_half)
+    theirs = jnp.where(core == 0, right_half, left_half)
+    grad_half = mine + swap(theirs, "c")
+    small_own = small_own + swap(small_own, "c")
+    small_own = (small_own + swap(small_own, "zh"))[0]
+    far_grad = z_flip(grad_half[padded : padded + table_rows].astype(BF))
+    grad_own = grad_half[:table_rows] + wide(far_grad)
+    grad_places = own_places.at[0].add(z_hi * len(MATRICES))
+    own_blocks = cut_tiles(
+        grad_places, [value for early, late in layer_grads[::-1] for value in (*late, *early)]
+    )
+    shared = joined(pos_own, jnp.pad(small_own[None], ((0, 7), (0, 0))))
+    shared = exchanged(jnp.tile(shared, (sequences, 1)), "dp").reshape(sequences, -1, model_width)
 
     g_table = grad_own / pick_count
-    g_pos = pos_sum / pick_count
-    g_small = small_sum / pick_count
     g_ce = own_blocks.reshape(weights.shape) / pick_count
     g_blocks = g_ce + ewc_weight * fisher * (weights - anchor)
     g_pos_own = pos_own / pick_count
     local_squares = jnp.sum(g_table * g_table) + jnp.sum(g_blocks * g_blocks)
     local_squares = local_squares + jnp.sum(g_pos_own * g_pos_own)
+    g_small_own = small_own / pick_count
     local_squares = local_squares + jnp.where(
-        (row_at == 0) & (seq_at == 0), jnp.sum(g_small * g_small), 0.0
+        (row_at < small_params.shape[0]) & (seq_at == 0), jnp.sum(g_small_own * g_small_own), 0.0
     )
     all_squares = exchanged(jnp.broadcast_to(local_squares, (len(COORDS), LANES)), ("seq", "dp"))
+
+    def products(grad, root_l, root_r):
+        return exact_mm(grad, grad.T), exact_mm(grad.T, grad), exact_mm(exact_mm(root_l, grad), root_r)
+
+    block_products = jax.vmap(products)(
+        squared_blocks(g_blocks), squared_blocks(root_left), squared_blocks(root_right)
+    )
+    left_mm, right_mm, direction = (value.reshape(weights.shape) for value in block_products)
+    all_squares, shared, left_mm, right_mm, direction = lax.optimization_barrier(
+        (all_squares, shared, left_mm, right_mm, direction)
+    )
+    pos_sum = shared[:, :own_rows].reshape(span_len, model_width)
+    small_all = shared[:, own_rows]
+    rows = small_params.shape[0]
+    ce_sum = jnp.sum(small_all[rows, :3])
+    g_pos = pos_sum / pick_count
+    g_small = small_all[:rows] / pick_count
     grad_norm = jnp.sqrt(jnp.sum(all_squares[:, 0]))
     factor = jnp.minimum(1.0, clip_bound / grad_norm)
     table_new, table_first, table_second = adam_update(
@@ -909,23 +810,13 @@
     )
     block_grad = factor * g_blocks
 
-    def products(grad, root_l, root_r):
-        return exact_mm(grad, grad.T), exact_mm(grad.T, grad), exact_mm(exact_mm(root_l, grad), root_r)
-
-    left_mm, right_mm, direction = jax.vmap(products)(
-        squared_blocks(g_blocks), squared_blocks(root_left), squared_blocks(root_right)
-    )
-    direction = (factor * direction).reshape(weights.shape)
+    direction = factor * direction
     mean_square = jnp.mean(direction * direction, axis=1, keepdims=True)
     direction = direction * lax.rsqrt(mean_square + graft_epsilon)
     weights_new = weights - shampoo_rate * (direction + decay_rate * weights)
     square = factor * factor
-    left_new = stat_decay * stat_left + (1.0 - stat_decay) * (
-        square * left_mm.reshape(weights.shape)
-    )
-    right_new = stat_decay * stat_right + (1.0 - stat_decay) * (
-        square * right_mm.reshape(weights.shape)
-    )
+    left_new = stat_decay * stat_left + (1.0 - stat_decay) * (square * left_mm)
+    right_new = stat_decay * stat_right + (1.0 - stat_decay) * (square * right_mm)
     fisher_new = fisher_decay * fisher + (1.0 - fisher_decay) * g_ce * g_ce
     return (
         ce_sum,

time: 1200 us -> 1610 us (1.34)
  waiting for transfers between devices: 238 us -> 1030 us
  starting transfers between devices: 286 us -> 104 us
  Pallas kernels: 119 us -> 25.7 us
  other arithmetic: 179 us -> 97.5 us
  local copies, waits for them, and re-layouts: 144 us -> 75.5 us
  matrix products: 163 us -> 193 us
    psum x0 -> x6, waiting for transfers between devices: none -> 810 us  [the longest x2 320 us: layer_backward(): early = lax.psum(early, ('seq', 'dp'))]
    ppermute x149 -> x27, starting transfers between devices: 224 us -> 56.3 us  [permuted(): return lax.ppermute(value, ('seq', 'dp'), pairs)]
    pallas_call x4 -> x3, Pallas kernels: 99.2 us -> 8.12 us  [the longest x2 7.08 us: spread_tiles(): pl.pallas_call(spread_kernel, grid_spec=pltpu.PrefetchScalarGridSpec(num_...]
    ppermute x149 -> x27, waiting for transfers between devices: 147 us -> 108 us  [permuted(): return lax.ppermute(value, ('seq', 'dp'), pairs)]
    dot_general x2 -> x10, matrix products: 12.9 us -> 47 us  [product_tn(): lax.dot_general(left, right, (((0,), (0,)), ((), ())), preferred_element_...]
    all_to_all x9 -> x6, waiting for transfers between devices: 90.6 us -> 117 us  [exchanged(): return lax.all_to_all(value, axes, 0, 0, tiled=True)]
    add x19 -> x8, other arithmetic: 24.2 us -> 2.95 us  [the longest x1 1.52 us: shards(): stat_decay * stat_right + (1.0 - stat_decay) * (square * right_mm)]
    slice x35 -> x13, local copies, waits for them, and re-layouts: 29.5 us -> 10.6 us  [the longest x4 6.16 us: attend(): key_heads = key_values[:, :model_width].reshape(-1, HEADS, HEAD_DIM)]
  transfers between devices with their start and end apart: 158 -> 39, of which waited for: 38 -> 28; matrix products, arithmetic and copies ran while one was open for 20% -> 11% of each run, Pallas kernels for 7% -> 2%
where the time goes in v3:
time: 1610 us; the launch traced here: 1600 us
  waiting for transfers between devices  1030 us (64%)
  matrix products  193 us (12%)
  starting transfers between devices  104 us (6%)
  other arithmetic  97.5 us (6%)
  local copies, waits for them, and re-layouts  75.5 us (5%)
  blocking collectives  41 us (3%)
  Pallas kernels  25.7 us (2%)
  between operations  23.8 us (1%)
    psum x2, waiting for transfers between devices, layer_backward(): early = lax.psum(early, ('seq', 'dp'))  320 us
    psum x2, waiting for transfers between devices, shards(): layer_weights.append(lax.psum(matrices, ('seq', 'dp')))  249 us
    psum x2, waiting for transfers between devices, layer_backward(): late = lax.psum(late, ('dp', 'seq'))  241 us
    all_to_all x6, waiting for transfers between devices, exchanged(): return lax.all_to_all(value, axes, 0, 0, tiled=True)  117 us
    ppermute x27, waiting for transfers between devices, permuted(): return lax.ppermute(value, ('seq', 'dp'), pairs)  108 us
    ppermute x27, starting transfers between devices, permuted(): return lax.ppermute(value, ('seq', 'dp'), pairs)  56.3 us
    all_to_all x6, starting transfers between devices, exchanged(): return lax.all_to_all(value, axes, 0, 0, tiled=True)  47.3 us
    dot_general x10, matrix products, product_tn(): lax.dot_general(left, right, (((0,), (0,)), ((), ())), preferred_element_...  47 us
  transfers between devices with their start and end apart: 39, of which 28 were waited for; matrix products, arithmetic and copies ran while one was open for 11% of the time, Pallas kernels for 2%

profile of v3, /device:TPU:1, one launch (start us, length us, event | category | flops | bytes accessed | tf_op | source)
XLA Modules:
  0.0 1600.7 jit_solution(7033467021288328068)
XLA Ops:
  28.0 10.0 collective-permute-done.45
  45.4 6.4 pick_table_rows.1
  53.5 7.5 all-to-all-start
  76.2 6.3 collective-permute-done.43
  88.4 17.8 %all-to-all-done = bf16[32,64,768]{2,1,0:T(8,128)(2,1)} async-done(((bf16[32,64,768]{2,1,0:T(8,128)(2,1)}), bf16[32,64,768]{2,1,0:T(8,128)(2,1)}, u32[]{:S(2)}, u32[]{:S(2)}) %all-to-all-start) | async-done | bytes 3145760 | tf_op jit(solution)/shard_map/all_to_all | solution.py:99
  109.8 125.3 %all-reduce.27.cloned.1.call-done = (bf16[768,2304]{1,0:T(8,128)(2,1)}, bf16[768,768]{1,0:T(8,128)(2,1)}, bf16[768,3072]{1,0:T(8,128)(2,1)}, bf16[3072,768]{1,0:T(8,128)(2,1)}) async-done(((bf16[768,2304]{1,0:T(8,128)(2,1)}, bf16[768,768]{1,0:T(8,128)(2,1)}, bf16[768,3072]{1,0:T(8,128)(2,1)}, bf16[3072,768]{1,0:T(8,128)(2,1)}), (bf16[768,2304]{1,0:T(8,128)(2,1)}, bf16[768,768]{1,0:T(8,128)(2,1)}, ...) | async-done | bytes 14155792 | tf_op jit(solution)/shard_map/psum | solution.py:558
  240.3 9.4 collective-permute-done.49
  254.5 8.4 collective-permute-done.50
  277.2 11.0 fusion.200
  288.3 7.3 fusion.67
  301.0 123.6 %all-reduce.25.cloned.1.call-done = (bf16[768,2304]{1,0:T(8,128)(2,1)}, bf16[768,768]{1,0:T(8,128)(2,1)}, bf16[3072,768]{1,0:T(8,128)(2,1)}, bf16[768,3072]{1,0:T(8,128)(2,1)}) async-done(((bf16[768,2304]{1,0:T(8,128)(2,1)}, bf16[768,768]{1,0:T(8,128)(2,1)}, bf16[3072,768]{1,0:T(8,128)(2,1)}, bf16[768,3072]{1,0:T(8,128)(2,1)}), (bf16[768,2304]{1,0:T(8,128)(2,1)}, bf16[768,768]{1,0:T(8,128)(2,1)}, ...) | async-done | bytes 14155792 | tf_op jit(solution)/shard_map/psum | solution.py:558
  429.9 9.2 collective-permute-done.53
  442.1 8.7 collective-permute-done.54
  464.6 10.5 fusion.203
  475.1 6.8 fusion.70
  495.7 38.5 %all-to-all-done.1 = bf16[32,64,768]{2,1,0:T(8,128)(2,1)} async-done(((bf16[32,64,768]{2,1,0:T(8,128)(2,1)}), bf16[32,64,768]{2,1,0:T(8,128)(2,1)}, u32[]{:S(2)}, u32[]{:S(2)}) %all-to-all-start.1) | async-done | bytes 3145760 | tf_op jit(solution)/shard_map/all_to_all | solution.py:99
  534.2 8.4 select_reduce_fusion.1
  542.6 5.9 exponential_reduce_fusion
  549.9 8.6 all-to-all-start.2
  558.9 11.8 all-to-all-done.2
  574.5 8.2 select_convert_fusion
  582.8 6.2 convolution_convert_fusion
  589.0 41.0 %all_to_all.57 = bf16[32,64,768]{2,1,0:T(8,128)(2,1)S(1)} all-to-all(bf16[32,64,768]{2,1,0:T(8,128)(2,1)S(1)} %bitcast.235), channel_id=1, replica_groups=mesh['seq'=4,'dp'=32] {'dp'}, dimensions={0} | all-to-all | bytes 6291456 | tf_op jit(solution)/shard_map/all_to_all | solution.py:99
  634.1 5.8 fusion.183
  639.9 5.9 fusion.174
  658.6 5.7 fusion.30
  664.4 10.8 multiply_reduce_fusion.1
  675.2 5.9 multiply_convert_fusion.1
  694.1 11.7 collective-permute-done.58
  715.3 8.4 collective-permute-done.59
  734.1 6.8 fusion.206
  740.8 5.8 fusion.159
  758.9 11.5 multiply_reduce_fusion
  772.0 6.0 multiply_convert_fusion
  785.0 5.7 collective-permute-start.61
  796.8 11.3 collective-permute-done.62
  811.4 5.8 convolution_multiply_fusion.2
  821.9 94.0 %all-reduce.19.cloned.1.call-done = (f32[768,3072]{1,0:T(8,128)}, f32[3072,768]{1,0:T(8,128)}) async-done(((f32[768,3072]{1,0:T(8,128)}, f32[3072,768]{1,0:T(8,128)}), (f32[768,3072]{1,0:T(8,128)}, f32[3072,768]{1,0:T(8,128)})) %all-reduce.19.cloned.1.call-update) | async-done | bytes 18874384 | tf_op jit(solution)/shard_map/psum | solution.py:428
  925.3 158.6 %all-reduce.23.cloned.1.call-done = (f32[768,2304]{1,0:T(8,128)}, f32[768,768]{1,0:T(8,128)}) async-done(((f32[768,2304]{1,0:T(8,128)}, f32[768,768]{1,0:T(8,128)}), (f32[768,2304]{1,0:T(8,128)}, f32[768,768]{1,0:T(8,128)})) %all-reduce.23.cloned.1.call-update) | async-done | bytes 9437200 | tf_op jit(solution)/shard_map/psum | solution.py:477
  1098.9 10.2 fusion.207.start
  1109.1 42.1 %all-to-all-done.4 = bf16[32,80,768]{2,1,0:T(8,128)(2,1)} async-done(((bf16[32,80,768]{2,1,0:T(8,128)(2,1)}), bf16[32,80,768]{2,1,0:T(8,128)(2,1)}, u32[]{:S(2)}, u32[]{:S(2)}) %all-to-all-start.4) | async-done | bytes 3932192 | tf_op jit(solution)/shard_map/all_to_all | solution.py:99
  1153.5 11.2 add_table_rows.1
  1176.9 9.1 collective-permute-start.65
  1203.2 11.8 all-to-all-start.6
  1219.9 82.5 %all-reduce.21.cloned.1.call-done = (f32[768,2304]{1,0:T(8,128)}, f32[768,768]{1,0:T(8,128)}) async-done(((f32[768,2304]{1,0:T(8,128)}, f32[768,768]{1,0:T(8,128)}), (f32[768,2304]{1,0:T(8,128)}, f32[768,768]{1,0:T(8,128)})) %all-reduce.21.cloned.1.call-update) | async-done | bytes 9437200 | tf_op jit(solution)/shard_map/psum | solution.py:477
  1302.3 226.0 %all-reduce.17.cloned.1.call-done = (f32[768,3072]{1,0:T(8,128)}, f32[3072,768]{1,0:T(8,128)}) async-done(((f32[768,3072]{1,0:T(8,128)}, f32[3072,768]{1,0:T(8,128)}), (f32[768,3072]{1,0:T(8,128)}, f32[3072,768]{1,0:T(8,128)})) %all-reduce.17.cloned.1.call-update) | async-done | bytes 18874384 | tf_op jit(solution)/shard_map/psum | solution.py:428
  1556.0 8.3 all-to-all-start.5
  1567.3 6.5 all-to-all-done.5
  (668 shorter events, 312.5 us)
Async XLA Ops:
  7.2 227.8 %all-reduce.27.cloned.1.call-start = ((), (), s32[]{:S(2)}) async-start(), calls=%async_computation.12 | async-start | bytes 28311552 | tf_op jit(solution)/shard_map/psum | solution.py:558
  9.6 18.2 %collective-permute-start.44 = (bf16[832,384]{1,0:T(8,128)(2,1)}, bf16[832,384]{1,0:T(8,128)(2,1)}, u32[]{:S(2)}, u32[]{:S(2)}) collective-permute-start(bf16[832,384]{1,0:T(8,128)(2,1)} %get-tuple-element.320), channel_id=1, source_target_pairs={{0,4},{1,5},{2,6},{3,7},{4,64},{5,65},{6,66},{7,67},{8,12},{9,13},... | collective-permute-start | bytes 1916936 | tf_op jit(solution)/shard_map/ppermute | solution.py:73
  26.7 16.5 %collective-permute-start.46 = (bf16[832,384]{1,0:T(8,128)(2,1)}, bf16[832,384]{1,0:T(8,128)(2,1)S(1)}, u32[]{:S(2)}, u32[]{:S(2)}) collective-permute-start(bf16[832,384]{1,0:T(8,128)(2,1)} %get-tuple-element.320), channel_id=1, source_target_pairs={{0,32},{1,33},{2,34},{3,35},{4,36},{5,37},{6,38},{7,39},{8,40},{9,... | collective-permute-start | bytes 1916936 | tf_op jit(solution)/shard_map/ppermute | solution.py:73
  27.8 10.2 collective-permute-start.45
  38.0 5.1 collective-permute-start.47
  53.5 52.7 %all-to-all-start = ((bf16[32,64,768]{2,1,0:T(8,128)(2,1)}), bf16[32,64,768]{2,1,0:T(8,128)(2,1)}, u32[]{:S(2)}, u32[]{:S(2)}) async-start(bf16[32,64,768]{2,1,0:T(8,128)(2,1)} %bitcast.202), calls=%async_computation | async-start | bytes 6291456 | tf_op jit(solution)/shard_map/all_to_all | solution.py:99
  61.0 363.6 %all-reduce.25.cloned.1.call-start = ((), (), s32[]{:S(2)}) async-start(), calls=%async_computation.11 | async-start | bytes 28311552 | tf_op jit(solution)/shard_map/psum | solution.py:558
  63.3 2.8 collective-permute-start.42
  66.1 169.0 %copy-start.101 = (f32[768]{0:T(1024)}, f32[768]{0:T(1024)S(1)}, u32[]{:S(2)}) copy-start(f32[768]{0:T(1024)S(1)} %get-tuple-element.212) | copy-start | bytes 9220
  66.1 230.4 %copy-start.94 = (f32[768]{0:T(1024)}, f32[768]{0:T(1024)S(1)}, u32[]{:S(2)}) copy-start(f32[768]{0:T(1024)S(1)} %get-tuple-element.208) | copy-start | bytes 9220
  66.1 230.4 %copy-start.103 = (f32[768]{0:T(1024)}, f32[768]{0:T(1024)S(1)}, u32[]{:S(2)}) copy-start(f32[768]{0:T(1024)S(1)} %get-tuple-element.207) | copy-start | bytes 9220
  66.1 358.5 %copy-start.96 = (f32[768]{0:T(1024)}, f32[768]{0:T(1024)S(1)}, u32[]{:S(2)}) copy-start(f32[768]{0:T(1024)S(1)} %get-tuple-element.205) | copy-start | bytes 9220
  66.1 358.5 %copy-start.105 = (f32[768]{0:T(1024)}, f32[768]{0:T(1024)S(1)}, u32[]{:S(2)}) copy-start(f32[768]{0:T(1024)S(1)} %get-tuple-element.204) | copy-start | bytes 9220
  66.2 16.3 %collective-permute-start.43 = (f32[2,128]{1,0:T(2,128)S(1)}, f32[2,128]{1,0:T(2,128)S(1)}, u32[]{:S(2)}, u32[]{:S(2)}) collective-permute-start(f32[2,128]{1,0:T(2,128)S(1)} %broadcast_add_fusion.5), channel_id=1, source_target_pairs={{0,64},{1,65},{2,66},{3,67},{4,68},{5,69},{6,70},{7,71},{8,72},{9,... | collective-permute-start | bytes 3080 | tf_op jit(solution)/shard_map/ppermute | solution.py:73
  109.5 186.1 %copy-start.27 = (f32[256,768]{1,0:T(8,128)}, f32[256,768]{1,0:T(8,128)S(1)}, u32[]{:S(2)}) copy-start(f32[256,768]{1,0:T(8,128)S(1)} %get-tuple-element.341) | copy-start | bytes 2359300
  238.3 11.3 collective-permute-start.49
  249.6 13.2 collective-permute-start.50
  254.5 13.6 collective-permute-start.48
  262.9 6.8 collective-permute-start.51
  300.7 181.2 %copy-start.31 = (f32[256,768]{1,0:T(8,128)}, f32[256,768]{1,0:T(8,128)S(1)}, u32[]{:S(2)}) copy-start(f32[256,768]{1,0:T(8,128)S(1)} %get-tuple-element.347) | copy-start | bytes 2359300
  427.9 11.2 collective-permute-start.53
  439.1 11.7 collective-permute-start.54
  441.9 13.3 collective-permute-start.52
  450.9 6.4 collective-permute-start.55
  489.9 44.2 %all-to-all-start.1 = ((bf16[32,64,768]{2,1,0:T(8,128)(2,1)}), bf16[32,64,768]{2,1,0:T(8,128)(2,1)}, u32[]{:S(2)}, u32[]{:S(2)}) async-start(bf16[32,64,768]{2,1,0:T(8,128)(2,1)} %tile.8), calls=%async_computation.1 | async-start | bytes 6291456 | tf_op jit(solution)/shard_map/all_to_all | solution.py:99
  549.9 20.7 %all-to-all-start.2 = ((f32[32,1,6144]{2,1,0:T(1,128)}), f32[32,1,6144]{2,1,0:T(1,128)S(1)}, u32[]{:S(2)}, u32[]{:S(2)}) async-start(f32[32,1,6144]{2,1,0:T(1,128)} %tile.10), calls=%async_computation.2 | async-start | bytes 1572864 | tf_op jit(solution)/shard_map/all_to_all | solution.py:99
  558.6 357.3 %all-reduce.19.cloned.1.call-start = ((), (), s32[]{:S(2)}) async-start(), calls=%async_computation.8 | async-start | bytes 37748736 | tf_op jit(solution)/shard_map/psum | solution.py:428
  684.0 6.9 collective-permute-start.57
  692.7 13.1 collective-permute-start.58
  692.7 22.6 %collective-permute-start.56 = (f32[256,1536]{0,1:T(8,128)}, f32[256,1536]{0,1:T(8,128)}, u32[]{:S(2)}, u32[]{:S(2)}) collective-permute-start(f32[256,1536]{0,1:T(8,128)} %get-tuple-element.309), channel_id=1, source_target_pairs={{0,32},{1,33},{2,34},{3,35},{4,36},{5,37},{6,38},{7,39},{8,40},{9,... | collective-permute-start | bytes 4718600 | tf_op jit(solution)/shard_map/ppermute | solution.py:73
  694.0 389.9 %all-reduce.23.cloned.1.call-start = ((), (), s32[]{:S(2)}) async-start(), calls=%async_computation.10 | async-start | bytes 18874368 | tf_op jit(solution)/shard_map/psum | solution.py:477
  705.8 17.9 %collective-permute-start.59 = (bf16[256,1536]{0,1:T(8,128)(2,1)}, bf16[256,1536]{0,1:T(8,128)(2,1)S(1)}, u32[]{:S(2)}, u32[]{:S(2)}) collective-permute-start(bf16[256,1536]{0,1:T(8,128)(2,1)} %collective-permute-done.58), channel_id=1, source_target_pairs={{0,4},{1,5},{2,6},{3,7},{4,64},{5,65},{6,66},{7,67},{8,12},{9,13},... | collective-permute-start | bytes 2359304 | tf_op jit(solution)/shard_map/ppermute | solution.py:73
  785.0 9.1 collective-permute-start.61
  790.8 511.6 %all-reduce.21.cloned.1.call-start = ((), (), s32[]{:S(2)}) async-start(), calls=%async_computation.9 | async-start | bytes 18874368 | tf_op jit(solution)/shard_map/psum | solution.py:477
  796.3 11.8 collective-permute-start.62
  796.4 20.8 %collective-permute-start.60 = (f32[256,1536]{0,1:T(8,128)S(1)}, f32[256,1536]{0,1:T(8,128)S(1)}, u32[]{:S(2)}, u32[]{:S(2)}) collective-permute-start(f32[256,1536]{0,1:T(8,128)S(1)} %get-tuple-element.307), channel_id=1, source_target_pairs={{0,32},{1,33},{2,34},{3,35},{4,36},{5,37},{6,38},{7,39},{8,40},{9,... | collective-permute-start | bytes 4718600 | tf_op jit(solution)/shard_map/ppermute | solution.py:73
  808.1 12.5 collective-permute-start.63
  1092.6 58.6 %all-to-all-start.4 = ((bf16[32,80,768]{2,1,0:T(8,128)(2,1)}), bf16[32,80,768]{2,1,0:T(8,128)(2,1)}, u32[]{:S(2)}, u32[]{:S(2)}) async-start(bf16[32,80,768]{2,1,0:T(8,128)(2,1)} %maximum_maximum_fusion), calls=%async_computation.4 | async-start | bytes 7864320 | tf_op jit(solution)/shard_map/all_to_all | solution.py:99
  1098.1 430.3 %all-reduce.17.cloned.1.call-start = ((), (), s32[]{:S(2)}) async-start(), calls=%async_computation.7 | async-start | bytes 37748736 | tf_op jit(solution)/shard_map/psum | solution.py:428
  1167.8 7.1 collective-permute-start.64
  1176.9 17.2 %collective-permute-start.65 = (bf16[786,384]{1,0:T(8,128)(2,1)S(1)}, bf16[786,384]{1,0:T(8,128)(2,1)}, u32[]{:S(2)}, u32[]{:S(2)}) collective-permute-start(bf16[786,384]{1,0:T(8,128)(2,1)S(1)} %slice.409), channel_id=1, source_target_pairs={{0,4},{1,5},{2,6},{3,7},{4,64},{5,65},{6,66},{7,67},{8,12},{9,13},... | collective-permute-start | bytes 1810952 | tf_op jit(solution)/shard_map/ppermute | solution.py:73
  1189.5 7.8 collective-permute-start.67
  1194.1 22.9 %collective-permute-start.66 = (bf16[786,384]{1,0:T(8,128)(2,1)}, bf16[786,384]{1,0:T(8,128)(2,1)S(1)}, u32[]{:S(2)}, u32[]{:S(2)}) collective-permute-start(bf16[786,384]{1,0:T(8,128)(2,1)} %collective-permute-done.65), channel_id=1, source_target_pairs={{0,4},{1,5},{2,6},{3,7},{4,64},{5,65},{6,66},{7,67},{8,12},{9,13},... | collective-permute-start | bytes 1810952 | tf_op jit(solution)/shard_map/ppermute | solution.py:73
  1197.3 4.5 collective-permute-start.68
  1201.9 326.5 %copy-start.10 = (f32[768,768]{1,0:T(8,128)S(1)}, f32[768,768]{1,0:T(8,128)}, u32[]{:S(2)}) copy-start(f32[768,768]{1,0:T(8,128)} %get-tuple-element.170.refs_5_) | copy-start | bytes 7077892
  1203.2 352.2 %all-to-all-start.6 = ((f32[32,16,768]{2,1,0:T(8,128)}), f32[32,16,768]{2,1,0:T(8,128)}, u32[]{:S(2)}, u32[]{:S(2)}) async-start(f32[32,16,768]{2,1,0:T(8,128)} %tile.11), calls=%async_computation.6 | async-start | bytes 3145728 | tf_op jit(solution)/shard_map/all_to_all | solution.py:99
  1217.0 311.4 %copy-start.64 = (bf16[786,384]{1,0:T(8,128)(2,1)}, bf16[786,384]{1,0:T(8,128)(2,1)S(1)}, u32[]{:S(2)}) copy-start(bf16[786,384]{1,0:T(8,128)(2,1)S(1)} %collective-permute-done.66) | copy-start | bytes 1810948
  1556.0 17.8 %all-to-all-start.5 = ((f32[128,1,128]{2,1,0:T(1,128)}), f32[128,1,128]{2,1,0:T(1,128)}, u32[]{:S(2)}, u32[]{:S(2)}) async-start(f32[128,1,128]{2,1,0:T(1,128)} %broadcast_in_dim.313), calls=%async_computation.5 | async-start | bytes 131072 | tf_op jit(solution)/shard_map/all_to_all | solution.py:99
  (161 other events, 2236.5 us)
Sparse Core Ops, SparseCore 0:
  26.8 208.2 all-reduce.26
  252.6 172.0 all-reduce.24
  694.1 221.7 all-reduce.18
  921.6 162.2 all-reduce.22
  1089.6 212.7 all-reduce.20
  1308.7 219.6 all-reduce.16
